TPU v7x, 1024 devices: a whole 4x8x16 slice. The times are simulated.
1024 devices in a mesh: gz: 16 (over y, core), blk: 64 (over z, x).
Axes of the slice: x: 4, y: 8, z: 16, core: 2. Of those that a mesh axis runs over, the one named last changes fastest.
Arguments:
- state_old: float32 [16, 64, 4, 5, 4096], P('gz', 'blk'), may hold values from -2 to 8, as said below
- counts_old: int32 [16, 16, 4], replicated, may hold values from 1 to 4, 8 in all within a row
- counts_new: int32 [16, 16, 4], replicated, may hold values from 1 to 4, 8 in all within a row
Outputs:
- state_new: float32 [16, 64, 4, 5, 4096], P('gz', 'blk')
Inputs may be any that keep to these rules, and one draw needn't show every extreme that they name: `state_old`: on every cell density and pressure lie in 0.5 to 2 and each velocity component in -1 to 1, in every slot. `counts_old`: in every slab each aligned group of four devices along blk holds exactly 8 meshblocks together, and one device of every group holds 4. `counts_new`: in every slab each aligned group of four devices along blk holds exactly 8 meshblocks together, and one device of every group holds 4.
All inputs are finite; a program needn't handle non-finite values.
Results may differ from a plain program's by a relative error of at most 0.0003.
Values sent between devices are 32-bit elements; how exact they have to be, the bound alone decides.
No kernel may reach another device: no remote copies, remote signals or barrier semaphores. Data moves between devices by JAX's collectives and lax.ppermute only.
A program may use at most 64 MiB of HBM per device.

v0:
```python
import jax
import jax.numpy as jnp
import numpy as np
from jax import lax
from jax.sharding import PartitionSpec as P

BLOCK = 16


adiabatic_index = 1.4
time_step = 0.08


def from_behind(block, axis, distance):
    devices = range(lax.axis_size(axis))
    route = [(i - distance, i) for i in devices if i - distance in devices]
    return lax.ppermute(block, axis, route)


def shifted(value, axis, by):
    peers = lax.axis_size(axis)
    return lax.ppermute(value, axis, [(i, (i + by) % peers) for i in range(peers)])


def limited_slope(left, right):
    return jnp.where(
        left * right > 0.0, jnp.where(jnp.abs(left) < jnp.abs(right), left, right), 0.0
    )


def flux_terms(primitive, normal):
    density, velocity_x, velocity_y, velocity_z, pressure = primitive
    speed = (velocity_x, velocity_y, velocity_z)[normal]
    energy = pressure / (adiabatic_index - 1.0) + 0.5 * density * (
        velocity_x * velocity_x + velocity_y * velocity_y + velocity_z * velocity_z
    )
    conserved = [density, density * velocity_x, density * velocity_y, density * velocity_z, energy]
    fluxes = [value * speed for value in conserved]
    fluxes[1 + normal] = fluxes[1 + normal] + pressure
    fluxes[4] = fluxes[4] + pressure * speed
    sound = jnp.sqrt(adiabatic_index * pressure / density)
    return (conserved, fluxes, speed, sound)


def wave_flux(left, right, normal):
    left_state, left_flux, left_speed, left_sound = flux_terms(left, normal)
    right_state, right_flux, right_speed, right_sound = flux_terms(right, normal)
    fastest = jnp.maximum(jnp.maximum(left_speed + left_sound, right_speed + right_sound), 0.0)
    slowest = jnp.minimum(jnp.minimum(left_speed - left_sound, right_speed - right_sound), 0.0)
    inverse = 1.0 / (fastest - slowest)
    return [
        (
            fastest * left_part
            - slowest * right_part
            + fastest * slowest * (right_value - left_value)
        )
        * inverse
        for left_part, right_part, left_value, right_value in zip(
            left_flux, right_flux, left_state, right_state
        )
    ]


def sweep(extended, normal):
    length = extended.shape[0]
    density = extended[:, :, 0]
    momentum_x = extended[:, :, 1]
    momentum_y = extended[:, :, 2]
    momentum_z = extended[:, :, 3]
    energy = extended[:, :, 4]
    velocity_x = momentum_x / density
    velocity_y = momentum_y / density
    velocity_z = momentum_z / density
    pressure = (adiabatic_index - 1.0) * (
        energy - 0.5 * (momentum_x * velocity_x + momentum_y * velocity_y + momentum_z * velocity_z)
    )
    primitive = [density, velocity_x, velocity_y, velocity_z, pressure]
    slopes = [
        limited_slope(
            value[1 : length - 1] - value[0 : length - 2], value[2:length] - value[1 : length - 1]
        )
        for value in primitive
    ]
    left = [
        value[1 : length - 2] + 0.5 * slope[0 : length - 3]
        for value, slope in zip(primitive, slopes)
    ]
    right = [
        value[2 : length - 1] - 0.5 * slope[1 : length - 2]
        for value, slope in zip(primitive, slopes)
    ]
    fluxes = wave_flux(left, right, normal)
    inner = length - 4
    return jnp.stack([flux[0:inner] - flux[1 : inner + 1] for flux in fluxes], 2)


def starts_of(slab_counts, row_blocks):
    base = jnp.arange(slab_counts.shape[-2], dtype=jnp.int32)[:, None] * (2 * row_blocks)
    return base + jnp.cumsum(slab_counts, axis=-1) - slab_counts


def owner(slab_counts, block_keys, row_blocks):
    group_count = slab_counts.shape[0]
    inclusive = jnp.cumsum(slab_counts, axis=1)
    exclusive = inclusive - slab_counts
    group = block_keys // (2 * row_blocks)
    local = block_keys - group * (2 * row_blocks)
    pick = (group[..., None] == jnp.arange(group_count, dtype=jnp.int32)).astype(jnp.int32)
    bounds = jnp.sum(pick[..., None] * inclusive, axis=-2)
    lower = jnp.sum(pick[..., None] * exclusive, axis=-2)
    position = jnp.minimum(jnp.sum((bounds <= local[..., None]).astype(jnp.int32), axis=-1), 3)
    first = jnp.sum(
        jnp.where(jnp.arange(4, dtype=jnp.int32) == position[..., None], lower, 0), axis=-1
    )
    return (group * 4 + position, local - first)


def body(state_old, counts_old, counts_new):
    blk_count = lax.axis_size("blk")
    slab_count = lax.axis_size("gz")
    slab = lax.axis_index("gz")
    place = lax.axis_index("blk")
    row_blocks = state_old.shape[2]
    plane = row_blocks * blk_count // 2
    line_count = plane // row_blocks
    face_cells = 5 * 2 * BLOCK * BLOCK
    slot_ids = jnp.arange(row_blocks, dtype=jnp.int32)
    here_new = lax.dynamic_index_in_dim(counts_new, slab, 0, keepdims=False)
    count_here = lax.dynamic_index_in_dim(here_new.reshape(-1), place, 0, keepdims=False)
    start_here = lax.dynamic_index_in_dim(
        starts_of(here_new, row_blocks).reshape(-1), place, 0, keepdims=False
    )
    valid = slot_ids < count_here
    block_keys = (start_here + slot_ids) % plane
    here_old = lax.dynamic_index_in_dim(counts_old, slab, 0, keepdims=False)
    old_dev, old_slot = owner(here_old, block_keys, row_blocks)
    held_flat = state_old[0, 0].reshape(row_blocks, -1)
    moved = [
        held_flat if offset == 0 else from_behind(held_flat, "blk", offset)
        for offset in range(-3, 4)
    ]
    moved_rows = jnp.clip((place - old_dev + 3) * row_blocks + old_slot, 0, 7 * row_blocks - 1)
    state = jnp.take(jnp.concatenate(moved, 0), moved_rows, axis=0).reshape(row_blocks, 5, BLOCK**3)
    reach = []
    for distance in range(1, 8):
        for signed in (distance, -distance):
            residue = signed % blk_count
            reach.append(signed)
    table = np.zeros(blk_count, np.int32)
    for position, signed in enumerate(reach):
        table[signed % blk_count] = position + 1
    lookup = jnp.asarray(table)
    line = block_keys // row_blocks
    column = block_keys % row_blocks
    neighbours = [
        line * row_blocks + (column - 1) % row_blocks,
        line * row_blocks + (column + 1) % row_blocks,
        (line - 1) % line_count * row_blocks + column,
        (line + 1) % line_count * row_blocks + column,
    ]
    plane_rows = []
    for neighbour, code in zip(neighbours, (1, 0, 3, 2)):
        source_dev, source_slot = owner(here_new, neighbour, row_blocks)
        residue_here = (place - source_dev) % blk_count
        which = jnp.sum(
            jnp.where(residue_here[:, None] == jnp.arange(blk_count, dtype=jnp.int32), lookup, 0),
            axis=1,
        )
        plane_rows.append(((which * 4 + code) * row_blocks + source_slot).astype(jnp.int32))
    plane_rows = jnp.concatenate(plane_rows)
    below_counts = lax.dynamic_index_in_dim(counts_new, (slab - 1) % slab_count, 0, keepdims=False)
    above_counts = lax.dynamic_index_in_dim(counts_new, (slab + 1) % slab_count, 0, keepdims=False)
    below_dev, below_slot = owner(below_counts, block_keys, row_blocks)
    above_dev, above_slot = owner(above_counts, block_keys, row_blocks)
    below_rows = jnp.clip((place - below_dev + 3) * row_blocks + below_slot, 0, 7 * row_blocks - 1)
    above_rows = jnp.clip((place - above_dev + 3) * row_blocks + above_slot, 0, 7 * row_blocks - 1)

    def vertical(piece_set, base):
        return jnp.concatenate(
            [shifted(piece_set, ("gz", "blk"), base + offset) for offset in range(-3, 4)], 0
        )

    def pack(layers):
        return layers.transpose(1, 0, 2, 3).reshape(row_blocks, face_cells)

    def unpack(rows):
        return rows.reshape(row_blocks, 2, 5, BLOCK * BLOCK).transpose(1, 0, 2, 3)

    def derivative(current):
        cube = current.reshape(row_blocks, 5, BLOCK, BLOCK, BLOCK)
        along_x = cube.transpose(4, 0, 1, 2, 3).reshape(BLOCK, row_blocks, 5, BLOCK * BLOCK)
        along_y = cube.transpose(3, 0, 1, 2, 4).reshape(BLOCK, row_blocks, 5, BLOCK * BLOCK)
        along_z = cube.reshape(row_blocks, 5, BLOCK, BLOCK * BLOCK).transpose(2, 0, 1, 3)
        low_x = pack(along_x[0:2])
        high_x = pack(along_x[BLOCK - 2 :])
        low_y = pack(along_y[0:2])
        high_y = pack(along_y[BLOCK - 2 :])
        low_z = pack(along_z[0:2])
        high_z = pack(along_z[BLOCK - 2 :])
        plane_set = jnp.concatenate([low_x, high_x, low_y, high_y], 0)
        arrived = [shifted(plane_set, "blk", signed) for signed in reach]
        plane_pool = jnp.concatenate([plane_set] + arrived, 0)
        plane_ghost = jnp.take(plane_pool, plane_rows, axis=0).reshape(4, row_blocks, face_cells)
        below_ghost = jnp.take(vertical(high_z, blk_count), below_rows, axis=0)
        above_ghost = jnp.take(vertical(low_z, -blk_count), above_rows, axis=0)
        extended_x = jnp.concatenate([unpack(plane_ghost[0]), along_x, unpack(plane_ghost[1])], 0)
        extended_y = jnp.concatenate([unpack(plane_ghost[2]), along_y, unpack(plane_ghost[3])], 0)
        extended_z = jnp.concatenate([unpack(below_ghost), along_z, unpack(above_ghost)], 0)
        change_x = (
            sweep(extended_x, 0)
            .reshape(BLOCK, row_blocks, 5, BLOCK, BLOCK)
            .transpose(1, 2, 3, 4, 0)
        )
        change_y = (
            sweep(extended_y, 1)
            .reshape(BLOCK, row_blocks, 5, BLOCK, BLOCK)
            .transpose(1, 2, 3, 0, 4)
        )
        change_z = sweep(extended_z, 2).transpose(1, 2, 0, 3)
        total = change_x.reshape(row_blocks, 5, BLOCK**3) + change_y.reshape(
            row_blocks, 5, BLOCK**3
        )
        return total + change_z.reshape(row_blocks, 5, BLOCK**3)

    first = state + time_step * derivative(state)
    second = 0.5 * state + 0.5 * (first + time_step * derivative(first))
    return jnp.where(valid[:, None, None], second, 0.0)[None, None]


def solution(mesh):
    in_specs = (P("gz", "blk", None, None, None), P(), P())
    out_specs = P("gz", "blk", None, None, None)
    return jax.shard_map(body, mesh=mesh, in_specs=in_specs, out_specs=out_specs, check_vma=False)
```

profile of v0, /device:TPU:56, one launch (start us, length us, event | category | flops | bytes accessed | tf_op | source)
XLA Modules:
  0.0 508.5 jit_solution(7391735644257792954)
XLA Ops:
  3.9 4.6 collective-permute-start.3
  8.5 6.1 %collective-permute-start.4 = (f32[4,20480]{1,0:T(4,128)}, f32[4,20480]{1,0:T(4,128)S(1)}, u32[]{:S(2)}, u32[]{:S(2)}) collective-permute-start(f32[4,20480]{1,0:T(4,128)} %bitcast.697), channel_id=1, source_target_pairs={{0,2},{1,3},{2,4},{3,5},{4,6},{5,7},{6,8},{7,9},{8,10},{9,11},{10,... | collective-permute-start | bytes 983048 | tf_op jit(solution)/shard_map/ppermute | solution.py:17
  36.4 7.3 %collective-permute-start.5 = (f32[4,20480]{1,0:T(4,128)}, f32[4,20480]{1,0:T(4,128)}, u32[]{:S(2)}, u32[]{:S(2)}) collective-permute-start(f32[4,20480]{1,0:T(4,128)} %bitcast.698), channel_id=1, source_target_pairs={{0,3},{1,4},{2,5},{3,6},{4,7},{5,8},{6,9},{7,10},{8,11},{9,12},{10... | collective-permute-start | bytes 983048 | tf_op jit(solution)/shard_map/ppermute | solution.py:17
  48.8 9.9 %concatenate.102 = f32[28,20480]{1,0:T(8,128)S(1)} concatenate(f32[4,20480]{1,0:T(4,128)S(1)} %collective-permute-done, f32[4,20480]{1,0:T(4,128)S(1)} %collective-permute-done.1, f32[4,20480]{1,0:T(4,128)} %copy-done.26, f32[4,20480]{1,0:T(4,128)} %bitcast.699, f32[4,20480]{1,0:T(4,128)} %copy-done.27, f32[4,20480]{1,0:T(4,128)} %copy-done.28, f32[4,20480]{1,0:T(4,128)} %collective-permute-done.5), dimensions={0} | concatenate | bytes 4587520 | tf_op jit(solution)/shard_map/concatenate | solution.py:143
  59.5 2.4 gather.18
  63.5 19.3 %collective-permute-start.20 = (f32[4,2560]{1,0:T(4,128)}, f32[4,2560]{1,0:T(4,128)S(1)}, u32[]{:S(2)}, u32[]{:S(2)}) collective-permute-start(f32[4,2560]{1,0:T(4,128)} %reshape.848), channel_id=1, source_target_pairs={{0,61},{1,62},{2,63},{3,64},{4,65},{5,66},{6,67},{7,68},{8,69},{9,... | collective-permute-start | bytes 122888 | tf_op jit(solution)/shard_map/ppermute | solution.py:22
  82.8 3.2 collective-permute-start.21
  86.0 4.9 collective-permute-start.22
  90.9 3.7 collective-permute-start.24
  94.6 4.4 fusion.2
  99.0 3.3 fusion.257
  102.3 3.8 copy.213
  106.3 3.8 copy.214
  112.6 2.8 copy.217
  115.4 2.8 reshape.846
  118.9 2.2 collective-permute-start.25
  121.1 3.2 collective-permute-start.26
  124.3 6.9 %collective-permute-start.27 = (f32[4,2560]{1,0:T(4,128)}, f32[4,2560]{1,0:T(4,128)S(1)}, u32[]{:S(2)}, u32[]{:S(2)}) collective-permute-start(f32[4,2560]{1,0:T(4,128)} %reshape.850), channel_id=1, source_target_pairs={{0,957},{1,958},{2,959},{3,960},{4,961},{5,962},{6,963},{7,964},{8... | collective-permute-start | bytes 122888 | tf_op jit(solution)/shard_map/ppermute | solution.py:22
  131.2 5.5 %collective-permute-start.28 = (f32[4,2560]{1,0:T(4,128)}, f32[4,2560]{1,0:T(4,128)}, u32[]{:S(2)}, u32[]{:S(2)}) collective-permute-start(f32[4,2560]{1,0:T(4,128)} %reshape.850), channel_id=1, source_target_pairs={{0,958},{1,959},{2,960},{3,961},{4,962},{5,963},{6,964},{7,965},{8... | collective-permute-start | bytes 122888 | tf_op jit(solution)/shard_map/ppermute | solution.py:22
  140.8 3.3 collective-permute-start.29
  147.1 3.3 concatenate.112
  151.0 4.4 collective-permute-start.32
  155.4 4.4 collective-permute-start.33
  162.0 6.0 %collective-permute-start.11 = (f32[16,2560]{1,0:T(8,128)}, f32[16,2560]{1,0:T(8,128)S(1)}, u32[]{:S(2)}, u32[]{:S(2)}) collective-permute-start(f32[16,2560]{1,0:T(8,128)} %pad_maximum_fusion.6), channel_id=1, source_target_pairs={{0,61},{1,62},{2,63},{3,0},{4,1},{5,2},{6,3},{7,4},{8,5},{9,6},{10... | collective-permute-start | bytes 491528 | tf_op jit(solution)/shard_map/ppermute | solution.py:22
  170.0 5.1 %collective-permute-start.13 = (f32[16,2560]{1,0:T(8,128)}, f32[16,2560]{1,0:T(8,128)}, u32[]{:S(2)}, u32[]{:S(2)}) collective-permute-start(f32[16,2560]{1,0:T(8,128)} %pad_maximum_fusion.6), channel_id=1, source_target_pairs={{0,60},{1,61},{2,62},{3,63},{4,0},{5,1},{6,2},{7,3},{8,4},{9,5},{1... | collective-permute-start | bytes 491528 | tf_op jit(solution)/shard_map/ppermute | solution.py:22
  179.9 8.1 %collective-permute-start.15 = (f32[16,2560]{1,0:T(8,128)}, f32[16,2560]{1,0:T(8,128)S(1)}, u32[]{:S(2)}, u32[]{:S(2)}) collective-permute-start(f32[16,2560]{1,0:T(8,128)} %pad_maximum_fusion.6), channel_id=1, source_target_pairs={{0,59},{1,60},{2,61},{3,62},{4,63},{5,0},{6,1},{7,2},{8,3},{9,4},{... | collective-permute-start | bytes 491528 | tf_op jit(solution)/shard_map/ppermute | solution.py:22
  190.0 8.4 %collective-permute-start.17 = (f32[16,2560]{1,0:T(8,128)}, f32[16,2560]{1,0:T(8,128)S(1)}, u32[]{:S(2)}, u32[]{:S(2)}) collective-permute-start(f32[16,2560]{1,0:T(8,128)} %pad_maximum_fusion.6), channel_id=1, source_target_pairs={{0,58},{1,59},{2,60},{3,61},{4,62},{5,63},{6,0},{7,1},{8,2},{9,3},... | collective-permute-start | bytes 491528 | tf_op jit(solution)/shard_map/ppermute | solution.py:22
  200.4 6.9 %collective-permute-start.19 = (f32[16,2560]{1,0:T(8,128)}, f32[16,2560]{1,0:T(8,128)S(1)}, u32[]{:S(2)}, u32[]{:S(2)}) collective-permute-start(f32[16,2560]{1,0:T(8,128)} %pad_maximum_fusion.6), channel_id=1, source_target_pairs={{0,57},{1,58},{2,59},{3,60},{4,61},{5,62},{6,63},{7,0},{8,1},{9,2}... | collective-permute-start | bytes 491528 | tf_op jit(solution)/shard_map/ppermute | solution.py:22
  209.3 7.2 %collective-permute-start.7 = (f32[16,2560]{1,0:T(8,128)}, f32[16,2560]{1,0:T(8,128)S(1)}, u32[]{:S(2)}, u32[]{:S(2)}) collective-permute-start(f32[16,2560]{1,0:T(8,128)} %pad_maximum_fusion.6), channel_id=1, source_target_pairs={{0,63},{1,0},{2,1},{3,2},{4,3},{5,4},{6,5},{7,6},{8,7},{9,8},{10,9... | collective-permute-start | bytes 491528 | tf_op jit(solution)/shard_map/ppermute | solution.py:22
  218.6 7.9 %collective-permute-start.9 = (f32[16,2560]{1,0:T(8,128)}, f32[16,2560]{1,0:T(8,128)}, u32[]{:S(2)}, u32[]{:S(2)}) collective-permute-start(f32[16,2560]{1,0:T(8,128)} %pad_maximum_fusion.6), channel_id=1, source_target_pairs={{0,62},{1,63},{2,0},{3,1},{4,2},{5,3},{6,4},{7,5},{8,6},{9,7},{10,... | collective-permute-start | bytes 491528 | tf_op jit(solution)/shard_map/ppermute | solution.py:22
  226.5 2.3 reshape.853
  231.2 12.1 %concatenate.104 = f32[240,2560]{1,0:T(8,128)S(1)} concatenate(f32[4,2560]{1,0:T(4,128)S(1)} %bitcast.684, f32[4,2560]{1,0:T(4,128)S(1)} %bitcast.686, f32[4,2560]{1,0:T(4,128)S(1)} %bitcast.676, f32[4,2560]{1,0:T(4,128)S(1)} %bitcast.680, f32[16,2560]{1,0:T(8,128)} %copy-done.45, f32[16,2560]{1,0:T(8,128)} %copy-done.47, f32[16,2560]{1,0:T(8,128)} %copy-done.49, ...), dimensions={0} | concatenate | bytes 4915200 | tf_op jit(solution)/shard_map/concatenate | solution.py:202
  257.2 2.1 copy.224
  262.8 2.1 copy.225
  268.4 2.2 copy.226
  291.7 4.5 fusion.1
  296.2 2.4 copy.235
  298.6 3.4 add.1326
  305.9 6.0 %collective-permute-start.49 = (f32[4,2560]{1,0:T(4,128)}, f32[4,2560]{1,0:T(4,128)}, u32[]{:S(2)}, u32[]{:S(2)}) collective-permute-start(f32[4,2560]{1,0:T(4,128)} %reshape.860), channel_id=1, source_target_pairs={{0,62},{1,63},{2,64},{3,65},{4,66},{5,67},{6,68},{7,69},{8,70},{9,... | collective-permute-start | bytes 122888 | tf_op jit(solution)/shard_map/ppermute | solution.py:22
  313.9 2.8 collective-permute-start.52
  316.7 3.3 fusion.255
  320.8 4.6 copy.244
  326.5 4.6 copy.245
  334.2 5.1 collective-permute-start.53
  339.3 4.2 collective-permute-start.54
  343.6 4.6 collective-permute-start.55
  348.2 5.1 %collective-permute-start.56 = (f32[4,2560]{1,0:T(4,128)}, f32[4,2560]{1,0:T(4,128)S(1)}, u32[]{:S(2)}, u32[]{:S(2)}) collective-permute-start(f32[4,2560]{1,0:T(4,128)} %reshape.862), channel_id=1, source_target_pairs={{0,958},{1,959},{2,960},{3,961},{4,962},{5,963},{6,964},{7,965},{8... | collective-permute-start | bytes 122888 | tf_op jit(solution)/shard_map/ppermute | solution.py:22
  354.0 2.8 copy.249
  358.0 3.8 add.1236
  363.7 2.6 collective-permute-start.57
  367.5 2.7 collective-permute-start.59
  370.2 3.3 concatenate.125
  374.2 5.0 collective-permute-start.60
  379.2 6.4 %collective-permute-start.61 = (f32[4,2560]{1,0:T(4,128)}, f32[4,2560]{1,0:T(4,128)S(1)}, u32[]{:S(2)}, u32[]{:S(2)}) collective-permute-start(f32[4,2560]{1,0:T(4,128)} %reshape.862), channel_id=1, source_target_pairs={{0,963},{1,964},{2,965},{3,966},{4,967},{5,968},{6,969},{7,970},{8... | collective-permute-start | bytes 122888 | tf_op jit(solution)/shard_map/ppermute | solution.py:22
  385.7 2.8 collective-permute-start.34
  388.5 6.4 %collective-permute-start.35 = (f32[16,2560]{1,0:T(8,128)}, f32[16,2560]{1,0:T(8,128)S(1)}, u32[]{:S(2)}, u32[]{:S(2)}) collective-permute-start(f32[16,2560]{1,0:T(8,128)} %pad_maximum_fusion.7), channel_id=1, source_target_pairs={{0,63},{1,0},{2,1},{3,2},{4,3},{5,4},{6,5},{7,6},{8,7},{9,8},{10,9... | collective-permute-start | bytes 491528 | tf_op jit(solution)/shard_map/ppermute | solution.py:22
  396.9 7.5 %collective-permute-start.37 = (f32[16,2560]{1,0:T(8,128)}, f32[16,2560]{1,0:T(8,128)S(1)}, u32[]{:S(2)}, u32[]{:S(2)}) collective-permute-start(f32[16,2560]{1,0:T(8,128)} %pad_maximum_fusion.7), channel_id=1, source_target_pairs={{0,62},{1,63},{2,0},{3,1},{4,2},{5,3},{6,4},{7,5},{8,6},{9,7},{10,... | collective-permute-start | bytes 491528 | tf_op jit(solution)/shard_map/ppermute | solution.py:22
  404.4 2.1 collective-permute-start.38
  408.7 6.0 %collective-permute-start.39 = (f32[16,2560]{1,0:T(8,128)}, f32[16,2560]{1,0:T(8,128)S(1)}, u32[]{:S(2)}, u32[]{:S(2)}) collective-permute-start(f32[16,2560]{1,0:T(8,128)} %pad_maximum_fusion.7), channel_id=1, source_target_pairs={{0,61},{1,62},{2,63},{3,0},{4,1},{5,2},{6,3},{7,4},{8,5},{9,6},{10... | collective-permute-start | bytes 491528 | tf_op jit(solution)/shard_map/ppermute | solution.py:22
  416.7 5.1 %collective-permute-start.41 = (f32[16,2560]{1,0:T(8,128)}, f32[16,2560]{1,0:T(8,128)S(1)}, u32[]{:S(2)}, u32[]{:S(2)}) collective-permute-start(f32[16,2560]{1,0:T(8,128)} %pad_maximum_fusion.7), channel_id=1, source_target_pairs={{0,60},{1,61},{2,62},{3,63},{4,0},{5,1},{6,2},{7,3},{8,4},{9,5},{1... | collective-permute-start | bytes 491528 | tf_op jit(solution)/shard_map/ppermute | solution.py:22
  423.9 8.1 %collective-permute-start.43 = (f32[16,2560]{1,0:T(8,128)}, f32[16,2560]{1,0:T(8,128)S(1)}, u32[]{:S(2)}, u32[]{:S(2)}) collective-permute-start(f32[16,2560]{1,0:T(8,128)} %pad_maximum_fusion.7), channel_id=1, source_target_pairs={{0,59},{1,60},{2,61},{3,62},{4,63},{5,0},{6,1},{7,2},{8,3},{9,4},{... | collective-permute-start | bytes 491528 | tf_op jit(solution)/shard_map/ppermute | solution.py:22
  434.0 8.4 %collective-permute-start.45 = (f32[16,2560]{1,0:T(8,128)}, f32[16,2560]{1,0:T(8,128)S(1)}, u32[]{:S(2)}, u32[]{:S(2)}) collective-permute-start(f32[16,2560]{1,0:T(8,128)} %pad_maximum_fusion.7), channel_id=1, source_target_pairs={{0,58},{1,59},{2,60},{3,61},{4,62},{5,63},{6,0},{7,1},{8,2},{9,3},... | collective-permute-start | bytes 491528 | tf_op jit(solution)/shard_map/ppermute | solution.py:22
  444.4 6.9 %collective-permute-start.47 = (f32[16,2560]{1,0:T(8,128)}, f32[16,2560]{1,0:T(8,128)}, u32[]{:S(2)}, u32[]{:S(2)}) collective-permute-start(f32[16,2560]{1,0:T(8,128)} %pad_maximum_fusion.7), channel_id=1, source_target_pairs={{0,57},{1,58},{2,59},{3,60},{4,61},{5,62},{6,63},{7,0},{8,1},{9,2}... | collective-permute-start | bytes 491528 | tf_op jit(solution)/shard_map/ppermute | solution.py:22
  454.5 12.1 %concatenate.118 = f32[240,2560]{1,0:T(8,128)S(1)} concatenate(f32[4,2560]{1,0:T(4,128)S(1)} %bitcast.688, f32[4,2560]{1,0:T(4,128)S(1)} %bitcast.690, f32[4,2560]{1,0:T(4,128)S(1)} %bitcast.678, f32[4,2560]{1,0:T(4,128)S(1)} %bitcast.682, f32[16,2560]{1,0:T(8,128)} %copy-done.29, f32[16,2560]{1,0:T(8,128)} %copy-done.30, f32[16,2560]{1,0:T(8,128)} %copy-done.32, ...), dimensions={0} | concatenate | bytes 4915200 | tf_op jit(solution)/shard_map/concatenate | solution.py:202
  (484 shorter events, 176.7 us)
Async XLA Ops:
  0.0 36.4 %collective-permute-start = (f32[4,20480]{1,0:T(4,128)}, f32[4,20480]{1,0:T(4,128)S(1)}, u32[]{:S(2)}, u32[]{:S(2)}) collective-permute-start(f32[4,20480]{1,0:T(4,128)} %bitcast.693), channel_id=1, source_target_pairs={{3,0},{4,1},{5,2},{6,3},{7,4},{8,5},{9,6},{10,7},{11,8},{12,9},{13... | collective-permute-start | bytes 983048 | tf_op jit(solution)/shard_map/ppermute | solution.py:17
  1.3 44.3 %collective-permute-start.1 = (f32[4,20480]{1,0:T(4,128)}, f32[4,20480]{1,0:T(4,128)S(1)}, u32[]{:S(2)}, u32[]{:S(2)}) collective-permute-start(f32[4,20480]{1,0:T(4,128)} %bitcast.694), channel_id=1, source_target_pairs={{2,0},{3,1},{4,2},{5,3},{6,4},{7,5},{8,6},{9,7},{10,8},{11,9},{12,... | collective-permute-start | bytes 983048 | tf_op jit(solution)/shard_map/ppermute | solution.py:17
  2.6 43.0 %collective-permute-start.2 = (f32[4,20480]{1,0:T(4,128)}, f32[4,20480]{1,0:T(4,128)S(1)}, u32[]{:S(2)}, u32[]{:S(2)}) collective-permute-start(f32[4,20480]{1,0:T(4,128)} %bitcast.695), channel_id=1, source_target_pairs={{1,0},{2,1},{3,2},{4,3},{5,4},{6,5},{7,6},{8,7},{9,8},{10,9},{11,1... | collective-permute-start | bytes 983048 | tf_op jit(solution)/shard_map/ppermute | solution.py:17
  3.9 41.7 %collective-permute-start.3 = (f32[4,20480]{1,0:T(4,128)}, f32[4,20480]{1,0:T(4,128)S(1)}, u32[]{:S(2)}, u32[]{:S(2)}) collective-permute-start(f32[4,20480]{1,0:T(4,128)} %bitcast.696), channel_id=1, source_target_pairs={{0,1},{1,2},{2,3},{3,4},{4,5},{5,6},{6,7},{7,8},{8,9},{9,10},{10,1... | collective-permute-start | bytes 983048 | tf_op jit(solution)/shard_map/ppermute | solution.py:17
  8.5 37.2 %collective-permute-start.4 = (f32[4,20480]{1,0:T(4,128)}, f32[4,20480]{1,0:T(4,128)S(1)}, u32[]{:S(2)}, u32[]{:S(2)}) collective-permute-start(f32[4,20480]{1,0:T(4,128)} %bitcast.697), channel_id=1, source_target_pairs={{0,2},{1,3},{2,4},{3,5},{4,6},{5,7},{6,8},{7,9},{8,10},{9,11},{10,... | collective-permute-start | bytes 983048 | tf_op jit(solution)/shard_map/ppermute | solution.py:17
  31.5 212.5 %copy-start.56 = (pred[16]{0:T(512)(128)(4,1)}, pred[16]{0:T(512)(128)(4,1)S(1)}, u32[]{:S(2)}) copy-start(pred[16]{0:T(512)(128)(4,1)S(1)} %get-tuple-element.102) | copy-start | bytes 52
  31.5 211.9 %copy-start.53 = (s32[1024]{0:T(1024)}, s32[1024]{0:T(1024)S(1)}, u32[]{:S(2)}) copy-start(s32[1024]{0:T(1024)S(1)} %pad_clamp_fusion.2) | copy-start | bytes 12292
  36.4 12.4 %collective-permute-start.5 = (f32[4,20480]{1,0:T(4,128)}, f32[4,20480]{1,0:T(4,128)}, u32[]{:S(2)}, u32[]{:S(2)}) collective-permute-start(f32[4,20480]{1,0:T(4,128)} %bitcast.698), channel_id=1, source_target_pairs={{0,3},{1,4},{2,5},{3,6},{4,7},{5,8},{6,9},{7,10},{8,11},{9,12},{10... | collective-permute-start | bytes 983048 | tf_op jit(solution)/shard_map/ppermute | solution.py:17
  63.5 55.4 %collective-permute-start.20 = (f32[4,2560]{1,0:T(4,128)}, f32[4,2560]{1,0:T(4,128)S(1)}, u32[]{:S(2)}, u32[]{:S(2)}) collective-permute-start(f32[4,2560]{1,0:T(4,128)} %reshape.848), channel_id=1, source_target_pairs={{0,61},{1,62},{2,63},{3,64},{4,65},{5,66},{6,67},{7,68},{8,69},{9,... | collective-permute-start | bytes 122888 | tf_op jit(solution)/shard_map/ppermute | solution.py:22
  82.8 38.3 %collective-permute-start.21 = (f32[4,2560]{1,0:T(4,128)}, f32[4,2560]{1,0:T(4,128)}, u32[]{:S(2)}, u32[]{:S(2)}) collective-permute-start(f32[4,2560]{1,0:T(4,128)} %reshape.848), channel_id=1, source_target_pairs={{0,62},{1,63},{2,64},{3,65},{4,66},{5,67},{6,68},{7,69},{8,70},{9,... | collective-permute-start | bytes 122888 | tf_op jit(solution)/shard_map/ppermute | solution.py:22
  86.0 38.3 %collective-permute-start.22 = (f32[4,2560]{1,0:T(4,128)}, f32[4,2560]{1,0:T(4,128)}, u32[]{:S(2)}, u32[]{:S(2)}) collective-permute-start(f32[4,2560]{1,0:T(4,128)} %reshape.848), channel_id=1, source_target_pairs={{0,63},{1,64},{2,65},{3,66},{4,67},{5,68},{6,69},{7,70},{8,71},{9,... | collective-permute-start | bytes 122888 | tf_op jit(solution)/shard_map/ppermute | solution.py:22
  90.9 40.3 %collective-permute-start.23 = (f32[4,2560]{1,0:T(4,128)}, f32[4,2560]{1,0:T(4,128)}, u32[]{:S(2)}, u32[]{:S(2)}) collective-permute-start(f32[4,2560]{1,0:T(4,128)} %reshape.848), channel_id=1, source_target_pairs={{0,64},{1,65},{2,66},{3,67},{4,68},{5,69},{6,70},{7,71},{8,72},{9,... | collective-permute-start | bytes 122888 | tf_op jit(solution)/shard_map/ppermute | solution.py:22
  90.9 49.9 %collective-permute-start.24 = (f32[4,2560]{1,0:T(4,128)}, f32[4,2560]{1,0:T(4,128)}, u32[]{:S(2)}, u32[]{:S(2)}) collective-permute-start(f32[4,2560]{1,0:T(4,128)} %reshape.848), channel_id=1, source_target_pairs={{0,65},{1,66},{2,67},{3,68},{4,69},{5,70},{6,71},{7,72},{8,73},{9,... | collective-permute-start | bytes 122888 | tf_op jit(solution)/shard_map/ppermute | solution.py:22
  118.9 25.2 %collective-permute-start.25 = (f32[4,2560]{1,0:T(4,128)}, f32[4,2560]{1,0:T(4,128)}, u32[]{:S(2)}, u32[]{:S(2)}) collective-permute-start(f32[4,2560]{1,0:T(4,128)} %reshape.848), channel_id=1, source_target_pairs={{0,66},{1,67},{2,68},{3,69},{4,70},{5,71},{6,72},{7,73},{8,74},{9,... | collective-permute-start | bytes 122888 | tf_op jit(solution)/shard_map/ppermute | solution.py:22
  121.1 24.1 %collective-permute-start.26 = (f32[4,2560]{1,0:T(4,128)}, f32[4,2560]{1,0:T(4,128)}, u32[]{:S(2)}, u32[]{:S(2)}) collective-permute-start(f32[4,2560]{1,0:T(4,128)} %reshape.848), channel_id=1, source_target_pairs={{0,67},{1,68},{2,69},{3,70},{4,71},{5,72},{6,73},{7,74},{8,75},{9,... | collective-permute-start | bytes 122888 | tf_op jit(solution)/shard_map/ppermute | solution.py:22
  124.3 26.7 %collective-permute-start.27 = (f32[4,2560]{1,0:T(4,128)}, f32[4,2560]{1,0:T(4,128)S(1)}, u32[]{:S(2)}, u32[]{:S(2)}) collective-permute-start(f32[4,2560]{1,0:T(4,128)} %reshape.850), channel_id=1, source_target_pairs={{0,957},{1,958},{2,959},{3,960},{4,961},{5,962},{6,963},{7,964},{8... | collective-permute-start | bytes 122888 | tf_op jit(solution)/shard_map/ppermute | solution.py:22
  131.2 24.3 %collective-permute-start.28 = (f32[4,2560]{1,0:T(4,128)}, f32[4,2560]{1,0:T(4,128)}, u32[]{:S(2)}, u32[]{:S(2)}) collective-permute-start(f32[4,2560]{1,0:T(4,128)} %reshape.850), channel_id=1, source_target_pairs={{0,958},{1,959},{2,960},{3,961},{4,962},{5,963},{6,964},{7,965},{8... | collective-permute-start | bytes 122888 | tf_op jit(solution)/shard_map/ppermute | solution.py:22
  140.8 19.3 %collective-permute-start.29 = (f32[4,2560]{1,0:T(4,128)}, f32[4,2560]{1,0:T(4,128)S(1)}, u32[]{:S(2)}, u32[]{:S(2)}) collective-permute-start(f32[4,2560]{1,0:T(4,128)} %reshape.850), channel_id=1, source_target_pairs={{0,959},{1,960},{2,961},{3,962},{4,963},{5,964},{6,965},{7,966},{8... | collective-permute-start | bytes 122888 | tf_op jit(solution)/shard_map/ppermute | solution.py:22
  144.0 17.9 %collective-permute-start.30 = (f32[4,2560]{1,0:T(4,128)}, f32[4,2560]{1,0:T(4,128)S(1)}, u32[]{:S(2)}, u32[]{:S(2)}) collective-permute-start(f32[4,2560]{1,0:T(4,128)} %reshape.850), channel_id=1, source_target_pairs={{0,960},{1,961},{2,962},{3,963},{4,964},{5,965},{6,966},{7,967},{8... | collective-permute-start | bytes 122888 | tf_op jit(solution)/shard_map/ppermute | solution.py:22
  145.2 22.8 %collective-permute-start.31 = (f32[4,2560]{1,0:T(4,128)}, f32[4,2560]{1,0:T(4,128)S(1)}, u32[]{:S(2)}, u32[]{:S(2)}) collective-permute-start(f32[4,2560]{1,0:T(4,128)} %reshape.850), channel_id=1, source_target_pairs={{0,961},{1,962},{2,963},{3,964},{4,965},{5,966},{6,967},{7,968},{8... | collective-permute-start | bytes 122888 | tf_op jit(solution)/shard_map/ppermute | solution.py:22
  151.0 19.0 %collective-permute-start.32 = (f32[4,2560]{1,0:T(4,128)}, f32[4,2560]{1,0:T(4,128)S(1)}, u32[]{:S(2)}, u32[]{:S(2)}) collective-permute-start(f32[4,2560]{1,0:T(4,128)} %reshape.850), channel_id=1, source_target_pairs={{0,962},{1,963},{2,964},{3,965},{4,966},{5,967},{6,968},{7,969},{8... | collective-permute-start | bytes 122888 | tf_op jit(solution)/shard_map/ppermute | solution.py:22
  155.4 19.7 %collective-permute-start.33 = (f32[4,2560]{1,0:T(4,128)}, f32[4,2560]{1,0:T(4,128)S(1)}, u32[]{:S(2)}, u32[]{:S(2)}) collective-permute-start(f32[4,2560]{1,0:T(4,128)} %reshape.850), channel_id=1, source_target_pairs={{0,963},{1,964},{2,965},{3,966},{4,967},{5,968},{6,969},{7,970},{8... | collective-permute-start | bytes 122888 | tf_op jit(solution)/shard_map/ppermute | solution.py:22
  160.0 19.9 %collective-permute-start.10 = (f32[16,2560]{1,0:T(8,128)}, f32[16,2560]{1,0:T(8,128)S(1)}, u32[]{:S(2)}, u32[]{:S(2)}) collective-permute-start(f32[16,2560]{1,0:T(8,128)} %pad_maximum_fusion.6), channel_id=1, source_target_pairs={{0,3},{1,4},{2,5},{3,6},{4,7},{5,8},{6,9},{7,10},{8,11},{9,12},{10... | collective-permute-start | bytes 491528 | tf_op jit(solution)/shard_map/ppermute | solution.py:22
  162.0 26.1 %collective-permute-start.11 = (f32[16,2560]{1,0:T(8,128)}, f32[16,2560]{1,0:T(8,128)S(1)}, u32[]{:S(2)}, u32[]{:S(2)}) collective-permute-start(f32[16,2560]{1,0:T(8,128)} %pad_maximum_fusion.6), channel_id=1, source_target_pairs={{0,61},{1,62},{2,63},{3,0},{4,1},{5,2},{6,3},{7,4},{8,5},{9,6},{10... | collective-permute-start | bytes 491528 | tf_op jit(solution)/shard_map/ppermute | solution.py:22
  168.0 22.0 %collective-permute-start.12 = (f32[16,2560]{1,0:T(8,128)}, f32[16,2560]{1,0:T(8,128)S(1)}, u32[]{:S(2)}, u32[]{:S(2)}) collective-permute-start(f32[16,2560]{1,0:T(8,128)} %pad_maximum_fusion.6), channel_id=1, source_target_pairs={{0,4},{1,5},{2,6},{3,7},{4,8},{5,9},{6,10},{7,11},{8,12},{9,13},{1... | collective-permute-start | bytes 491528 | tf_op jit(solution)/shard_map/ppermute | solution.py:22
  170.0 28.5 %collective-permute-start.13 = (f32[16,2560]{1,0:T(8,128)}, f32[16,2560]{1,0:T(8,128)}, u32[]{:S(2)}, u32[]{:S(2)}) collective-permute-start(f32[16,2560]{1,0:T(8,128)} %pad_maximum_fusion.6), channel_id=1, source_target_pairs={{0,60},{1,61},{2,62},{3,63},{4,0},{5,1},{6,2},{7,3},{8,4},{9,5},{1... | collective-permute-start | bytes 491528 | tf_op jit(solution)/shard_map/ppermute | solution.py:22
  175.1 25.3 %collective-permute-start.14 = (f32[16,2560]{1,0:T(8,128)}, f32[16,2560]{1,0:T(8,128)}, u32[]{:S(2)}, u32[]{:S(2)}) collective-permute-start(f32[16,2560]{1,0:T(8,128)} %pad_maximum_fusion.6), channel_id=1, source_target_pairs={{0,5},{1,6},{2,7},{3,8},{4,9},{5,10},{6,11},{7,12},{8,13},{9,14},{... | collective-permute-start | bytes 491528 | tf_op jit(solution)/shard_map/ppermute | solution.py:22
  179.9 27.5 %collective-permute-start.15 = (f32[16,2560]{1,0:T(8,128)}, f32[16,2560]{1,0:T(8,128)S(1)}, u32[]{:S(2)}, u32[]{:S(2)}) collective-permute-start(f32[16,2560]{1,0:T(8,128)} %pad_maximum_fusion.6), channel_id=1, source_target_pairs={{0,59},{1,60},{2,61},{3,62},{4,63},{5,0},{6,1},{7,2},{8,3},{9,4},{... | collective-permute-start | bytes 491528 | tf_op jit(solution)/shard_map/ppermute | solution.py:22
  188.1 21.2 %collective-permute-start.16 = (f32[16,2560]{1,0:T(8,128)}, f32[16,2560]{1,0:T(8,128)S(1)}, u32[]{:S(2)}, u32[]{:S(2)}) collective-permute-start(f32[16,2560]{1,0:T(8,128)} %pad_maximum_fusion.6), channel_id=1, source_target_pairs={{0,6},{1,7},{2,8},{3,9},{4,10},{5,11},{6,12},{7,13},{8,14},{9,15},... | collective-permute-start | bytes 491528 | tf_op jit(solution)/shard_map/ppermute | solution.py:22
  190.0 26.6 %collective-permute-start.17 = (f32[16,2560]{1,0:T(8,128)}, f32[16,2560]{1,0:T(8,128)S(1)}, u32[]{:S(2)}, u32[]{:S(2)}) collective-permute-start(f32[16,2560]{1,0:T(8,128)} %pad_maximum_fusion.6), channel_id=1, source_target_pairs={{0,58},{1,59},{2,60},{3,61},{4,62},{5,63},{6,0},{7,1},{8,2},{9,3},... | collective-permute-start | bytes 491528 | tf_op jit(solution)/shard_map/ppermute | solution.py:22
  198.5 20.1 %collective-permute-start.18 = (f32[16,2560]{1,0:T(8,128)}, f32[16,2560]{1,0:T(8,128)S(1)}, u32[]{:S(2)}, u32[]{:S(2)}) collective-permute-start(f32[16,2560]{1,0:T(8,128)} %pad_maximum_fusion.6), channel_id=1, source_target_pairs={{0,7},{1,8},{2,9},{3,10},{4,11},{5,12},{6,13},{7,14},{8,15},{9,16}... | collective-permute-start | bytes 491528 | tf_op jit(solution)/shard_map/ppermute | solution.py:22
  200.4 29.4 %collective-permute-start.19 = (f32[16,2560]{1,0:T(8,128)}, f32[16,2560]{1,0:T(8,128)S(1)}, u32[]{:S(2)}, u32[]{:S(2)}) collective-permute-start(f32[16,2560]{1,0:T(8,128)} %pad_maximum_fusion.6), channel_id=1, source_target_pairs={{0,57},{1,58},{2,59},{3,60},{4,61},{5,62},{6,63},{7,0},{8,1},{9,2}... | collective-permute-start | bytes 491528 | tf_op jit(solution)/shard_map/ppermute | solution.py:22
  207.4 22.4 %collective-permute-start.6 = (f32[16,2560]{1,0:T(8,128)}, f32[16,2560]{1,0:T(8,128)S(1)}, u32[]{:S(2)}, u32[]{:S(2)}) collective-permute-start(f32[16,2560]{1,0:T(8,128)} %pad_maximum_fusion.6), channel_id=1, source_target_pairs={{0,1},{1,2},{2,3},{3,4},{4,5},{5,6},{6,7},{7,8},{8,9},{9,10},{10,1... | collective-permute-start | bytes 491528 | tf_op jit(solution)/shard_map/ppermute | solution.py:22
  209.3 20.5 %collective-permute-start.7 = (f32[16,2560]{1,0:T(8,128)}, f32[16,2560]{1,0:T(8,128)S(1)}, u32[]{:S(2)}, u32[]{:S(2)}) collective-permute-start(f32[16,2560]{1,0:T(8,128)} %pad_maximum_fusion.6), channel_id=1, source_target_pairs={{0,63},{1,0},{2,1},{3,2},{4,3},{5,4},{6,5},{7,6},{8,7},{9,8},{10,9... | collective-permute-start | bytes 491528 | tf_op jit(solution)/shard_map/ppermute | solution.py:22
  216.6 13.2 %collective-permute-start.8 = (f32[16,2560]{1,0:T(8,128)}, f32[16,2560]{1,0:T(8,128)S(1)}, u32[]{:S(2)}, u32[]{:S(2)}) collective-permute-start(f32[16,2560]{1,0:T(8,128)} %pad_maximum_fusion.6), channel_id=1, source_target_pairs={{0,2},{1,3},{2,4},{3,5},{4,6},{5,7},{6,8},{7,9},{8,10},{9,11},{10,... | collective-permute-start | bytes 491528 | tf_op jit(solution)/shard_map/ppermute | solution.py:22
  218.6 12.7 %collective-permute-start.9 = (f32[16,2560]{1,0:T(8,128)}, f32[16,2560]{1,0:T(8,128)}, u32[]{:S(2)}, u32[]{:S(2)}) collective-permute-start(f32[16,2560]{1,0:T(8,128)} %pad_maximum_fusion.6), channel_id=1, source_target_pairs={{0,62},{1,63},{2,0},{3,1},{4,2},{5,3},{6,4},{7,5},{8,6},{9,7},{10,... | collective-permute-start | bytes 491528 | tf_op jit(solution)/shard_map/ppermute | solution.py:22
  304.0 30.3 %collective-permute-start.48 = (f32[4,2560]{1,0:T(4,128)}, f32[4,2560]{1,0:T(4,128)}, u32[]{:S(2)}, u32[]{:S(2)}) collective-permute-start(f32[4,2560]{1,0:T(4,128)} %reshape.860), channel_id=1, source_target_pairs={{0,61},{1,62},{2,63},{3,64},{4,65},{5,66},{6,67},{7,68},{8,69},{9,... | collective-permute-start | bytes 122888 | tf_op jit(solution)/shard_map/ppermute | solution.py:22
  305.9 33.4 %collective-permute-start.49 = (f32[4,2560]{1,0:T(4,128)}, f32[4,2560]{1,0:T(4,128)}, u32[]{:S(2)}, u32[]{:S(2)}) collective-permute-start(f32[4,2560]{1,0:T(4,128)} %reshape.860), channel_id=1, source_target_pairs={{0,62},{1,63},{2,64},{3,65},{4,66},{5,67},{6,68},{7,69},{8,70},{9,... | collective-permute-start | bytes 122888 | tf_op jit(solution)/shard_map/ppermute | solution.py:22
  311.9 31.6 %collective-permute-start.50 = (f32[4,2560]{1,0:T(4,128)}, f32[4,2560]{1,0:T(4,128)}, u32[]{:S(2)}, u32[]{:S(2)}) collective-permute-start(f32[4,2560]{1,0:T(4,128)} %reshape.860), channel_id=1, source_target_pairs={{0,63},{1,64},{2,65},{3,66},{4,67},{5,68},{6,69},{7,70},{8,71},{9,... | collective-permute-start | bytes 122888 | tf_op jit(solution)/shard_map/ppermute | solution.py:22
  313.8 34.4 %collective-permute-start.51 = (f32[4,2560]{1,0:T(4,128)}, f32[4,2560]{1,0:T(4,128)}, u32[]{:S(2)}, u32[]{:S(2)}) collective-permute-start(f32[4,2560]{1,0:T(4,128)} %reshape.860), channel_id=1, source_target_pairs={{0,64},{1,65},{2,66},{3,67},{4,68},{5,69},{6,70},{7,71},{8,72},{9,... | collective-permute-start | bytes 122888 | tf_op jit(solution)/shard_map/ppermute | solution.py:22
  313.9 49.8 %collective-permute-start.52 = (f32[4,2560]{1,0:T(4,128)}, f32[4,2560]{1,0:T(4,128)}, u32[]{:S(2)}, u32[]{:S(2)}) collective-permute-start(f32[4,2560]{1,0:T(4,128)} %reshape.860), channel_id=1, source_target_pairs={{0,65},{1,66},{2,67},{3,68},{4,69},{5,70},{6,71},{7,72},{8,73},{9,... | collective-permute-start | bytes 122888 | tf_op jit(solution)/shard_map/ppermute | solution.py:22
  334.2 32.1 %collective-permute-start.53 = (f32[4,2560]{1,0:T(4,128)}, f32[4,2560]{1,0:T(4,128)}, u32[]{:S(2)}, u32[]{:S(2)}) collective-permute-start(f32[4,2560]{1,0:T(4,128)} %reshape.860), channel_id=1, source_target_pairs={{0,66},{1,67},{2,68},{3,69},{4,70},{5,71},{6,72},{7,73},{8,74},{9,... | collective-permute-start | bytes 122888 | tf_op jit(solution)/shard_map/ppermute | solution.py:22
  339.3 28.2 %collective-permute-start.54 = (f32[4,2560]{1,0:T(4,128)}, f32[4,2560]{1,0:T(4,128)}, u32[]{:S(2)}, u32[]{:S(2)}) collective-permute-start(f32[4,2560]{1,0:T(4,128)} %reshape.860), channel_id=1, source_target_pairs={{0,67},{1,68},{2,69},{3,70},{4,71},{5,72},{6,73},{7,74},{8,75},{9,... | collective-permute-start | bytes 122888 | tf_op jit(solution)/shard_map/ppermute | solution.py:22
  343.6 30.6 %collective-permute-start.55 = (f32[4,2560]{1,0:T(4,128)}, f32[4,2560]{1,0:T(4,128)S(1)}, u32[]{:S(2)}, u32[]{:S(2)}) collective-permute-start(f32[4,2560]{1,0:T(4,128)} %reshape.862), channel_id=1, source_target_pairs={{0,957},{1,958},{2,959},{3,960},{4,961},{5,962},{6,963},{7,964},{8... | collective-permute-start | bytes 122888 | tf_op jit(solution)/shard_map/ppermute | solution.py:22
  348.2 30.9 %collective-permute-start.56 = (f32[4,2560]{1,0:T(4,128)}, f32[4,2560]{1,0:T(4,128)S(1)}, u32[]{:S(2)}, u32[]{:S(2)}) collective-permute-start(f32[4,2560]{1,0:T(4,128)} %reshape.862), channel_id=1, source_target_pairs={{0,958},{1,959},{2,960},{3,961},{4,962},{5,963},{6,964},{7,965},{8... | collective-permute-start | bytes 122888 | tf_op jit(solution)/shard_map/ppermute | solution.py:22
  363.7 22.0 %collective-permute-start.57 = (f32[4,2560]{1,0:T(4,128)}, f32[4,2560]{1,0:T(4,128)S(1)}, u32[]{:S(2)}, u32[]{:S(2)}) collective-permute-start(f32[4,2560]{1,0:T(4,128)} %reshape.862), channel_id=1, source_target_pairs={{0,959},{1,960},{2,961},{3,962},{4,963},{5,964},{6,965},{7,966},{8... | collective-permute-start | bytes 122888 | tf_op jit(solution)/shard_map/ppermute | solution.py:22
  366.3 22.2 %collective-permute-start.58 = (f32[4,2560]{1,0:T(4,128)}, f32[4,2560]{1,0:T(4,128)S(1)}, u32[]{:S(2)}, u32[]{:S(2)}) collective-permute-start(f32[4,2560]{1,0:T(4,128)} %reshape.862), channel_id=1, source_target_pairs={{0,960},{1,961},{2,962},{3,963},{4,964},{5,965},{6,966},{7,967},{8... | collective-permute-start | bytes 122888 | tf_op jit(solution)/shard_map/ppermute | solution.py:22
  367.5 27.4 %collective-permute-start.59 = (f32[4,2560]{1,0:T(4,128)}, f32[4,2560]{1,0:T(4,128)S(1)}, u32[]{:S(2)}, u32[]{:S(2)}) collective-permute-start(f32[4,2560]{1,0:T(4,128)} %reshape.862), channel_id=1, source_target_pairs={{0,961},{1,962},{2,963},{3,964},{4,965},{5,966},{6,967},{7,968},{8... | collective-permute-start | bytes 122888 | tf_op jit(solution)/shard_map/ppermute | solution.py:22
  374.2 22.7 %collective-permute-start.60 = (f32[4,2560]{1,0:T(4,128)}, f32[4,2560]{1,0:T(4,128)S(1)}, u32[]{:S(2)}, u32[]{:S(2)}) collective-permute-start(f32[4,2560]{1,0:T(4,128)} %reshape.862), channel_id=1, source_target_pairs={{0,962},{1,963},{2,964},{3,965},{4,966},{5,967},{6,968},{7,969},{8... | collective-permute-start | bytes 122888 | tf_op jit(solution)/shard_map/ppermute | solution.py:22
  379.2 25.2 %collective-permute-start.61 = (f32[4,2560]{1,0:T(4,128)}, f32[4,2560]{1,0:T(4,128)S(1)}, u32[]{:S(2)}, u32[]{:S(2)}) collective-permute-start(f32[4,2560]{1,0:T(4,128)} %reshape.862), channel_id=1, source_target_pairs={{0,963},{1,964},{2,965},{3,966},{4,967},{5,968},{6,969},{7,970},{8... | collective-permute-start | bytes 122888 | tf_op jit(solution)/shard_map/ppermute | solution.py:22
  385.7 23.0 %collective-permute-start.34 = (f32[16,2560]{1,0:T(8,128)}, f32[16,2560]{1,0:T(8,128)S(1)}, u32[]{:S(2)}, u32[]{:S(2)}) collective-permute-start(f32[16,2560]{1,0:T(8,128)} %pad_maximum_fusion.7), channel_id=1, source_target_pairs={{0,1},{1,2},{2,3},{3,4},{4,5},{5,6},{6,7},{7,8},{8,9},{9,10},{10,1... | collective-permute-start | bytes 491528 | tf_op jit(solution)/shard_map/ppermute | solution.py:22
  388.5 26.3 %collective-permute-start.35 = (f32[16,2560]{1,0:T(8,128)}, f32[16,2560]{1,0:T(8,128)S(1)}, u32[]{:S(2)}, u32[]{:S(2)}) collective-permute-start(f32[16,2560]{1,0:T(8,128)} %pad_maximum_fusion.7), channel_id=1, source_target_pairs={{0,63},{1,0},{2,1},{3,2},{4,3},{5,4},{6,5},{7,6},{8,7},{9,8},{10,9... | collective-permute-start | bytes 491528 | tf_op jit(solution)/shard_map/ppermute | solution.py:22
  394.9 21.8 %collective-permute-start.36 = (f32[16,2560]{1,0:T(8,128)}, f32[16,2560]{1,0:T(8,128)S(1)}, u32[]{:S(2)}, u32[]{:S(2)}) collective-permute-start(f32[16,2560]{1,0:T(8,128)} %pad_maximum_fusion.7), channel_id=1, source_target_pairs={{0,2},{1,3},{2,4},{3,5},{4,6},{5,7},{6,8},{7,9},{8,10},{9,11},{10,... | collective-permute-start | bytes 491528 | tf_op jit(solution)/shard_map/ppermute | solution.py:22
  396.9 25.0 %collective-permute-start.37 = (f32[16,2560]{1,0:T(8,128)}, f32[16,2560]{1,0:T(8,128)S(1)}, u32[]{:S(2)}, u32[]{:S(2)}) collective-permute-start(f32[16,2560]{1,0:T(8,128)} %pad_maximum_fusion.7), channel_id=1, source_target_pairs={{0,62},{1,63},{2,0},{3,1},{4,2},{5,3},{6,4},{7,5},{8,6},{9,7},{10,... | collective-permute-start | bytes 491528 | tf_op jit(solution)/shard_map/ppermute | solution.py:22
  404.4 19.5 %collective-permute-start.38 = (f32[16,2560]{1,0:T(8,128)}, f32[16,2560]{1,0:T(8,128)S(1)}, u32[]{:S(2)}, u32[]{:S(2)}) collective-permute-start(f32[16,2560]{1,0:T(8,128)} %pad_maximum_fusion.7), channel_id=1, source_target_pairs={{0,3},{1,4},{2,5},{3,6},{4,7},{5,8},{6,9},{7,10},{8,11},{9,12},{10... | collective-permute-start | bytes 491528 | tf_op jit(solution)/shard_map/ppermute | solution.py:22
  408.7 23.3 %collective-permute-start.39 = (f32[16,2560]{1,0:T(8,128)}, f32[16,2560]{1,0:T(8,128)S(1)}, u32[]{:S(2)}, u32[]{:S(2)}) collective-permute-start(f32[16,2560]{1,0:T(8,128)} %pad_maximum_fusion.7), channel_id=1, source_target_pairs={{0,61},{1,62},{2,63},{3,0},{4,1},{5,2},{6,3},{7,4},{8,5},{9,6},{10... | collective-permute-start | bytes 491528 | tf_op jit(solution)/shard_map/ppermute | solution.py:22
  414.8 19.2 %collective-permute-start.40 = (f32[16,2560]{1,0:T(8,128)}, f32[16,2560]{1,0:T(8,128)S(1)}, u32[]{:S(2)}, u32[]{:S(2)}) collective-permute-start(f32[16,2560]{1,0:T(8,128)} %pad_maximum_fusion.7), channel_id=1, source_target_pairs={{0,4},{1,5},{2,6},{3,7},{4,8},{5,9},{6,10},{7,11},{8,12},{9,13},{1... | collective-permute-start | bytes 491528 | tf_op jit(solution)/shard_map/ppermute | solution.py:22
  416.7 25.7 %collective-permute-start.41 = (f32[16,2560]{1,0:T(8,128)}, f32[16,2560]{1,0:T(8,128)S(1)}, u32[]{:S(2)}, u32[]{:S(2)}) collective-permute-start(f32[16,2560]{1,0:T(8,128)} %pad_maximum_fusion.7), channel_id=1, source_target_pairs={{0,60},{1,61},{2,62},{3,63},{4,0},{5,1},{6,2},{7,3},{8,4},{9,5},{1... | collective-permute-start | bytes 491528 | tf_op jit(solution)/shard_map/ppermute | solution.py:22
  421.9 22.5 %collective-permute-start.42 = (f32[16,2560]{1,0:T(8,128)}, f32[16,2560]{1,0:T(8,128)S(1)}, u32[]{:S(2)}, u32[]{:S(2)}) collective-permute-start(f32[16,2560]{1,0:T(8,128)} %pad_maximum_fusion.7), channel_id=1, source_target_pairs={{0,5},{1,6},{2,7},{3,8},{4,9},{5,10},{6,11},{7,12},{8,13},{9,14},{... | collective-permute-start | bytes 491528 | tf_op jit(solution)/shard_map/ppermute | solution.py:22
  423.9 28.4 %collective-permute-start.43 = (f32[16,2560]{1,0:T(8,128)}, f32[16,2560]{1,0:T(8,128)S(1)}, u32[]{:S(2)}, u32[]{:S(2)}) collective-permute-start(f32[16,2560]{1,0:T(8,128)} %pad_maximum_fusion.7), channel_id=1, source_target_pairs={{0,59},{1,60},{2,61},{3,62},{4,63},{5,0},{6,1},{7,2},{8,3},{9,4},{... | collective-permute-start | bytes 491528 | tf_op jit(solution)/shard_map/ppermute | solution.py:22
  432.0 20.2 %collective-permute-start.44 = (f32[16,2560]{1,0:T(8,128)}, f32[16,2560]{1,0:T(8,128)S(1)}, u32[]{:S(2)}, u32[]{:S(2)}) collective-permute-start(f32[16,2560]{1,0:T(8,128)} %pad_maximum_fusion.7), channel_id=1, source_target_pairs={{0,6},{1,7},{2,8},{3,9},{4,10},{5,11},{6,12},{7,13},{8,14},{9,15},... | collective-permute-start | bytes 491528 | tf_op jit(solution)/shard_map/ppermute | solution.py:22
  434.0 18.3 %collective-permute-start.45 = (f32[16,2560]{1,0:T(8,128)}, f32[16,2560]{1,0:T(8,128)S(1)}, u32[]{:S(2)}, u32[]{:S(2)}) collective-permute-start(f32[16,2560]{1,0:T(8,128)} %pad_maximum_fusion.7), channel_id=1, source_target_pairs={{0,58},{1,59},{2,60},{3,61},{4,62},{5,63},{6,0},{7,1},{8,2},{9,3},... | collective-permute-start | bytes 491528 | tf_op jit(solution)/shard_map/ppermute | solution.py:22
  442.4 10.5 %collective-permute-start.46 = (f32[16,2560]{1,0:T(8,128)}, f32[16,2560]{1,0:T(8,128)}, u32[]{:S(2)}, u32[]{:S(2)}) collective-permute-start(f32[16,2560]{1,0:T(8,128)} %pad_maximum_fusion.7), channel_id=1, source_target_pairs={{0,7},{1,8},{2,9},{3,10},{4,11},{5,12},{6,13},{7,14},{8,15},{9,16}... | collective-permute-start | bytes 491528 | tf_op jit(solution)/shard_map/ppermute | solution.py:22
  444.4 10.1 %collective-permute-start.47 = (f32[16,2560]{1,0:T(8,128)}, f32[16,2560]{1,0:T(8,128)}, u32[]{:S(2)}, u32[]{:S(2)}) collective-permute-start(f32[16,2560]{1,0:T(8,128)} %pad_maximum_fusion.7), channel_id=1, source_target_pairs={{0,57},{1,58},{2,59},{3,60},{4,61},{5,62},{6,63},{7,0},{8,1},{9,2}... | collective-permute-start | bytes 491528 | tf_op jit(solution)/shard_map/ppermute | solution.py:22
  (61 other events, 1246.8 us)
where the time goes:
time: 518 us; the launch traced here: 508 us
  starting transfers between devices  262 us (51%)
  local copies, waits for them, and re-layouts  176 us (34%)
  other arithmetic  64.4 us (12%)
    ppermute x56, starting transfers between devices, shifted(): lax.ppermute(value, axis, [(i, (i + by) % peers) for i in range(peers)])  240 us
    another operation x29, local copies, waits for them, and re-layouts, sweep(): return jnp.stack([flux[0:inner] - flux[1:inner + 1] for flux in fluxes], 2)  35.8 us
    concatenate x2, local copies, waits for them, and re-layouts, derivative(): plane_pool = jnp.concatenate([plane_set] + arrived, 0)  24.3 us
    ppermute x6, starting transfers between devices, from_behind(): return lax.ppermute(block, axis, route)  21.9 us
    unnamed x144, local copies, waits for them, and re-layouts  19.8 us
    slice x6, local copies, waits for them, and re-layouts, derivative(): high_x = pack(along_x[BLOCK - 2:])  16.3 us
    sub x20, other arithmetic, sweep(): return jnp.stack([flux[0:inner] - flux[1:inner + 1] for flux in fluxes], 2)  14.3 us
    add x4, local copies, waits for them, and re-layouts, derivative(): change_x.reshape(row_blocks, 5, BLOCK ** 3)  11.7 us
  transfers between devices with their start and end apart: 62, of which 3 were waited for; matrix products, arithmetic and copies ran while one was open for 19% of the time, Pallas kernels for 0%

commit v1 on v0

v1 whole, which is shorter than its diff:
```python
import jax
import jax.numpy as jnp
from jax import lax
from jax.experimental import pallas as pl
from jax.experimental.pallas import tpu as pltpu
from jax.sharding import PartitionSpec as P


FIELDS = 5
GROUP = 4
SLOTS = 4
KEYS = 8
ROWS = 8
LANES = 128
QUARTER = 4
HALO = 4

TIME_STEP = 0.08
GAMMA = 1.4

VMEM = pl.BlockSpec(memory_space=pltpu.VMEM)
SMEM = pl.BlockSpec(memory_space=pltpu.SMEM)


def call(kernel, out_shapes, in_specs, scratch=(), flops=0, data=1 << 20):
    return pl.pallas_call(
        kernel,
        out_shape=out_shapes,
        in_specs=in_specs,
        out_specs=jax.tree.map(lambda _: VMEM, out_shapes),
        scratch_shapes=list(scratch),
        compiler_params=pltpu.CompilerParams(vmem_limit_bytes=24 << 20),
        cost_estimate=pl.CostEstimate(flops=flops, bytes_accessed=data, transcendentals=0),
    )


def f32(*shape):
    return jax.ShapeDtypeStruct(shape, jnp.float32)


def split_kernel(state, message):
    for slot in range(SLOTS):
        for part in range(GROUP):
            for row in range(ROWS):
                chunk = (part * ROWS + row) * LANES
                message[part, slot, :, row, :] = state[slot, :, chunk : chunk + LANES]


def place_of(counts, key):
    position = jnp.int32(0)
    first = jnp.int32(0)
    upto = jnp.int32(0)
    for device in range(GROUP - 1):
        upto = upto + counts[device]
        beyond = upto <= key
        position = position + beyond.astype(jnp.int32)
        first = jnp.where(beyond, upto, first)
    return position, jnp.clip(key - first, 0, SLOTS - 1)


def edge_kernel(counts, received, lower, upper):
    for out, block_y, half in ((lower, 0, 0), (upper, 1, 1)):
        for xb in range(4):
            device, slot = place_of(counts, block_y * 4 + xb)
            to = (xb % 2) * 4
            for field in range(FIELDS):
                out[field, xb // 2, to : to + 4, :] = received[
                    device, slot, field, pl.ds(half, 4, stride=2), :
                ]


def gather_kernel(counts, received, from_above, from_below, piece):
    for block_y in range(2):
        for xb in range(4):
            device, slot = place_of(counts, block_y * 4 + xb)
            for field in range(FIELDS):
                for z in range(QUARTER):
                    piece[field, z * 2 + block_y, 2 * xb : 2 * xb + 2, :] = received[
                        device, slot, field, 2 * z : 2 * z + 2, :
                    ]
    lane = lax.broadcasted_iota(jnp.int32, (FIELDS, 2, ROWS, LANES), 3)
    piece[:, 8:10] = jnp.where(lane < 64, from_above[...], from_below[...])


def minmod(left, right):
    return jnp.maximum(jnp.minimum(left, right), 0.0) + jnp.minimum(jnp.maximum(left, right), 0.0)


def primitives(conserved):
    density, mx, my, mz, energy = conserved
    inverse = 1.0 / density
    vx, vy, vz = mx * inverse, my * inverse, mz * inverse
    pressure = (GAMMA - 1.0) * (energy - 0.5 * (mx * vx + my * vy + mz * vz))
    return [density, vx, vy, vz, pressure]


def face_terms(primitive, normal):
    density, vx, vy, vz, pressure = primitive
    energy = pressure * (1.0 / (GAMMA - 1.0)) + (0.5 * density) * (vx * vx + vy * vy + vz * vz)
    conserved = [density, density * vx, density * vy, density * vz, energy]
    stiff = GAMMA * pressure
    sound = stiff * lax.rsqrt(stiff * density)
    return conserved, primitive[1 + normal], pressure, sound


def face_flux(left, right, normal):
    left_u, left_v, left_p, left_c = face_terms(left, normal)
    right_u, right_v, right_p, right_c = face_terms(right, normal)
    fastest = jnp.maximum(jnp.maximum(left_v + left_c, right_v + right_c), 0.0)
    slowest = jnp.minimum(jnp.minimum(left_v - left_c, right_v - right_c), 0.0)
    inverse = 1.0 / (fastest - slowest)
    plus = fastest * inverse
    minus = slowest * inverse
    left_weight = plus * (left_v - slowest)
    right_weight = minus * (right_v - fastest)
    left_push = plus * left_p
    right_push = minus * right_p
    fluxes = [left_weight * a - right_weight * b for a, b in zip(left_u, right_u)]
    fluxes[1 + normal] = fluxes[1 + normal] + (left_push - right_push)
    fluxes[4] = fluxes[4] + (left_push * left_v - right_push * right_v)
    return fluxes


def shift_x(value, amount):
    axis = value.ndim - 1
    x = lax.broadcasted_iota(jnp.int32, value.shape, axis) % 16
    if amount > 0:
        inner = pltpu.roll(value, 1, axis)
        outer = pltpu.roll(pltpu.roll(value, 2, axis - 1), LANES - 15, axis)
        return jnp.where(x == 0, outer, inner)
    inner = pltpu.roll(value, LANES - 1, axis)
    outer = pltpu.roll(pltpu.roll(value, ROWS - 2, axis - 1), 15, axis)
    return jnp.where(x == 15, outer, inner)


def shift_y(value, amount):
    lane = lax.broadcasted_iota(jnp.int32, (ROWS, LANES), 1)
    odd = lax.broadcasted_iota(jnp.int32, (ROWS, LANES), 0) % 2 == 1
    if amount > 0:
        moved = [pltpu.roll(v, 16, 1) for v in value]
        edge = [
            jnp.where(odd, pltpu.roll(moved[i], 1, 0), pltpu.roll(moved[i - 1], ROWS - 1, 0))
            for i in range(3)
        ]
        return [jnp.where(lane < 16, e, m) for e, m in zip(edge, moved)]
    moved = [pltpu.roll(v, LANES - 16, 1) for v in value]
    edge = [
        jnp.where(odd, pltpu.roll(moved[(i + 1) % 3], 1, 0), pltpu.roll(moved[i], ROWS - 1, 0))
        for i in range(3)
    ]
    return [jnp.where(lane >= LANES - 16, e, m) for e, m in zip(edge, moved)]


def sweep_x(primitive):
    ahead = [shift_x(q, -1) for q in primitive]
    steps = [b - q for q, b in zip(primitive, ahead)]
    half = [0.5 * minmod(shift_x(d, 1), d) for d in steps]
    left = [q + h for q, h in zip(primitive, half)]
    right = [shift_x(q - h, -1) for q, h in zip(primitive, half)]
    return [shift_x(f, 1) - f for f in face_flux(left, right, 0)]


def sweep_y(primitive):
    left, right = [], []
    for q in primitive:
        ahead = shift_y(q, -1)
        steps = [b - a for a, b in zip(q, ahead)]
        behind = shift_y(steps, 1)
        half = [0.5 * minmod(b, d) for b, d in zip(behind, steps)]
        left.append([a + h for a, h in zip(q, half)])
        right.append(shift_y([a - h for a, h in zip(q, half)], -1))
    fluxes = [face_flux([l[i] for l in left], [r[i] for r in right], 1) for i in range(3)]
    out = []
    for field in range(FIELDS):
        flux = [fluxes[i][field] for i in range(3)]
        out.append([b - f for b, f in zip(shift_y(flux, 1), flux)])
    return out


def rate_into(total, prim, count, width):
    def plane(z, carry):
        for i in range(width):
            values = [prim[f, z + 2, i] for f in range(FIELDS)]
            for f, change in enumerate(sweep_x(values)):
                total[f, z, i] = change
        changes = sweep_y([[prim[f, z + 2, i] for i in range(3)] for f in range(FIELDS)])
        for f in range(FIELDS):
            for i in range(width):
                total[f, z, i] = total[f, z, i] + changes[f][i]
        return carry

    lax.fori_loop(0, count, plane, 0)

    for i in range(width):
        here = [prim[f, 1, i] for f in range(FIELDS)]
        step = [h - prim[f, 0, i] for f, h in enumerate(here)]
        ahead = [prim[f, 2, i] for f in range(FIELDS)]
        ahead_step = [a - h for a, h in zip(ahead, here)]
        half = [0.5 * minmod(a, b) for a, b in zip(step, ahead_step)]

        def face(z, state):
            here, half, ahead, ahead_step, below = state
            beyond = [prim[f, z + 3, i] for f in range(FIELDS)]
            beyond_step = [b - a for a, b in zip(ahead, beyond)]
            ahead_half = [0.5 * minmod(a, b) for a, b in zip(ahead_step, beyond_step)]
            left = [q + h for q, h in zip(here, half)]
            right = [q - h for q, h in zip(ahead, ahead_half)]
            fluxes = face_flux(left, right, 2)
            return (ahead, ahead_half, beyond, beyond_step, fluxes)

        state = face(0, (here, half, ahead, ahead_step, None))

        def layer(z, state):
            below = state[4]
            state = face(z + 1, state)
            for f in range(FIELDS):
                total[f, z, i] = total[f, z, i] + (below[f] - state[4][f])
            return state

        lax.fori_loop(0, count, layer, state)


def advance_kernel(counts, low, own, high, message, u0, w0, u1, w1, change, done):
    for base, piece in ((0, low), (QUARTER, own), (2 * QUARTER, high)):
        for field in range(FIELDS):
            for z in range(QUARTER):
                for block_y in range(2):
                    u0[field, base + z, block_y] = piece[field, z * 2 + block_y]
                for xb in range(4):
                    row = (xb % 2) * 4 + z
                    halo = piece[field, 8 + xb // 2, row : row + 1, :]
                    u0[field, base + z, 2, 2 * xb : 2 * xb + 2, :] = jnp.broadcast_to(
                        halo, (2, LANES)
                    )

    def to_primitive(z, carry):
        for f, value in enumerate(primitives([u0[f, z] for f in range(FIELDS)])):
            w0[f, z] = value
        return carry

    lax.fori_loop(0, QUARTER + 2 * HALO, to_primitive, 0)
    rate_into(change, w0, QUARTER + HALO, 3)

    def first_step(z, carry):
        values = [u0[f, z + 2] + TIME_STEP * change[f, z] for f in range(FIELDS)]
        for f, value in enumerate(values):
            u1[f, z] = value
        for f, value in enumerate(primitives(values)):
            w1[f, z] = value
        return carry

    lax.fori_loop(0, QUARTER + HALO, first_step, 0)
    rate_into(change, w1, QUARTER, 2)

    for z in range(QUARTER):
        for field in range(FIELDS):
            for block_y in range(2):
                value = 0.5 * u0[field, z + HALO, block_y] + 0.5 * (
                    u1[field, z + 2, block_y] + TIME_STEP * change[field, z, block_y]
                )
                for xb in range(4):
                    done[block_y * 4 + xb, field, 2 * z : 2 * z + 2, :] = value[
                        2 * xb : 2 * xb + 2, :
                    ]

    start = jnp.int32(0)
    for device in range(GROUP):
        for slot in range(SLOTS):
            message[device, slot] = done[jnp.minimum(start + slot, KEYS - 1)]
        start = start + counts[device]


def join_kernel(count, received, state):
    for slot in range(SLOTS):
        valid = slot < count[0]
        for part in range(GROUP):
            for row in range(ROWS):
                chunk = (part * ROWS + row) * LANES
                value = received[part, slot, :, row, :]
                state[slot, :, chunk : chunk + LANES] = jnp.where(valid, value, 0.0)


def body(state_old, counts_old, counts_new):
    slabs = lax.axis_size("gz")
    places = lax.axis_size("blk")
    groups = places // GROUP
    slab = lax.axis_index("gz")
    place = lax.axis_index("blk")
    group = place // GROUP

    def row_of(counts):
        return lax.dynamic_slice(counts, (slab, group, 0), (1, 1, GROUP)).reshape(GROUP)

    old_here = row_of(counts_old)
    new_here = row_of(counts_new)
    count_here = lax.dynamic_slice(new_here, (place % GROUP,), (1,))
    members = [[g * GROUP + k for k in range(GROUP)] for g in range(groups)]

    def exchange(message):
        return lax.all_to_all(message, "blk", 0, 0, axis_index_groups=members)

    def along_y(value, by):
        route = [(i, (i + by * GROUP) % places) for i in range(places)]
        return lax.ppermute(value, "blk", route)

    def along_z(value, by):
        route = []
        for g in range(slabs):
            for i in range(places):
                layer = (g * GROUP + i % GROUP + by) % (slabs * GROUP)
                target = layer // GROUP * places + i // GROUP * GROUP + layer % GROUP
                route.append((g * places + i, target))
        return lax.ppermute(value, ("gz", "blk"), route)

    parts = f32(GROUP, SLOTS, FIELDS, ROWS, LANES)
    held = state_old.reshape(SLOTS, FIELDS, GROUP * ROWS * LANES)
    sent = call(split_kernel, parts, [VMEM])(held)
    received = exchange(sent)

    edge = f32(FIELDS, 2, ROWS, LANES)
    lower, upper = call(edge_kernel, [edge, edge], [SMEM, VMEM])(old_here, received)
    from_above = along_y(lower, -1)
    from_below = along_y(upper, 1)
    own = call(gather_kernel, f32(FIELDS, 10, ROWS, LANES), [SMEM, VMEM, VMEM, VMEM])(
        old_here, received, from_above, from_below
    )
    low = along_z(own, 1)
    high = along_z(own, -1)

    def work(layers):
        return pltpu.VMEM((FIELDS, layers, 3, ROWS, LANES), jnp.float32)

    deep, wide = QUARTER + 2 * HALO, QUARTER + HALO
    finished = call(
        advance_kernel,
        parts,
        [SMEM, VMEM, VMEM, VMEM],
        [work(deep), work(deep), work(wide), work(wide), work(wide)]
        + [pltpu.VMEM((KEYS, FIELDS, ROWS, LANES), jnp.float32)],
        flops=1 << 24,
    )(new_here, low, own, high)
    returned = exchange(finished)
    state = call(join_kernel, f32(SLOTS, FIELDS, GROUP * ROWS * LANES), [SMEM, VMEM])(
        count_here, returned
    )
    return state[None, None]


def solution(mesh):
    in_specs = (P("gz", "blk", None, None, None), P(), P())
    out_specs = P("gz", "blk", None, None, None)
    return jax.shard_map(body, mesh=mesh, in_specs=in_specs, out_specs=out_specs, check_vma=False)
```

time: 518 us -> 76.7 us (0.15)
  the two profiles are of different devices: /device:TPU:56 before, /device:TPU:1 now
where the time goes in v1:
time: 76.7 us; the launch traced here: 76.3 us
  starting transfers between devices  36.6 us (48%)
  waiting for transfers between devices  23.7 us (31%)
  Pallas kernels  11.4 us (15%)
  local copies, waits for them, and re-layouts  4.46 us (6%)
    ppermute x2, starting transfers between devices, along_y(): return lax.ppermute(value, 'blk', route)  20.1 us
    all_to_all x2, waiting for transfers between devices, exchange(): return lax.all_to_all(message, 'blk', 0, 0, axis_index_groups=members)  12 us
    pallas_call x1, Pallas kernels, body(): call(advance_kernel, parts, [SMEM, VMEM, VMEM, VMEM], [work(deep), work(d...  8.32 us
    all_to_all x2, starting transfers between devices, exchange(): return lax.all_to_all(message, 'blk', 0, 0, axis_index_groups=members)  8.3 us
    ppermute x2, starting transfers between devices, along_z(): return lax.ppermute(value, ('gz', 'blk'), route)  8.19 us
    ppermute x2, waiting for transfers between devices, along_z(): return lax.ppermute(value, ('gz', 'blk'), route)  7.68 us
    ppermute x2, waiting for transfers between devices, along_y(): return lax.ppermute(value, 'blk', route)  4.02 us
  transfers between devices with their start and end apart: 6, of which 5 were waited for; matrix products, arithmetic and copies ran while one was open for 3% of the time, Pallas kernels for 0%

profile of v1, /device:TPU:1, one launch (start us, length us, event | category | flops | bytes accessed | tf_op | source)
XLA Modules:
  0.0 76.3 jit_solution(16723961225695183629)
XLA Ops:
  0.0 0.0 copy-start
  0.0 1.2 %copy.7 = f32[1,1,4,5,4096]{4,3,2,1,0:T(8,128)S(1)} copy(f32[1,1,4,5,4096]{4,2,3,1,0:T(4,128)} %param.3) | data formatting | bytes 655360 | tf_op args[0]
  1.2 0.9 %shard_map.37 = f32[4,4,5,8,128]{4,3,2,1,0:T(8,128)} custom-call(f32[4,5,4096]{2,1,0:T(8,128)S(1)} %bitcast.6), custom_call_target="tpu_custom_call" | custom-call | bytes 1048576 | tf_op jit(solution)/shard_map/pallas_call | solution.py:317
  2.1 4.8 %all-to-all-start = ((f32[4,4,5,8,128]{4,3,2,1,0:T(8,128)}), f32[4,4,5,8,128]{4,3,2,1,0:T(8,128)S(1)}, u32[]{:S(2)}, u32[]{:S(2)}) async-start(f32[4,4,5,8,128]{4,3,2,1,0:T(8,128)} %shard_map.37), calls=%async_computation | async-start | bytes 655360 | tf_op jit(solution)/shard_map/all_to_all | solution.py:300
  7.0 0.0 copy-done
  7.0 0.2 dynamic-slice_reduce_fusion.counts
  7.2 5.7 %all-to-all-done.received = f32[4,4,5,8,128]{4,3,2,1,0:T(8,128)S(1)} async-done(((f32[4,4,5,8,128]{4,3,2,1,0:T(8,128)}), f32[4,4,5,8,128]{4,3,2,1,0:T(8,128)S(1)}, u32[]{:S(2)}, u32[]{:S(2)}) %all-to-all-start) | async-done | bytes 327712 | tf_op jit(solution)/shard_map/all_to_all | solution.py:300
  12.8 0.6 shard_map.38
  13.5 18.2 %collective-permute-start = (f32[5,2,8,128]{3,2,1,0:T(8,128)S(1)}, f32[5,2,8,128]{3,2,1,0:T(8,128)S(1)}, u32[]{:S(2)}, u32[]{:S(2)}) collective-permute-start(f32[5,2,8,128]{3,2,1,0:T(8,128)S(1)} %get-tuple-element.7), channel_id=1, source_target_pairs={{0,60},{1,61},{2,62},{3,63},{4,0},{5,1},{6,2},{7,3},{8,4},{9,5},{1... | collective-permute-start | bytes 122888 | tf_op jit(solution)/shard_map/ppermute | solution.py:304
  31.7 1.9 %collective-permute-start.1 = (f32[5,2,8,128]{3,2,1,0:T(8,128)S(1)}, f32[5,2,8,128]{3,2,1,0:T(8,128)S(1)}, u32[]{:S(2)}, u32[]{:S(2)}) collective-permute-start(f32[5,2,8,128]{3,2,1,0:T(8,128)S(1)} %get-tuple-element.8), channel_id=1, source_target_pairs={{0,4},{1,5},{2,6},{3,7},{4,8},{5,9},{6,10},{7,11},{8,12},{9,13},{1... | collective-permute-start | bytes 122888 | tf_op jit(solution)/shard_map/ppermute | solution.py:304
  33.6 0.0 collective-permute-done.from_above
  33.6 4.0 %collective-permute-done.1.from_below = f32[5,2,8,128]{3,2,1,0:T(8,128)S(1)} collective-permute-done((f32[5,2,8,128]{3,2,1,0:T(8,128)S(1)}, f32[5,2,8,128]{3,2,1,0:T(8,128)S(1)}, u32[]{:S(2)}, u32[]{:S(2)}) %collective-permute-start.1) | collective-permute-done | bytes 40992 | tf_op jit(solution)/shard_map/ppermute | solution.py:304
  37.7 0.6 shard_map.39.own
  38.3 6.3 %collective-permute-start.3 = (f32[5,10,8,128]{3,2,1,0:T(8,128)S(1)}, f32[5,10,8,128]{3,2,1,0:T(8,128)S(1)}, u32[]{:S(2)}, u32[]{:S(2)}) collective-permute-start(f32[5,10,8,128]{3,2,1,0:T(8,128)S(1)} %shard_map.39.own), channel_id=1, source_target_pairs={{0,963},{1,0},{2,1},{3,2},{4,967},{5,4},{6,5},{7,6},{8,971},{9,8},... | collective-permute-start | bytes 614408 | tf_op jit(solution)/shard_map/ppermute | solution.py:313
  44.6 1.9 %collective-permute-start.2 = (f32[5,10,8,128]{3,2,1,0:T(8,128)S(1)}, f32[5,10,8,128]{3,2,1,0:T(8,128)S(1)}, u32[]{:S(2)}, u32[]{:S(2)}) collective-permute-start(f32[5,10,8,128]{3,2,1,0:T(8,128)S(1)} %shard_map.39.own), channel_id=1, source_target_pairs={{0,1},{1,2},{2,3},{3,64},{4,5},{5,6},{6,7},{7,68},{8,9},{9,10},{10... | collective-permute-start | bytes 614408 | tf_op jit(solution)/shard_map/ppermute | solution.py:313
  46.5 0.9 %dynamic-slice_reduce_fusion.1.counts = s32[4]{0:T(128)S(1)} fusion(s32[16,16,4]{1,2,0:T(4,128)} %param.5, s32[]{:T(128)S(6)} %select_n.28, s32[]{:T(128)S(6)} %select_n.31), kind=kLoop, calls=%fused_computation.2 | loop fusion | bytes 40 | tf_op jit(solution)/shard_map/dynamic_slice | solution.py:292
  47.4 2.1 %collective-permute-done.3.high = f32[5,10,8,128]{3,2,1,0:T(8,128)S(1)} collective-permute-done((f32[5,10,8,128]{3,2,1,0:T(8,128)S(1)}, f32[5,10,8,128]{3,2,1,0:T(8,128)S(1)}, u32[]{:S(2)}, u32[]{:S(2)}) %collective-permute-start.3) | collective-permute-done | bytes 204832 | tf_op jit(solution)/shard_map/ppermute | solution.py:313
  49.5 5.6 %collective-permute-done.2.low = f32[5,10,8,128]{3,2,1,0:T(8,128)S(1)} collective-permute-done((f32[5,10,8,128]{3,2,1,0:T(8,128)S(1)}, f32[5,10,8,128]{3,2,1,0:T(8,128)S(1)}, u32[]{:S(2)}, u32[]{:S(2)}) %collective-permute-start.2) | collective-permute-done | bytes 204832 | tf_op jit(solution)/shard_map/ppermute | solution.py:313
  55.1 8.3 %shard_map.40 = f32[4,4,5,8,128]{4,3,2,1,0:T(8,128)} custom-call(s32[4]{0:T(128)S(1)} %dynamic-slice_reduce_fusion.1.counts, f32[5,10,8,128]{3,2,1,0:T(8,128)S(1)} %collective-permute-done.2.low, f32[5,10,8,128]{3,2,1,0:T(8,128)S(1)} %shard_map.39.own, f32[5,10,8,128]{3,2,1,0:T(8,128)S(1)} %collective-permute-done.3.high), custom_call_target="tpu_custom_call" | custom-call | flops 16777216 | bytes 1048576 | tf_op jit(solution)/shard_map/pallas_call | solution.py:334
  63.4 3.5 %all-to-all-start.1 = ((f32[4,4,5,8,128]{4,3,2,1,0:T(8,128)}), f32[4,4,5,8,128]{4,3,2,1,0:T(8,128)S(1)}, u32[]{:S(2)}, u32[]{:S(2)}) async-start(f32[4,4,5,8,128]{4,3,2,1,0:T(8,128)} %shard_map.40), calls=%async_computation.1 | async-start | bytes 655360 | tf_op jit(solution)/shard_map/all_to_all | solution.py:300
  66.9 1.3 %dynamic_slice.11 = s32[1,1,1]{1,2,0:T(1,128)} dynamic-slice(s32[16,16,4]{1,2,0:T(4,128)} %param.5, s32[]{:T(128)S(6)} %select_n.29, s32[]{:T(128)S(6)} %select_n.32, s32[]{:T(128)S(6)} %select_n.35), dynamic_slice_sizes={1,1,1} | dynamic-slice | bytes 12 | tf_op jit(solution)/shard_map/dynamic_slice | solution.py:296
  68.2 6.3 %all-to-all-done.1.received = f32[4,4,5,8,128]{4,3,2,1,0:T(8,128)S(1)} async-done(((f32[4,4,5,8,128]{4,3,2,1,0:T(8,128)}), f32[4,4,5,8,128]{4,3,2,1,0:T(8,128)S(1)}, u32[]{:S(2)}, u32[]{:S(2)}) %all-to-all-start.1) | async-done | bytes 327712 | tf_op jit(solution)/shard_map/all_to_all | solution.py:300
  74.4 0.9 %shard_map.41 = f32[4,5,4096]{2,1,0:T(8,128)S(1)} custom-call(s32[1]{0:T(128)} %bitcast.count, f32[4,4,5,8,128]{4,3,2,1,0:T(8,128)S(1)} %all-to-all-done.1.received), custom_call_target="tpu_custom_call" | custom-call | bytes 1048576 | tf_op jit(solution)/shard_map/pallas_call | solution.py:343
  75.3 0.9 %copy.5 = f32[1,1,4,5,4096]{4,2,3,1,0:T(4,128)} copy(f32[1,1,4,5,4096]{4,3,2,1,0:T(8,128)S(1)} %bitcast.5) | data formatting | bytes 655360 | tf_op jit(solution)/shard_map/broadcast_in_dim | solution.py:346
Async XLA Ops:
  0.0 7.0 %copy-start = (s32[16,16,4]{1,2,0:T(4,128)S(1)}, s32[16,16,4]{1,2,0:T(4,128)}, u32[]{:S(2)}) copy-start(s32[16,16,4]{1,2,0:T(4,128)} %param.4) | copy-start | bytes 12292
  2.1 10.7 %all-to-all-start = ((f32[4,4,5,8,128]{4,3,2,1,0:T(8,128)}), f32[4,4,5,8,128]{4,3,2,1,0:T(8,128)S(1)}, u32[]{:S(2)}, u32[]{:S(2)}) async-start(f32[4,4,5,8,128]{4,3,2,1,0:T(8,128)} %shard_map.37), calls=%async_computation | async-start | bytes 655360 | tf_op jit(solution)/shard_map/all_to_all | solution.py:300
  13.5 20.2 %collective-permute-start = (f32[5,2,8,128]{3,2,1,0:T(8,128)S(1)}, f32[5,2,8,128]{3,2,1,0:T(8,128)S(1)}, u32[]{:S(2)}, u32[]{:S(2)}) collective-permute-start(f32[5,2,8,128]{3,2,1,0:T(8,128)S(1)} %get-tuple-element.7), channel_id=1, source_target_pairs={{0,60},{1,61},{2,62},{3,63},{4,0},{5,1},{6,2},{7,3},{8,4},{9,5},{1... | collective-permute-start | bytes 122888 | tf_op jit(solution)/shard_map/ppermute | solution.py:304
  31.7 6.0 %collective-permute-start.1 = (f32[5,2,8,128]{3,2,1,0:T(8,128)S(1)}, f32[5,2,8,128]{3,2,1,0:T(8,128)S(1)}, u32[]{:S(2)}, u32[]{:S(2)}) collective-permute-start(f32[5,2,8,128]{3,2,1,0:T(8,128)S(1)} %get-tuple-element.8), channel_id=1, source_target_pairs={{0,4},{1,5},{2,6},{3,7},{4,8},{5,9},{6,10},{7,11},{8,12},{9,13},{1... | collective-permute-start | bytes 122888 | tf_op jit(solution)/shard_map/ppermute | solution.py:304
  38.3 11.2 %collective-permute-start.3 = (f32[5,10,8,128]{3,2,1,0:T(8,128)S(1)}, f32[5,10,8,128]{3,2,1,0:T(8,128)S(1)}, u32[]{:S(2)}, u32[]{:S(2)}) collective-permute-start(f32[5,10,8,128]{3,2,1,0:T(8,128)S(1)} %shard_map.39.own), channel_id=1, source_target_pairs={{0,963},{1,0},{2,1},{3,2},{4,967},{5,4},{6,5},{7,6},{8,971},{9,8},... | collective-permute-start | bytes 614408 | tf_op jit(solution)/shard_map/ppermute | solution.py:313
  44.6 10.5 %collective-permute-start.2 = (f32[5,10,8,128]{3,2,1,0:T(8,128)S(1)}, f32[5,10,8,128]{3,2,1,0:T(8,128)S(1)}, u32[]{:S(2)}, u32[]{:S(2)}) collective-permute-start(f32[5,10,8,128]{3,2,1,0:T(8,128)S(1)} %shard_map.39.own), channel_id=1, source_target_pairs={{0,1},{1,2},{2,3},{3,64},{4,5},{5,6},{6,7},{7,68},{8,9},{9,10},{10... | collective-permute-start | bytes 614408 | tf_op jit(solution)/shard_map/ppermute | solution.py:313
  63.4 11.1 %all-to-all-start.1 = ((f32[4,4,5,8,128]{4,3,2,1,0:T(8,128)}), f32[4,4,5,8,128]{4,3,2,1,0:T(8,128)S(1)}, u32[]{:S(2)}, u32[]{:S(2)}) async-start(f32[4,4,5,8,128]{4,3,2,1,0:T(8,128)} %shard_map.40), calls=%async_computation.1 | async-start | bytes 655360 | tf_op jit(solution)/shard_map/all_to_all | solution.py:300

commit v2 on v1

v2 whole, which is shorter than its diff:
```python
import jax
import jax.numpy as jnp
from jax import lax
from jax.experimental import pallas as pl
from jax.experimental.pallas import tpu as pltpu
from jax.sharding import PartitionSpec as P


FIELDS = 5
GROUP = 4
SLOTS = 4
KEYS = 8
ROWS = 8
LANES = 128
QUARTER = 4
HALO = 4

TIME_STEP = 0.08
GAMMA = 1.4

VMEM = pl.BlockSpec(memory_space=pltpu.VMEM)
SMEM = pl.BlockSpec(memory_space=pltpu.SMEM)


def call(kernel, out_shapes, in_specs, scratch=(), flops=0, data=1 << 20):
    return pl.pallas_call(
        kernel,
        out_shape=out_shapes,
        in_specs=in_specs,
        out_specs=jax.tree.map(lambda _: VMEM, out_shapes),
        scratch_shapes=list(scratch),
        compiler_params=pltpu.CompilerParams(vmem_limit_bytes=24 << 20),
        cost_estimate=pl.CostEstimate(flops=flops, bytes_accessed=data, transcendentals=0),
    )


def f32(*shape):
    return jax.ShapeDtypeStruct(shape, jnp.float32)


def split_kernel(state, message):
    for field in range(FIELDS):
        for part in range(GROUP):
            for row in range(ROWS):
                chunk = (part * ROWS + row) * LANES
                message[part, field, 4 * row : 4 * row + 4, :] = state[
                    field, :, chunk : chunk + LANES
                ]


def place_of(counts, key):
    position = jnp.int32(0)
    first = jnp.int32(0)
    upto = jnp.int32(0)
    for device in range(GROUP - 1):
        upto = upto + counts[device]
        beyond = upto <= key
        position = position + beyond.astype(jnp.int32)
        first = jnp.where(beyond, upto, first)
    return position, jnp.clip(key - first, 0, SLOTS - 1)


def gather_kernel(counts, received, piece):
    for block_y in range(2):
        for xb in range(4):
            device, slot = place_of(counts, block_y * 4 + xb)
            for field in range(FIELDS):
                block = received[device, field, pl.ds(slot, ROWS, stride=SLOTS), :]
                for z in range(QUARTER):
                    piece[field, z * 2 + block_y, 2 * xb : 2 * xb + 2, :] = block[
                        2 * z : 2 * z + 2
                    ]


def layers_of(low, own, high):
    return [(low, 2), (low, 3)] + [(own, z) for z in range(QUARTER)] + [(high, 0), (high, 1)]


def edge_kernel(low, own, high, lower, upper):
    layers = layers_of(low, own, high)
    first_half = lax.broadcasted_iota(jnp.int32, (4, LANES), 1) < 64
    for field in range(FIELDS):
        for pair in range(4):
            to = (pair % 2) * 4

            def rows(index, block_y):
                piece, z = layers[index]
                return piece[field, z * 2 + block_y, pl.ds(block_y, 4, stride=2), :]

            lower[field, pair // 2, to : to + 4, :] = jnp.where(
                first_half, rows(pair, 0), pltpu.roll(rows(pair + 4, 0), 64, 1)
            )
            upper[field, pair // 2, to : to + 4, :] = jnp.where(
                first_half, pltpu.roll(rows(pair, 1), 64, 1), rows(pair + 4, 1)
            )


def minmod(left, right):
    return jnp.maximum(jnp.minimum(left, right), 0.0) + jnp.minimum(jnp.maximum(left, right), 0.0)


def primitives(conserved):
    density, mx, my, mz, energy = conserved
    inverse = 1.0 / density
    vx, vy, vz = mx * inverse, my * inverse, mz * inverse
    pressure = (GAMMA - 1.0) * (energy - 0.5 * (mx * vx + my * vy + mz * vz))
    return [density, vx, vy, vz, pressure]


def face_terms(primitive, normal):
    density, vx, vy, vz, pressure = primitive
    energy = pressure * (1.0 / (GAMMA - 1.0)) + (0.5 * density) * (vx * vx + vy * vy + vz * vz)
    conserved = [density, density * vx, density * vy, density * vz, energy]
    stiff = GAMMA * pressure
    sound = stiff * lax.rsqrt(stiff * density)
    return conserved, primitive[1 + normal], pressure, sound


def face_flux(left, right, normal):
    left_u, left_v, left_p, left_c = face_terms(left, normal)
    right_u, right_v, right_p, right_c = face_terms(right, normal)
    fastest = jnp.maximum(jnp.maximum(left_v + left_c, right_v + right_c), 0.0)
    slowest = jnp.minimum(jnp.minimum(left_v - left_c, right_v - right_c), 0.0)
    inverse = 1.0 / (fastest - slowest)
    plus = fastest * inverse
    minus = slowest * inverse
    left_weight = plus * (left_v - slowest)
    right_weight = minus * (right_v - fastest)
    left_push = plus * left_p
    right_push = minus * right_p
    fluxes = [left_weight * a - right_weight * b for a, b in zip(left_u, right_u)]
    fluxes[1 + normal] = fluxes[1 + normal] + (left_push - right_push)
    fluxes[4] = fluxes[4] + (left_push * left_v - right_push * right_v)
    return fluxes


def shift_x(value, amount):
    axis = value.ndim - 1
    x = lax.broadcasted_iota(jnp.int32, value.shape, axis) % 16
    if amount > 0:
        inner = pltpu.roll(value, 1, axis)
        outer = pltpu.roll(pltpu.roll(value, 2, axis - 1), LANES - 15, axis)
        return jnp.where(x == 0, outer, inner)
    inner = pltpu.roll(value, LANES - 1, axis)
    outer = pltpu.roll(pltpu.roll(value, ROWS - 2, axis - 1), 15, axis)
    return jnp.where(x == 15, outer, inner)


def shift_y(value, amount):
    shape = value[0].shape
    across, down = len(shape) - 1, len(shape) - 2
    lane = lax.broadcasted_iota(jnp.int32, shape, across)
    odd = lax.broadcasted_iota(jnp.int32, shape, down) % 2 == 1
    if amount > 0:
        moved = [pltpu.roll(v, 16, across) for v in value]
        upper = moved
        lower = [moved[i - 1] for i in range(3)]
        outer = lane < 16
    else:
        moved = [pltpu.roll(v, LANES - 16, across) for v in value]
        upper = [moved[(i + 1) % 3] for i in range(3)]
        lower = moved
        outer = lane >= LANES - 16
    edge = [
        jnp.where(odd, pltpu.roll(u, 1, down), pltpu.roll(l, ROWS - 1, down))
        for u, l in zip(upper, lower)
    ]
    return [jnp.where(outer, e, m) for e, m in zip(edge, moved)]


def sweep_x(primitive):
    ahead = [shift_x(q, -1) for q in primitive]
    steps = [b - q for q, b in zip(primitive, ahead)]
    half = [0.5 * minmod(shift_x(d, 1), d) for d in steps]
    left = [q + h for q, h in zip(primitive, half)]
    right = [shift_x(q - h, -1) for q, h in zip(primitive, half)]
    return [shift_x(f, 1) - f for f in face_flux(left, right, 0)]


def sweep_y(primitive):
    left, right = [], []
    for q in primitive:
        ahead = shift_y(q, -1)
        steps = [b - a for a, b in zip(q, ahead)]
        behind = shift_y(steps, 1)
        half = [0.5 * minmod(b, d) for b, d in zip(behind, steps)]
        left.append([a + h for a, h in zip(q, half)])
        right.append(shift_y([a - h for a, h in zip(q, half)], -1))
    fluxes = [face_flux([l[i] for l in left], [r[i] for r in right], 1) for i in range(3)]
    out = []
    for field in range(FIELDS):
        flux = [fluxes[i][field] for i in range(3)]
        out.append([b - f for b, f in zip(shift_y(flux, 1), flux)])
    return out


X_LAYERS = 4
Y_LAYERS = 4


def rate_x(total, prim, count, blocks):
    def planes(step, carry):
        z = step * X_LAYERS
        values = [prim[f, pl.ds(z + 2, X_LAYERS), blocks] for f in range(FIELDS)]
        for f, change in enumerate(sweep_x(values)):
            total[f, pl.ds(z, X_LAYERS), blocks] = change
        return carry

    lax.fori_loop(0, count // X_LAYERS, planes, 0)


def rate_z(total, prim, count, blocks):
    def load(z):
        return [prim[f, z, blocks] for f in range(FIELDS)]

    here, ahead = load(1), load(2)
    step = [h - b for h, b in zip(here, load(0))]
    ahead_step = [a - h for a, h in zip(ahead, here)]
    half = [0.5 * minmod(a, b) for a, b in zip(step, ahead_step)]

    def face(z, here, half, ahead, ahead_step):
        beyond = load(z + 3)
        beyond_step = [b - a for a, b in zip(ahead, beyond)]
        ahead_half = [0.5 * minmod(a, b) for a, b in zip(ahead_step, beyond_step)]
        left = [q + h for q, h in zip(here, half)]
        right = [q - h for q, h in zip(ahead, ahead_half)]
        return ahead, ahead_half, beyond, beyond_step, face_flux(left, right, 2)

    def layer(z, state):
        after = face(z + 1, *state[:4])
        for f in range(FIELDS):
            total[f, z, blocks] = total[f, z, blocks] + (state[4][f] - after[4][f])
        return after

    lax.fori_loop(0, count, layer, face(0, here, half, ahead, ahead_step))


INNER = slice(0, 2)
EDGE = slice(2, 3)


def inner_kernel(low, own, high, w0, change):
    for base, piece in ((0, low), (QUARTER, own), (2 * QUARTER, high)):

        def to_primitive(z, carry):
            values = [piece[f, pl.ds(2 * z, 2)] for f in range(FIELDS)]
            for f, value in enumerate(primitives(values)):
                w0[f, base + z] = value
            return carry

        lax.fori_loop(0, QUARTER, to_primitive, 0)
    rate_x(change, w0, QUARTER + HALO, INNER)
    rate_z(change, w0, QUARTER + HALO, INNER)


def advance_kernel(
    counts, low, own, high, w0, inner, from_above, from_below, message,
    uh, wh, changeh, total, u1, w1, change, done,
):
    wide = QUARTER + HALO
    first_half = lax.broadcasted_iota(jnp.int32, (4, LANES), 1) < 64
    for field in range(FIELDS):
        for pair in range(4):
            rows = slice((pair % 2) * 4, (pair % 2) * 4 + 4)
            above = from_above[field, pair // 2, rows, :]
            below = from_below[field, pair // 2, rows, :]
            for z, halo in (
                (pair, jnp.where(first_half, above, pltpu.roll(below, 64, 1))),
                (pair + 4, jnp.where(first_half, pltpu.roll(above, 64, 1), below)),
            ):
                uh[field, z, 0, pl.ds(0, 4, stride=2), :] = halo
                uh[field, z, 0, pl.ds(1, 4, stride=2), :] = halo
    for f, value in enumerate(primitives([uh[f] for f in range(FIELDS)])):
        wh[f] = value

    rate_x(changeh, wh, QUARTER, slice(0, 1))
    rate_z(changeh, wh, QUARTER, slice(0, 1))

    def planes(step, carry):
        z = step * Y_LAYERS
        here, shifted = pl.ds(z, Y_LAYERS), pl.ds(z + 2, Y_LAYERS)
        prims = [[w0[f, shifted, 0], w0[f, shifted, 1], wh[f, here, 0]] for f in range(FIELDS)]
        changes = sweep_y(prims)
        for f in range(FIELDS):
            for i in range(2):
                total[f, here, i] = inner[f, here, i] + changes[f][i]
            total[f, here, 2] = changes[f][2]
        return carry

    lax.fori_loop(0, wide // Y_LAYERS, planes, 0)

    for index, (piece, z) in enumerate(layers_of(low, own, high)):
        values = [
            piece[f, 2 * z : 2 * z + 2] + TIME_STEP * total[f, index, INNER]
            for f in range(FIELDS)
        ]
        for f, value in enumerate(values):
            u1[f, index] = value
        for f, value in enumerate(primitives(values)):
            w1[f, index, INNER] = value
    for z in range(QUARTER):
        values = [
            uh[f, z + 2] + TIME_STEP * (total[f, z + 2, EDGE] + changeh[f, z])
            for f in range(FIELDS)
        ]
        for f, value in enumerate(primitives(values)):
            w1[f, z + 2, EDGE] = value

    rate_x(change, w1, QUARTER, INNER)
    rate_z(change, w1, QUARTER, INNER)

    def last_planes(step, carry):
        z = step * Y_LAYERS
        here, shifted = pl.ds(z, Y_LAYERS), pl.ds(z + 2, Y_LAYERS)
        changes = sweep_y([[w1[f, shifted, i] for i in range(3)] for f in range(FIELDS)])
        for f in range(FIELDS):
            for i in range(2):
                change[f, here, i] = change[f, here, i] + changes[f][i]
        return carry

    lax.fori_loop(0, QUARTER // Y_LAYERS, last_planes, 0)

    for z in range(QUARTER):
        for field in range(FIELDS):
            for block_y in range(2):
                value = 0.5 * own[field, 2 * z + block_y] + 0.5 * (
                    u1[field, z + 2, block_y] + TIME_STEP * change[field, z, block_y]
                )
                for xb in range(4):
                    done[block_y * 4 + xb, field, 2 * z : 2 * z + 2, :] = value[
                        2 * xb : 2 * xb + 2, :
                    ]

    start = jnp.int32(0)
    for device in range(GROUP):
        for slot in range(SLOTS):
            key = jnp.minimum(start + slot, KEYS - 1)
            for field in range(FIELDS):
                message[device, field, pl.ds(slot, ROWS, stride=SLOTS), :] = done[key, field]
        start = start + counts[device]


def join_kernel(count, received, state):
    valid = lax.broadcasted_iota(jnp.int32, (SLOTS, LANES), 0) < count[0]
    for field in range(FIELDS):
        for part in range(GROUP):
            for row in range(ROWS):
                chunk = (part * ROWS + row) * LANES
                state[field, :, chunk : chunk + LANES] = jnp.where(
                    valid, received[part, field, 4 * row : 4 * row + 4, :], 0.0
                )


def body(state_old, counts_old, counts_new):
    slabs = lax.axis_size("gz")
    places = lax.axis_size("blk")
    groups = places // GROUP
    slab = lax.axis_index("gz")
    place = lax.axis_index("blk")
    group = place // GROUP

    def row_of(counts):
        return lax.dynamic_slice(counts, (slab, group, 0), (1, 1, GROUP)).reshape(GROUP)

    old_here = row_of(counts_old)
    new_here = row_of(counts_new)
    count_here = lax.dynamic_slice(new_here, (place % GROUP,), (1,))
    members = [[g * GROUP + k for k in range(GROUP)] for g in range(groups)]

    def exchange(message):
        return lax.all_to_all(message, "blk", 0, 0, axis_index_groups=members)

    def along_y(value, by):
        route = [(i, (i + by * GROUP) % places) for i in range(places)]
        return lax.ppermute(value, "blk", route)

    def along_z(value, by):
        route = []
        for g in range(slabs):
            for i in range(places):
                layer = (g * GROUP + i % GROUP + by) % (slabs * GROUP)
                target = layer // GROUP * places + i // GROUP * GROUP + layer % GROUP
                route.append((g * places + i, target))
        return lax.ppermute(value, ("gz", "blk"), route)

    parts = f32(GROUP, FIELDS, ROWS * SLOTS, LANES)
    cells = GROUP * ROWS * LANES
    wide = QUARTER + HALO
    held = state_old.reshape(SLOTS, FIELDS, cells).transpose(1, 0, 2)
    received = exchange(call(split_kernel, parts, [VMEM])(held))

    own = call(gather_kernel, f32(FIELDS, 2 * QUARTER, ROWS, LANES), [SMEM, VMEM])(
        old_here, received
    )
    low = along_z(own, 1)
    high = along_z(own, -1)

    edge = f32(FIELDS, 2, ROWS, LANES)
    lower, upper = call(edge_kernel, [edge, edge], [VMEM] * 3)(low, own, high)
    from_above = along_y(lower, -1)
    from_below = along_y(upper, 1)
    w0, inner = call(
        inner_kernel,
        [f32(FIELDS, wide + HALO, 2, ROWS, LANES), f32(FIELDS, wide, 2, ROWS, LANES)],
        [VMEM] * 3,
        flops=1 << 24,
    )(low, own, high)

    def work(*shape):
        return pltpu.VMEM((FIELDS,) + shape + (ROWS, LANES), jnp.float32)

    finished = call(
        advance_kernel,
        parts,
        [SMEM] + [VMEM] * 7,
        [work(wide, 1), work(wide, 1), work(QUARTER, 1), work(wide, 3)]
        + [work(wide, 2), work(wide, 3), work(QUARTER, 2)]
        + [pltpu.VMEM((KEYS, FIELDS, ROWS, LANES), jnp.float32)],
        flops=1 << 24,
    )(new_here, low, own, high, w0, inner, from_above, from_below)
    returned = exchange(finished)
    state = call(join_kernel, f32(FIELDS, SLOTS, cells), [SMEM, VMEM])(count_here, returned)
    return state.transpose(1, 0, 2)[None, None]


def solution(mesh):
    in_specs = (P("gz", "blk", None, None, None), P(), P())
    out_specs = P("gz", "blk", None, None, None)
    return jax.shard_map(body, mesh=mesh, in_specs=in_specs, out_specs=out_specs, check_vma=False)
```

time: 76.7 us -> 69.1 us (0.901)
  the two profiles are of different devices: /device:TPU:1 before, /device:TPU:2 now
where the time goes in v2:
time: 69.1 us; the launch traced here: 68.6 us
  starting transfers between devices  39 us (56%)
  waiting for transfers between devices  17.3 us (25%)
  Pallas kernels  8.84 us (13%)
  local copies, waits for them, and re-layouts  3.38 us (5%)
    all_to_all x2, starting transfers between devices, exchange(): return lax.all_to_all(message, 'blk', 0, 0, axis_index_groups=members)  24.5 us
    all_to_all x2, waiting for transfers between devices, exchange(): return lax.all_to_all(message, 'blk', 0, 0, axis_index_groups=members)  9.62 us
    ppermute x2, starting transfers between devices, along_y(): return lax.ppermute(value, 'blk', route)  8.7 us
    ppermute x2, starting transfers between devices, along_z(): return lax.ppermute(value, ('gz', 'blk'), route)  5.84 us
    ppermute x2, waiting for transfers between devices, along_z(): return lax.ppermute(value, ('gz', 'blk'), route)  5.06 us
    pallas_call x1, Pallas kernels, body(): call(advance_kernel, parts, [SMEM] + [VMEM] * 7, [work(wide, 1), work(wid...  4.25 us
    ppermute x2, waiting for transfers between devices, along_y(): return lax.ppermute(value, 'blk', route)  2.65 us
    pallas_call x1, Pallas kernels, body(): call(inner_kernel, [f32(FIELDS, wide + HALO, 2, ROWS, LANES), f32(FIELDS,...  1.64 us
  transfers between devices with their start and end apart: 6, of which 5 were waited for; matrix products, arithmetic and copies ran while one was open for 3% of the time, Pallas kernels for 2%

profile of v2, /device:TPU:2, one launch (start us, length us, event | category | flops | bytes accessed | tf_op | source)
XLA Modules:
  0.0 68.6 jit_solution(815071107412690751)
XLA Ops:
  0.0 0.0 copy-start
  0.0 0.0 copy-start.1
  0.0 1.0 %copy-done.1 = f32[1,1,4,5,4096]{4,2,3,1,0:T(4,128)S(1)} copy-done((f32[1,1,4,5,4096]{4,2,3,1,0:T(4,128)S(1)}, f32[1,1,4,5,4096]{4,2,3,1,0:T(4,128)}, u32[]{:S(2)}) %copy-start.1) | copy-done | bytes 327704
  1.0 0.7 %shard_map.37 = f32[4,5,32,128]{3,2,1,0:T(8,128)} custom-call(f32[5,4,4096]{2,1,0:T(4,128)S(1)} %bitcast.7), custom_call_target="tpu_custom_call" | custom-call | bytes 1048576 | tf_op jit(solution)/shard_map/pallas_call | solution.py:390
  1.7 16.6 %all-to-all-start = ((f32[4,5,32,128]{3,2,1,0:T(8,128)}), f32[4,5,32,128]{3,2,1,0:T(8,128)S(1)}, u32[]{:S(2)}, u32[]{:S(2)}) async-start(f32[4,5,32,128]{3,2,1,0:T(8,128)} %shard_map.37), calls=%async_computation | async-start | bytes 655360 | tf_op jit(solution)/shard_map/all_to_all | solution.py:371
  18.3 0.0 copy-done
  18.3 0.2 dynamic-slice_reduce_fusion.counts
  18.5 5.4 %all-to-all-done.received = f32[4,5,32,128]{3,2,1,0:T(8,128)S(1)} async-done(((f32[4,5,32,128]{3,2,1,0:T(8,128)}), f32[4,5,32,128]{3,2,1,0:T(8,128)S(1)}, u32[]{:S(2)}, u32[]{:S(2)}) %all-to-all-start) | async-done | bytes 327712 | tf_op jit(solution)/shard_map/all_to_all | solution.py:371
  23.9 0.6 shard_map.38.own
  24.5 3.4 %collective-permute-start.1 = (f32[5,8,8,128]{3,2,1,0:T(8,128)S(1)}, f32[5,8,8,128]{3,2,1,0:T(8,128)S(1)}, u32[]{:S(2)}, u32[]{:S(2)}) collective-permute-start(f32[5,8,8,128]{3,2,1,0:T(8,128)S(1)} %shard_map.38.own), channel_id=1, source_target_pairs={{0,963},{1,0},{2,1},{3,2},{4,967},{5,4},{6,5},{7,6},{8,971},{9,8},... | collective-permute-start | bytes 491528 | tf_op jit(solution)/shard_map/ppermute | solution.py:384
  27.9 2.5 %collective-permute-start = (f32[5,8,8,128]{3,2,1,0:T(8,128)S(1)}, f32[5,8,8,128]{3,2,1,0:T(8,128)S(1)}, u32[]{:S(2)}, u32[]{:S(2)}) collective-permute-start(f32[5,8,8,128]{3,2,1,0:T(8,128)S(1)} %shard_map.38.own), channel_id=1, source_target_pairs={{0,1},{1,2},{2,3},{3,64},{4,5},{5,6},{6,7},{7,68},{8,9},{9,10},{10... | collective-permute-start | bytes 491528 | tf_op jit(solution)/shard_map/ppermute | solution.py:384
  30.4 1.4 %collective-permute-done.1.high = f32[5,8,8,128]{3,2,1,0:T(8,128)S(1)} collective-permute-done((f32[5,8,8,128]{3,2,1,0:T(8,128)S(1)}, f32[5,8,8,128]{3,2,1,0:T(8,128)S(1)}, u32[]{:S(2)}, u32[]{:S(2)}) %collective-permute-start.1) | collective-permute-done | bytes 163872 | tf_op jit(solution)/shard_map/ppermute | solution.py:384
  31.7 3.7 %collective-permute-done.low = f32[5,8,8,128]{3,2,1,0:T(8,128)S(1)} collective-permute-done((f32[5,8,8,128]{3,2,1,0:T(8,128)S(1)}, f32[5,8,8,128]{3,2,1,0:T(8,128)S(1)}, u32[]{:S(2)}, u32[]{:S(2)}) %collective-permute-start) | collective-permute-done | bytes 163872 | tf_op jit(solution)/shard_map/ppermute | solution.py:384
  35.5 0.1 shard_map.40
  35.6 6.8 %collective-permute-start.2 = (f32[5,2,8,128]{3,2,1,0:T(8,128)S(1)}, f32[5,2,8,128]{3,2,1,0:T(8,128)S(1)}, u32[]{:S(2)}, u32[]{:S(2)}) collective-permute-start(f32[5,2,8,128]{3,2,1,0:T(8,128)S(1)} %get-tuple-element.11), channel_id=1, source_target_pairs={{0,60},{1,61},{2,62},{3,63},{4,0},{5,1},{6,2},{7,3},{8,4},{9,5},{1... | collective-permute-start | bytes 122888 | tf_op jit(solution)/shard_map/ppermute | solution.py:375
  42.4 1.9 %collective-permute-start.3 = (f32[5,2,8,128]{3,2,1,0:T(8,128)S(1)}, f32[5,2,8,128]{3,2,1,0:T(8,128)S(1)}, u32[]{:S(2)}, u32[]{:S(2)}) collective-permute-start(f32[5,2,8,128]{3,2,1,0:T(8,128)S(1)} %get-tuple-element.12), channel_id=1, source_target_pairs={{0,4},{1,5},{2,6},{3,7},{4,8},{5,9},{6,10},{7,11},{8,12},{9,13},{1... | collective-permute-start | bytes 122888 | tf_op jit(solution)/shard_map/ppermute | solution.py:375
  44.3 0.9 %dynamic-slice_reduce_fusion.1.counts = s32[4]{0:T(128)S(1)} fusion(s32[16,16,4]{1,2,0:T(4,128)} %param.5, s32[]{:T(128)S(6)} %select_n.28, s32[]{:T(128)S(6)} %select_n.31), kind=kLoop, calls=%fused_computation.1 | loop fusion | bytes 40 | tf_op jit(solution)/shard_map/dynamic_slice | solution.py:363
  45.2 1.6 %shard_map.39 = (f32[5,12,2,8,128]{4,3,2,1,0:T(8,128)S(1)}, f32[5,8,2,8,128]{4,3,2,1,0:T(8,128)S(1)}) custom-call(f32[5,8,8,128]{3,2,1,0:T(8,128)S(1)} %collective-permute-done.low, f32[5,8,8,128]{3,2,1,0:T(8,128)S(1)} %shard_map.38.own, f32[5,8,8,128]{3,2,1,0:T(8,128)S(1)} %collective-permute-done.1.high), custom_call_target="tpu_custom_call" | custom-call | flops 16777216 | bytes 1048576 | tf_op jit(solution)/shard_map/pallas_call | solution.py:402
  46.8 0.0 collective-permute-done.2.from_above
  46.8 2.6 %collective-permute-done.3.from_below = f32[5,2,8,128]{3,2,1,0:T(8,128)S(1)} collective-permute-done((f32[5,2,8,128]{3,2,1,0:T(8,128)S(1)}, f32[5,2,8,128]{3,2,1,0:T(8,128)S(1)}, u32[]{:S(2)}, u32[]{:S(2)}) %collective-permute-start.3) | collective-permute-done | bytes 40992 | tf_op jit(solution)/shard_map/ppermute | solution.py:375
  49.5 4.3 %shard_map.41 = f32[4,5,32,128]{3,2,1,0:T(8,128)} custom-call(s32[4]{0:T(128)S(1)} %dynamic-slice_reduce_fusion.1.counts, f32[5,8,8,128]{3,2,1,0:T(8,128)S(1)} %collective-permute-done.low, f32[5,8,8,128]{3,2,1,0:T(8,128)S(1)} %shard_map.38.own, f32[5,8,8,128]{3,2,1,0:T(8,128)S(1)} %collective-permute-done.1.high, ...), custom_call_target="tpu_custom_call" | custom-call | flops 16777216 | bytes 1048576 | tf_op jit(solution)/shard_map/pallas_call | solution.py:412
  53.7 7.9 %all-to-all-start.1 = ((f32[4,5,32,128]{3,2,1,0:T(8,128)}), f32[4,5,32,128]{3,2,1,0:T(8,128)S(1)}, u32[]{:S(2)}, u32[]{:S(2)}) async-start(f32[4,5,32,128]{3,2,1,0:T(8,128)} %shard_map.41), calls=%async_computation.1 | async-start | bytes 655360 | tf_op jit(solution)/shard_map/all_to_all | solution.py:371
  61.6 1.3 %dynamic_slice.11 = s32[1,1,1]{1,2,0:T(1,128)} dynamic-slice(s32[16,16,4]{1,2,0:T(4,128)} %param.5, s32[]{:T(128)S(6)} %select_n.29, s32[]{:T(128)S(6)} %select_n.32, s32[]{:T(128)S(6)} %select_n.35), dynamic_slice_sizes={1,1,1} | dynamic-slice | bytes 12 | tf_op jit(solution)/shard_map/dynamic_slice | solution.py:367
  62.9 4.2 %all-to-all-done.1.received = f32[4,5,32,128]{3,2,1,0:T(8,128)S(1)} async-done(((f32[4,5,32,128]{3,2,1,0:T(8,128)}), f32[4,5,32,128]{3,2,1,0:T(8,128)S(1)}, u32[]{:S(2)}, u32[]{:S(2)}) %all-to-all-start.1) | async-done | bytes 327712 | tf_op jit(solution)/shard_map/all_to_all | solution.py:371
  67.2 1.5 %shard_map.42 = f32[5,4,4096]{2,1,0:T(4,128)} custom-call(s32[1]{0:T(128)} %bitcast.count, f32[4,5,32,128]{3,2,1,0:T(8,128)S(1)} %all-to-all-done.1.received), custom_call_target="tpu_custom_call" | custom-call | bytes 1048576 | tf_op jit(solution)/shard_map/pallas_call | solution.py:422
Async XLA Ops:
  0.0 18.3 %copy-start = (s32[16,16,4]{1,2,0:T(4,128)S(1)}, s32[16,16,4]{1,2,0:T(4,128)}, u32[]{:S(2)}) copy-start(s32[16,16,4]{1,2,0:T(4,128)} %param.4) | copy-start | bytes 12292
  0.0 1.0 %copy-start.1 = (f32[1,1,4,5,4096]{4,2,3,1,0:T(4,128)S(1)}, f32[1,1,4,5,4096]{4,2,3,1,0:T(4,128)}, u32[]{:S(2)}) copy-start(f32[1,1,4,5,4096]{4,2,3,1,0:T(4,128)} %param.3) | copy-start | bytes 983044
  1.7 22.2 %all-to-all-start = ((f32[4,5,32,128]{3,2,1,0:T(8,128)}), f32[4,5,32,128]{3,2,1,0:T(8,128)S(1)}, u32[]{:S(2)}, u32[]{:S(2)}) async-start(f32[4,5,32,128]{3,2,1,0:T(8,128)} %shard_map.37), calls=%async_computation | async-start | bytes 655360 | tf_op jit(solution)/shard_map/all_to_all | solution.py:371
  24.5 7.2 %collective-permute-start.1 = (f32[5,8,8,128]{3,2,1,0:T(8,128)S(1)}, f32[5,8,8,128]{3,2,1,0:T(8,128)S(1)}, u32[]{:S(2)}, u32[]{:S(2)}) collective-permute-start(f32[5,8,8,128]{3,2,1,0:T(8,128)S(1)} %shard_map.38.own), channel_id=1, source_target_pairs={{0,963},{1,0},{2,1},{3,2},{4,967},{5,4},{6,5},{7,6},{8,971},{9,8},... | collective-permute-start | bytes 491528 | tf_op jit(solution)/shard_map/ppermute | solution.py:384
  27.9 7.5 %collective-permute-start = (f32[5,8,8,128]{3,2,1,0:T(8,128)S(1)}, f32[5,8,8,128]{3,2,1,0:T(8,128)S(1)}, u32[]{:S(2)}, u32[]{:S(2)}) collective-permute-start(f32[5,8,8,128]{3,2,1,0:T(8,128)S(1)} %shard_map.38.own), channel_id=1, source_target_pairs={{0,1},{1,2},{2,3},{3,64},{4,5},{5,6},{6,7},{7,68},{8,9},{9,10},{10... | collective-permute-start | bytes 491528 | tf_op jit(solution)/shard_map/ppermute | solution.py:384
  35.6 11.2 %collective-permute-start.2 = (f32[5,2,8,128]{3,2,1,0:T(8,128)S(1)}, f32[5,2,8,128]{3,2,1,0:T(8,128)S(1)}, u32[]{:S(2)}, u32[]{:S(2)}) collective-permute-start(f32[5,2,8,128]{3,2,1,0:T(8,128)S(1)} %get-tuple-element.11), channel_id=1, source_target_pairs={{0,60},{1,61},{2,62},{3,63},{4,0},{5,1},{6,2},{7,3},{8,4},{9,5},{1... | collective-permute-start | bytes 122888 | tf_op jit(solution)/shard_map/ppermute | solution.py:375
  42.4 7.1 %collective-permute-start.3 = (f32[5,2,8,128]{3,2,1,0:T(8,128)S(1)}, f32[5,2,8,128]{3,2,1,0:T(8,128)S(1)}, u32[]{:S(2)}, u32[]{:S(2)}) collective-permute-start(f32[5,2,8,128]{3,2,1,0:T(8,128)S(1)} %get-tuple-element.12), channel_id=1, source_target_pairs={{0,4},{1,5},{2,6},{3,7},{4,8},{5,9},{6,10},{7,11},{8,12},{9,13},{1... | collective-permute-start | bytes 122888 | tf_op jit(solution)/shard_map/ppermute | solution.py:375
  53.7 13.4 %all-to-all-start.1 = ((f32[4,5,32,128]{3,2,1,0:T(8,128)}), f32[4,5,32,128]{3,2,1,0:T(8,128)S(1)}, u32[]{:S(2)}, u32[]{:S(2)}) async-start(f32[4,5,32,128]{3,2,1,0:T(8,128)} %shard_map.41), calls=%async_computation.1 | async-start | bytes 655360 | tf_op jit(solution)/shard_map/all_to_all | solution.py:371

commit v3 on v2

v3 whole, which is shorter than its diff:
```python
import jax
import jax.numpy as jnp
from jax import lax
from jax.experimental import pallas as pl
from jax.experimental.pallas import tpu as pltpu
from jax.sharding import PartitionSpec as P


FIELDS = 5
GROUP = 4
SLOTS = 4
KEYS = 8
ROWS = 8
LANES = 128
HALO = 4
DEPTH = 16
WIDE = DEPTH + HALO
DEEP = DEPTH + 2 * HALO

TIME_STEP = 0.08
GAMMA = 1.4

VMEM = pl.BlockSpec(memory_space=pltpu.VMEM)
SMEM = pl.BlockSpec(memory_space=pltpu.SMEM)


def call(kernel, out_shapes, in_specs, scratch=(), flops=0, data=1 << 20):
    return pl.pallas_call(
        kernel,
        out_shape=out_shapes,
        in_specs=in_specs,
        out_specs=jax.tree.map(lambda _: VMEM, out_shapes),
        scratch_shapes=list(scratch),
        compiler_params=pltpu.CompilerParams(vmem_limit_bytes=24 << 20),
        cost_estimate=pl.CostEstimate(flops=flops, bytes_accessed=data, transcendentals=0),
    )


def f32(*shape):
    return jax.ShapeDtypeStruct(shape, jnp.float32)


def place_of(counts, key):
    position = jnp.int32(0)
    first = jnp.int32(0)
    upto = jnp.int32(0)
    for device in range(GROUP - 1):
        upto = upto + counts[device]
        beyond = upto <= key
        position = position + beyond.astype(jnp.int32)
        first = jnp.where(beyond, upto, first)
    return position, jnp.clip(key - first, 0, SLOTS - 1)


def arrange(counts, received, part, piece, base):
    for block_y in range(2):
        for xb in range(4):
            device, slot = place_of(counts, block_y * 4 + xb)
            start = part * (SLOTS * ROWS) + slot
            for field in range(FIELDS):
                block = received[device, field, pl.ds(start, ROWS, stride=SLOTS), :]
                for z in range(HALO):
                    piece[field, base + z * 2 + block_y, 2 * xb : 2 * xb + 2, :] = block[
                        2 * z : 2 * z + 2
                    ]


def even_slab():
    return lax.axis_index("gz") % 2 == 0


def outer_kernel(counts, received, near, far):
    even = even_slab()
    top, bottom = DEPTH // HALO - 1, 0
    arrange(counts, received, jnp.where(even, top, bottom), near, 0)
    arrange(counts, received, jnp.where(even, bottom, top), far, 0)


def own_kernel(counts, received, own, prim, change):
    for part in range(DEPTH // HALO):
        arrange(counts, received, part, own, part * 2 * HALO)

    def to_primitive(z, carry):
        values = [own[f, pl.ds(4 * z, 4)] for f in range(FIELDS)]
        for f, value in enumerate(primitives(values)):
            prim[f, pl.ds(2 * z, 2), 0] = jnp.stack([value[0], value[2]])
            prim[f, pl.ds(2 * z, 2), 1] = jnp.stack([value[1], value[3]])
        return carry

    lax.fori_loop(0, DEPTH // 2, to_primitive, 0)
    rate_x(change, prim, 0, 0, DEPTH, INNER)


def below_above(near, far, index):
    even = even_slab()
    return jnp.where(even, far[index], near[index]), jnp.where(even, near[index], far[index])


def edge_kernel(near, far, own, lower, upper):
    first_half = lax.broadcasted_iota(jnp.int32, (4, LANES), 1) < 64
    even = even_slab()
    pairs = WIDE // 2

    def rows(field, layer, block_y):
        rest = pl.ds(block_y, 4, stride=2)
        if layer < 0:
            at = (field, 2 * (layer + HALO) + block_y, rest)
            return jnp.where(even, far[at], near[at])
        if layer >= DEPTH:
            at = (field, 2 * (layer - DEPTH) + block_y, rest)
            return jnp.where(even, near[at], far[at])
        return own[field, 2 * layer + block_y, rest]

    for field in range(FIELDS):
        for pair in range(pairs):
            to = (pair % 2) * 4
            one, two = pair - 2, pair - 2 + pairs
            lower[field, pair // 2, to : to + 4, :] = jnp.where(
                first_half, rows(field, one, 0), pltpu.roll(rows(field, two, 0), 64, 1)
            )
            upper[field, pair // 2, to : to + 4, :] = jnp.where(
                first_half, pltpu.roll(rows(field, one, 1), 64, 1), rows(field, two, 1)
            )


def minmod(left, right):
    return jnp.maximum(jnp.minimum(left, right), 0.0) + jnp.minimum(jnp.maximum(left, right), 0.0)


def primitives(conserved):
    density, mx, my, mz, energy = conserved
    inverse = 1.0 / density
    vx, vy, vz = mx * inverse, my * inverse, mz * inverse
    pressure = (GAMMA - 1.0) * (energy - 0.5 * (mx * vx + my * vy + mz * vz))
    return [density, vx, vy, vz, pressure]


def face_terms(primitive, normal):
    density, vx, vy, vz, pressure = primitive
    energy = pressure * (1.0 / (GAMMA - 1.0)) + (0.5 * density) * (vx * vx + vy * vy + vz * vz)
    conserved = [density, density * vx, density * vy, density * vz, energy]
    stiff = GAMMA * pressure
    sound = stiff * lax.rsqrt(stiff * density)
    return conserved, primitive[1 + normal], pressure, sound


def face_flux(left, right, normal):
    left_u, left_v, left_p, left_c = face_terms(left, normal)
    right_u, right_v, right_p, right_c = face_terms(right, normal)
    fastest = jnp.maximum(jnp.maximum(left_v + left_c, right_v + right_c), 0.0)
    slowest = jnp.minimum(jnp.minimum(left_v - left_c, right_v - right_c), 0.0)
    inverse = 1.0 / (fastest - slowest)
    plus = fastest * inverse
    minus = slowest * inverse
    left_weight = plus * (left_v - slowest)
    right_weight = minus * (right_v - fastest)
    left_push = plus * left_p
    right_push = minus * right_p
    fluxes = [left_weight * a - right_weight * b for a, b in zip(left_u, right_u)]
    fluxes[1 + normal] = fluxes[1 + normal] + (left_push - right_push)
    fluxes[4] = fluxes[4] + (left_push * left_v - right_push * right_v)
    return fluxes


def shift_x(value, amount):
    axis = value.ndim - 1
    x = lax.broadcasted_iota(jnp.int32, value.shape, axis) % 16
    if amount > 0:
        inner = pltpu.roll(value, 1, axis)
        outer = pltpu.roll(pltpu.roll(value, 2, axis - 1), LANES - 15, axis)
        return jnp.where(x == 0, outer, inner)
    inner = pltpu.roll(value, LANES - 1, axis)
    outer = pltpu.roll(pltpu.roll(value, ROWS - 2, axis - 1), 15, axis)
    return jnp.where(x == 15, outer, inner)


def shift_y(value, amount):
    shape = value[0].shape
    across, down = len(shape) - 1, len(shape) - 2
    lane = lax.broadcasted_iota(jnp.int32, shape, across)
    odd = lax.broadcasted_iota(jnp.int32, shape, down) % 2 == 1
    if amount > 0:
        moved = [pltpu.roll(v, 16, across) for v in value]
        upper = moved
        lower = [moved[i - 1] for i in range(3)]
        outer = lane < 16
    else:
        moved = [pltpu.roll(v, LANES - 16, across) for v in value]
        upper = [moved[(i + 1) % 3] for i in range(3)]
        lower = moved
        outer = lane >= LANES - 16
    edge = [
        jnp.where(odd, pltpu.roll(u, 1, down), pltpu.roll(l, ROWS - 1, down))
        for u, l in zip(upper, lower)
    ]
    return [jnp.where(outer, e, m) for e, m in zip(edge, moved)]


def sweep_x(primitive):
    ahead = [shift_x(q, -1) for q in primitive]
    steps = [b - q for q, b in zip(primitive, ahead)]
    half = [0.5 * minmod(shift_x(d, 1), d) for d in steps]
    left = [q + h for q, h in zip(primitive, half)]
    right = [shift_x(q - h, -1) for q, h in zip(primitive, half)]
    return [shift_x(f, 1) - f for f in face_flux(left, right, 0)]


def sweep_y(primitive):
    left, right = [], []
    for q in primitive:
        ahead = shift_y(q, -1)
        steps = [b - a for a, b in zip(q, ahead)]
        behind = shift_y(steps, 1)
        half = [0.5 * minmod(b, d) for b, d in zip(behind, steps)]
        left.append([a + h for a, h in zip(q, half)])
        right.append(shift_y([a - h for a, h in zip(q, half)], -1))
    fluxes = [face_flux([l[i] for l in left], [r[i] for r in right], 1) for i in range(3)]
    out = []
    for field in range(FIELDS):
        flux = [fluxes[i][field] for i in range(3)]
        out.append([b - f for b, f in zip(shift_y(flux, 1), flux)])
    return out


BATCH = 4


def rate_x(total, prim, target, source, count, blocks, batch=BATCH):
    def planes(step, carry):
        z = step * batch
        values = [prim[f, pl.ds(z + source, batch), blocks] for f in range(FIELDS)]
        for f, change in enumerate(sweep_x(values)):
            total[f, pl.ds(z + target, batch), blocks] = change
        return carry

    lax.fori_loop(0, count // batch, planes, 0)


def rate_z(total, prim, count, blocks):
    def load(z):
        return [prim[f, z, blocks] for f in range(FIELDS)]

    here, ahead = load(1), load(2)
    step = [h - b for h, b in zip(here, load(0))]
    ahead_step = [a - h for a, h in zip(ahead, here)]
    half = [0.5 * minmod(a, b) for a, b in zip(step, ahead_step)]

    def face(z, here, half, ahead, ahead_step):
        beyond = load(z + 3)
        beyond_step = [b - a for a, b in zip(ahead, beyond)]
        ahead_half = [0.5 * minmod(a, b) for a, b in zip(ahead_step, beyond_step)]
        left = [q + h for q, h in zip(here, half)]
        right = [q - h for q, h in zip(ahead, ahead_half)]
        return ahead, ahead_half, beyond, beyond_step, face_flux(left, right, 2)

    def layer(z, state):
        after = face(z + 1, *state[:4])
        for f in range(FIELDS):
            total[f, z, blocks] = total[f, z, blocks] + (state[4][f] - after[4][f])
        return after

    lax.fori_loop(0, count, layer, face(0, here, half, ahead, ahead_step))


INNER = slice(0, 2)
EDGE = slice(2, 3)


def inner_kernel(near, far, prim, x_change, w0, change):
    for z in range(HALO):
        index = (slice(None), slice(2 * z, 2 * z + 2))
        below, above = below_above(near, far, index)
        for base, piece in ((0, below), (HALO + DEPTH, above)):
            values = [piece[f] for f in range(FIELDS)]
            for f, value in enumerate(primitives(values)):
                w0[f, base + z] = value
    for f in range(FIELDS):
        w0[f, HALO : HALO + DEPTH] = prim[f]
        change[f, 2 : 2 + DEPTH] = x_change[f]
    rate_x(change, w0, 0, 2, 2, INNER, 2)
    rate_x(change, w0, 2 + DEPTH, HALO + DEPTH, 2, INNER, 2)
    rate_z(change, w0, WIDE, INNER)


def rate_y(prims, store, count):
    def planes(step, carry):
        here = pl.ds(step * BATCH, BATCH)
        shifted = pl.ds(step * BATCH + 2, BATCH)
        store(here, sweep_y(prims(here, shifted)))
        return carry

    lax.fori_loop(0, count // BATCH, planes, 0)


def advance_kernel(
    counts, near, far, own, w0, inner, from_above, from_below, state,
    uh, wh, changeh, total, u1, w1, change, final,
):
    first_half = lax.broadcasted_iota(jnp.int32, (4, LANES), 1) < 64
    pairs = WIDE // 2
    for field in range(FIELDS):
        for pair in range(pairs):
            rows = slice((pair % 2) * 4, (pair % 2) * 4 + 4)
            above = from_above[field, pair // 2, rows, :]
            below = from_below[field, pair // 2, rows, :]
            for z, halo in (
                (pair, jnp.where(first_half, above, pltpu.roll(below, 64, 1))),
                (pair + pairs, jnp.where(first_half, pltpu.roll(above, 64, 1), below)),
            ):
                uh[field, z, 0, pl.ds(0, 4, stride=2), :] = halo
                uh[field, z, 0, pl.ds(1, 4, stride=2), :] = halo

    def halo_primitive(step, carry):
        layers = pl.ds(step * BATCH, BATCH)
        values = [uh[f, layers] for f in range(FIELDS)]
        for f, value in enumerate(primitives(values)):
            wh[f, layers] = value
        return carry

    lax.fori_loop(0, WIDE // BATCH, halo_primitive, 0)

    rate_x(changeh, wh, 0, 2, DEPTH, slice(0, 1), 2 * BATCH)
    rate_z(changeh, wh, DEPTH, slice(0, 1))

    def first_prims(here, shifted):
        return [[w0[f, shifted, 0], w0[f, shifted, 1], wh[f, here, 0]] for f in range(FIELDS)]

    def first_store(here, changes):
        for f in range(FIELDS):
            for i in range(2):
                total[f, here, i] = inner[f, here, i] + changes[f][i]
            total[f, here, 2] = changes[f][2]

    rate_y(first_prims, first_store, WIDE)

    def first_step(base, layer):
        values = [v + TIME_STEP * total[f, layer, INNER] for f, v in enumerate(base)]
        for f, value in enumerate(values):
            u1[f, layer] = value
        for f, value in enumerate(primitives(values)):
            w1[f, layer, INNER] = value

    for z in range(2):
        below, _ = below_above(near, far, (slice(None), slice(2 * z + 4, 2 * z + 6)))
        _, above = below_above(near, far, (slice(None), slice(2 * z, 2 * z + 2)))
        first_step([below[f] for f in range(FIELDS)], z)
        first_step([above[f] for f in range(FIELDS)], z + 2 + DEPTH)

    def own_step(step, carry):
        for k in range(2):
            z = 2 * step + k
            first_step([own[f, pl.ds(2 * z, 2)] for f in range(FIELDS)], z + 2)
        layers, shifted = pl.ds(2 * step, 2), pl.ds(2 * step + 2, 2)
        values = [
            uh[f, shifted] + TIME_STEP * (total[f, shifted, EDGE] + changeh[f, layers])
            for f in range(FIELDS)
        ]
        for f, value in enumerate(primitives(values)):
            w1[f, shifted, EDGE] = value
        return carry

    lax.fori_loop(0, DEPTH // 2, own_step, 0)

    rate_x(change, w1, 0, 2, DEPTH, INNER)
    rate_z(change, w1, DEPTH, INNER)

    def last_prims(here, shifted):
        return [[w1[f, shifted, i] for i in range(3)] for f in range(FIELDS)]

    def last_store(here, changes):
        after = pl.ds(here.start + 2, BATCH)
        for f in range(FIELDS):
            for i in range(2):
                u0 = jnp.stack([own[f, 2 * (here.start + k) + i] for k in range(BATCH)])
                rate = change[f, here, i] + changes[f][i]
                final[f, here, i] = 0.5 * u0 + 0.5 * (u1[f, after, i] + TIME_STEP * rate)

    rate_y(last_prims, last_store, DEPTH)

    position = lax.axis_index("blk") % GROUP
    start = jnp.int32(0)
    count = jnp.int32(0)
    for device in range(GROUP):
        start = start + jnp.where(device < position, counts[device], 0)
        count = jnp.where(device == position, counts[device], count)
    for slot in range(SLOTS):
        key = jnp.minimum(start + slot, KEYS - 1)
        block_y, xb = key // 4, key % 4
        valid = slot < count
        for field in range(FIELDS):
            for z in range(DEPTH):
                block = final[field, z, block_y, pl.ds(2 * xb, 2), :]
                state[field, pl.ds(8 * z + slot, 2, stride=SLOTS), :] = jnp.where(
                    valid, block, 0.0
                )


def body(state_old, counts_old, counts_new):
    slabs = lax.axis_size("gz")
    places = lax.axis_size("blk")
    groups = places // GROUP
    slab = lax.axis_index("gz")
    place = lax.axis_index("blk")
    group = place // GROUP

    def row_of(counts):
        return lax.dynamic_slice(counts, (slab, group, 0), (1, 1, GROUP)).reshape(GROUP)

    old_here = row_of(counts_old)
    new_here = row_of(counts_new)
    members = [[g * GROUP + k for k in range(GROUP)] for g in range(groups)]

    def along_y(value, by):
        route = [(i, (i + by * GROUP) % places) for i in range(places)]
        return lax.ppermute(value, "blk", route)

    def trade(value, offset):
        route = []
        for g in range(slabs):
            partner = ((g + offset) ^ 1) - offset
            for i in range(places):
                route.append((g * places + i, partner % slabs * places + i))
        return lax.ppermute(value, ("gz", "blk"), route)

    lines = DEPTH * 2
    held = state_old.reshape(SLOTS, FIELDS, lines, LANES).transpose(1, 2, 0, 3)
    held = held.reshape(FIELDS, lines * SLOTS, LANES)
    received = lax.all_gather(held, "blk", axis_index_groups=members)

    layers = f32(FIELDS, 2 * HALO, ROWS, LANES)
    to_near, to_far = call(outer_kernel, [layers, layers], [SMEM, VMEM])(old_here, received)
    near = trade(to_near, 0)
    far = trade(to_far, 1)
    block = f32(FIELDS, DEPTH, 2, ROWS, LANES)
    own, prim, x_change = call(
        own_kernel,
        [f32(FIELDS, 2 * DEPTH, ROWS, LANES), block, block],
        [SMEM, VMEM],
        flops=1 << 24,
    )(old_here, received)

    edge = f32(FIELDS, WIDE // 4, ROWS, LANES)
    lower, upper = call(edge_kernel, [edge, edge], [VMEM] * 3)(near, far, own)
    from_above = along_y(lower, -1)
    from_below = along_y(upper, 1)
    w0, inner = call(
        inner_kernel,
        [f32(FIELDS, DEEP, 2, ROWS, LANES), f32(FIELDS, WIDE, 2, ROWS, LANES)],
        [VMEM] * 4,
        flops=1 << 24,
    )(near, far, prim, x_change)

    def work(*shape):
        return pltpu.VMEM((FIELDS,) + shape + (ROWS, LANES), jnp.float32)

    state = call(
        advance_kernel,
        f32(FIELDS, lines * SLOTS, LANES),
        [SMEM] + [VMEM] * 7,
        [work(WIDE, 1), work(WIDE, 1), work(DEPTH, 1), work(WIDE, 3)]
        + [work(WIDE, 2), work(WIDE, 3), work(DEPTH, 2), work(DEPTH, 2)],
        flops=1 << 24,
    )(new_here, near, far, own, w0, inner, from_above, from_below)
    state = state.reshape(FIELDS, lines, SLOTS, LANES).transpose(2, 0, 1, 3)
    return state.reshape(1, 1, SLOTS, FIELDS, lines * LANES)


def solution(mesh):
    in_specs = (P("gz", "blk", None, None, None), P(), P())
    out_specs = P("gz", "blk", None, None, None)
    return jax.shard_map(body, mesh=mesh, in_specs=in_specs, out_specs=out_specs, check_vma=False)
```

time: 69.1 us -> 98.5 us (1.43)
  the two profiles are of different devices: /device:TPU:2 before, /device:TPU:56 now
where the time goes in v3:
time: 98.5 us; the launch traced here: 97.4 us
  waiting for transfers between devices  50.3 us (51%)
  Pallas kernels  16.6 us (17%)
  starting transfers between devices  14.6 us (15%)
  between operations  13.5 us (14%)
  local copies, waits for them, and re-layouts  2.39 us (2%)
    all_gather x1, waiting for transfers between devices, body(): received = lax.all_gather(held, 'blk', axis_index_groups=members)  45.3 us
    pallas_call x1, Pallas kernels, body(): call(advance_kernel, f32(FIELDS, lines * SLOTS, LANES), [SMEM] + [VMEM] *...  11.2 us
    ppermute x2, starting transfers between devices, along_y(): return lax.ppermute(value, 'blk', route)  9.24 us
    ppermute x2, starting transfers between devices, trade(): return lax.ppermute(value, ('gz', 'blk'), route)  5.37 us
    ppermute x2, waiting for transfers between devices, along_y(): return lax.ppermute(value, 'blk', route)  4.1 us
    pallas_call x1, Pallas kernels, body(): call(own_kernel, [f32(FIELDS, 2 * DEPTH, ROWS, LANES), block, block], [SM...  2.94 us
  transfers between devices with their start and end apart: 5, of which 3 were waited for; matrix products, arithmetic and copies ran while one was open for 1% of the time, Pallas kernels for 5%

profile of v3, /device:TPU:56, one launch (start us, length us, event | category | flops | bytes accessed | tf_op | source)
XLA Modules:
  0.0 97.4 jit_solution(12841806322283283574)
XLA Ops:
  6.5 0.0 copy-start
  6.5 0.0 all-gather.2.cloned.1.call-start
  6.5 0.7 all-gather.2.cloned.1.call-update
  7.3 0.0 copy-done
  7.3 0.2 dynamic-slice_reduce_fusion.counts
  7.5 45.3 %all-gather.2.cloned.1.call-done.received = f32[4,5,128,128]{3,2,1,0:T(8,128)} async-done(((f32[1,5,128,128]{3,2,1,0:T(8,128)}), f32[4,5,128,128]{3,2,1,0:T(8,128)}) %all-gather.2.cloned.1.call-update) | async-done | bytes 1310736 | tf_op jit(solution)/shard_map/all_gather | solution.py:428
  52.8 0.0 copy-start.1
  52.8 1.3 %copy-done.1 = f32[4,5,128,128]{3,2,1,0:T(8,128)S(1)} copy-done((f32[4,5,128,128]{3,2,1,0:T(8,128)S(1)}, f32[4,5,128,128]{3,2,1,0:T(8,128)}, u32[]{:S(2)}) %copy-start.1) | copy-done | bytes 1310744
  54.1 0.7 shard_map.37
  54.8 1.9 %collective-permute-start = (f32[5,8,8,128]{3,2,1,0:T(8,128)S(1)}, f32[5,8,8,128]{3,2,1,0:T(8,128)S(1)}, u32[]{:S(2)}, u32[]{:S(2)}) collective-permute-start(f32[5,8,8,128]{3,2,1,0:T(8,128)S(1)} %get-tuple-element.14), channel_id=1, source_target_pairs={{0,64},{1,65},{2,66},{3,67},{4,68},{5,69},{6,70},{7,71},{8,72},{9,... | collective-permute-start | bytes 491528 | tf_op jit(solution)/shard_map/ppermute | solution.py:423
  56.7 3.5 %collective-permute-start.1 = (f32[5,8,8,128]{3,2,1,0:T(8,128)S(1)}, f32[5,8,8,128]{3,2,1,0:T(8,128)S(1)}, u32[]{:S(2)}, u32[]{:S(2)}) collective-permute-start(f32[5,8,8,128]{3,2,1,0:T(8,128)S(1)} %get-tuple-element.15), channel_id=1, source_target_pairs={{0,960},{1,961},{2,962},{3,963},{4,964},{5,965},{6,966},{7,967},{8... | collective-permute-start | bytes 491528 | tf_op jit(solution)/shard_map/ppermute | solution.py:423
  60.2 2.9 %shard_map.38 = (f32[5,32,8,128]{3,2,1,0:T(8,128)S(1)}, f32[5,16,2,8,128]{4,3,2,1,0:T(8,128)S(1)}, f32[5,16,2,8,128]{4,3,2,1,0:T(8,128)S(1)}) custom-call(s32[4]{0:T(128)S(1)} %dynamic-slice_reduce_fusion.counts, f32[4,5,128,128]{3,2,1,0:T(8,128)S(1)} %copy-done.1), custom_call_target="tpu_custom_call" | custom-call | flops 16777216 | bytes 1048576 | tf_op jit(solution)/shard_map/pallas_call | solution.py:435
  63.1 0.0 collective-permute-done.near
  63.1 0.2 collective-permute-done.1.far
  63.3 0.2 shard_map.40
  63.5 7.3 %collective-permute-start.2 = (f32[5,5,8,128]{3,2,1,0:T(8,128)S(1)}, f32[5,5,8,128]{3,2,1,0:T(8,128)S(1)}, u32[]{:S(2)}, u32[]{:S(2)}) collective-permute-start(f32[5,5,8,128]{3,2,1,0:T(8,128)S(1)} %get-tuple-element.21), channel_id=1, source_target_pairs={{0,60},{1,61},{2,62},{3,63},{4,0},{5,1},{6,2},{7,3},{8,4},{9,5},{1... | collective-permute-start | bytes 307208 | tf_op jit(solution)/shard_map/ppermute | solution.py:415
  70.9 1.9 %collective-permute-start.3 = (f32[5,5,8,128]{3,2,1,0:T(8,128)S(1)}, f32[5,5,8,128]{3,2,1,0:T(8,128)S(1)}, u32[]{:S(2)}, u32[]{:S(2)}) collective-permute-start(f32[5,5,8,128]{3,2,1,0:T(8,128)S(1)} %get-tuple-element.22), channel_id=1, source_target_pairs={{0,4},{1,5},{2,6},{3,7},{4,8},{5,9},{6,10},{7,11},{8,12},{9,13},{1... | collective-permute-start | bytes 307208 | tf_op jit(solution)/shard_map/ppermute | solution.py:415
  72.8 0.9 dynamic-slice_reduce_fusion.1.counts
  73.7 1.6 %shard_map.39 = (f32[5,24,2,8,128]{4,3,2,1,0:T(8,128)S(1)}, f32[5,20,2,8,128]{4,3,2,1,0:T(8,128)S(1)}) custom-call(f32[5,8,8,128]{3,2,1,0:T(8,128)S(1)} %collective-permute-done.near, f32[5,8,8,128]{3,2,1,0:T(8,128)S(1)} %collective-permute-done.1.far, f32[5,16,2,8,128]{4,3,2,1,0:T(8,128)S(1)} %get-tuple-element.17.prim, ...), custom_call_target="tpu_custom_call" | custom-call | flops 16777216 | bytes 1048576 | tf_op jit(solution)/shard_map/pallas_call | solution.py:446
  75.2 0.0 collective-permute-done.2.from_above
  75.2 4.1 %collective-permute-done.3.from_below = f32[5,5,8,128]{3,2,1,0:T(8,128)S(1)} collective-permute-done((f32[5,5,8,128]{3,2,1,0:T(8,128)S(1)}, f32[5,5,8,128]{3,2,1,0:T(8,128)S(1)}, u32[]{:S(2)}, u32[]{:S(2)}) %collective-permute-start.3) | collective-permute-done | bytes 102432 | tf_op jit(solution)/shard_map/ppermute | solution.py:415
  79.3 11.2 %shard_map.41 = f32[5,128,128]{2,1,0:T(8,128)} custom-call(s32[4]{0:T(128)S(1)} %dynamic-slice_reduce_fusion.1.counts, f32[5,8,8,128]{3,2,1,0:T(8,128)S(1)} %collective-permute-done.near, f32[5,8,8,128]{3,2,1,0:T(8,128)S(1)} %collective-permute-done.1.far, f32[5,32,8,128]{3,2,1,0:T(8,128)S(1)} %get-tuple-element.16.own, ...), custom_call_target="tpu_custom_call" | custom-call | flops 16777216 | bytes 1048576 | tf_op jit(solution)/shard_map/pallas_call | solution.py:456
Async XLA Ops:
  6.5 0.8 copy-start
  6.5 46.2 %all-gather.2.cloned.1.call-start = ((), (), s32[]{:S(2)}) async-start(), calls=%async_computation | async-start | bytes 1638400 | tf_op jit(solution)/shard_map/all_gather | solution.py:428
  52.8 1.3 %copy-start.1 = (f32[4,5,128,128]{3,2,1,0:T(8,128)S(1)}, f32[4,5,128,128]{3,2,1,0:T(8,128)}, u32[]{:S(2)}) copy-start(f32[4,5,128,128]{3,2,1,0:T(8,128)} %all-gather.2.cloned.1.call-done.received) | copy-start | bytes 3932164
  54.8 8.3 %collective-permute-start = (f32[5,8,8,128]{3,2,1,0:T(8,128)S(1)}, f32[5,8,8,128]{3,2,1,0:T(8,128)S(1)}, u32[]{:S(2)}, u32[]{:S(2)}) collective-permute-start(f32[5,8,8,128]{3,2,1,0:T(8,128)S(1)} %get-tuple-element.14), channel_id=1, source_target_pairs={{0,64},{1,65},{2,66},{3,67},{4,68},{5,69},{6,70},{7,71},{8,72},{9,... | collective-permute-start | bytes 491528 | tf_op jit(solution)/shard_map/ppermute | solution.py:423
  56.7 6.6 %collective-permute-start.1 = (f32[5,8,8,128]{3,2,1,0:T(8,128)S(1)}, f32[5,8,8,128]{3,2,1,0:T(8,128)S(1)}, u32[]{:S(2)}, u32[]{:S(2)}) collective-permute-start(f32[5,8,8,128]{3,2,1,0:T(8,128)S(1)} %get-tuple-element.15), channel_id=1, source_target_pairs={{0,960},{1,961},{2,962},{3,963},{4,964},{5,965},{6,966},{7,967},{8... | collective-permute-start | bytes 491528 | tf_op jit(solution)/shard_map/ppermute | solution.py:423
  63.5 11.7 %collective-permute-start.2 = (f32[5,5,8,128]{3,2,1,0:T(8,128)S(1)}, f32[5,5,8,128]{3,2,1,0:T(8,128)S(1)}, u32[]{:S(2)}, u32[]{:S(2)}) collective-permute-start(f32[5,5,8,128]{3,2,1,0:T(8,128)S(1)} %get-tuple-element.21), channel_id=1, source_target_pairs={{0,60},{1,61},{2,62},{3,63},{4,0},{5,1},{6,2},{7,3},{8,4},{9,5},{1... | collective-permute-start | bytes 307208 | tf_op jit(solution)/shard_map/ppermute | solution.py:415
  70.9 8.5 %collective-permute-start.3 = (f32[5,5,8,128]{3,2,1,0:T(8,128)S(1)}, f32[5,5,8,128]{3,2,1,0:T(8,128)S(1)}, u32[]{:S(2)}, u32[]{:S(2)}) collective-permute-start(f32[5,5,8,128]{3,2,1,0:T(8,128)S(1)} %get-tuple-element.22), channel_id=1, source_target_pairs={{0,4},{1,5},{2,6},{3,7},{4,8},{5,9},{6,10},{7,11},{8,12},{9,13},{1... | collective-permute-start | bytes 307208 | tf_op jit(solution)/shard_map/ppermute | solution.py:415
Sparse Core Ops, SparseCore 0:
  10.0 42.6 all-gather.1

commit v4 on v2

--- a/solution.py
+++ b/solution.py
@@ -14,23 +14,25 @@
 LANES = 128
 QUARTER = 4
 HALO = 4
+LINES = ROWS * SLOTS
 
 TIME_STEP = 0.08
 GAMMA = 1.4
 
 VMEM = pl.BlockSpec(memory_space=pltpu.VMEM)
 SMEM = pl.BlockSpec(memory_space=pltpu.SMEM)
-
-
-def call(kernel, out_shapes, in_specs, scratch=(), flops=0, data=1 << 20):
+HBM = pl.BlockSpec(memory_space=pltpu.HBM)
+
+
+def call(kernel, out_shapes, in_specs, scratch=(), flops=0, out=VMEM):
     return pl.pallas_call(
         kernel,
         out_shape=out_shapes,
         in_specs=in_specs,
-        out_specs=jax.tree.map(lambda _: VMEM, out_shapes),
+        out_specs=jax.tree.map(lambda _: out, out_shapes),
         scratch_shapes=list(scratch),
         compiler_params=pltpu.CompilerParams(vmem_limit_bytes=24 << 20),
-        cost_estimate=pl.CostEstimate(flops=flops, bytes_accessed=data, transcendentals=0),
+        cost_estimate=pl.CostEstimate(flops=flops, bytes_accessed=1 << 20, transcendentals=0),
     )
 
 
@@ -38,14 +40,38 @@
     return jax.ShapeDtypeStruct(shape, jnp.float32)
 
 
-def split_kernel(state, message):
-    for field in range(FIELDS):
-        for part in range(GROUP):
-            for row in range(ROWS):
-                chunk = (part * ROWS + row) * LANES
-                message[part, field, 4 * row : 4 * row + 4, :] = state[
-                    field, :, chunk : chunk + LANES
-                ]
+def quarter_of(device):
+    return jnp.where(lax.axis_index("gz") % 2 == 0, device, GROUP - 1 - device)
+
+
+def even_quarter():
+    return (lax.axis_index("blk") + lax.axis_index("gz")) % 2 == 0
+
+
+def split_kernel(state, message, arrived):
+    copies = []
+    for device in range(GROUP):
+        rows = pl.ds(pl.multiple_of(quarter_of(device) * LINES, LINES), LINES)
+        copies.append(
+            pltpu.make_async_copy(state.at[:, rows], message.at[device], arrived.at[device])
+        )
+    for copy in copies:
+        copy.start()
+    for copy in copies:
+        copy.wait()
+
+
+def join_kernel(received, state, arrived):
+    copies = []
+    for device in range(GROUP):
+        rows = pl.ds(pl.multiple_of(quarter_of(device) * LINES, LINES), LINES)
+        copies.append(
+            pltpu.make_async_copy(received.at[device], state.at[:, rows], arrived.at[device])
+        )
+    for copy in copies:
+        copy.start()
+    for copy in copies:
+        copy.wait()
 
 
 def place_of(counts, key):
@@ -72,26 +98,34 @@
                     ]
 
 
-def layers_of(low, own, high):
-    return [(low, 2), (low, 3)] + [(own, z) for z in range(QUARTER)] + [(high, 0), (high, 1)]
-
-
-def edge_kernel(low, own, high, lower, upper):
-    layers = layers_of(low, own, high)
+def below_above(first, second, index):
+    even = even_quarter()
+    return (
+        jnp.where(even, second[index], first[index]),
+        jnp.where(even, first[index], second[index]),
+    )
+
+
+def edge_kernel(first, own, second, lower, upper):
     first_half = lax.broadcasted_iota(jnp.int32, (4, LANES), 1) < 64
+
+    def rows(field, layer, block_y):
+        rest = pl.ds(block_y, 4, stride=2)
+        if layer < 0:
+            return below_above(first, second, (field, 2 * (layer + HALO) + block_y, rest))[0]
+        if layer >= QUARTER:
+            return below_above(first, second, (field, 2 * (layer - QUARTER) + block_y, rest))[1]
+        return own[field, 2 * layer + block_y, rest]
+
     for field in range(FIELDS):
         for pair in range(4):
             to = (pair % 2) * 4
-
-            def rows(index, block_y):
-                piece, z = layers[index]
-                return piece[field, z * 2 + block_y, pl.ds(block_y, 4, stride=2), :]
-
+            one, two = pair - 2, pair + 2
             lower[field, pair // 2, to : to + 4, :] = jnp.where(
-                first_half, rows(pair, 0), pltpu.roll(rows(pair + 4, 0), 64, 1)
+                first_half, rows(field, one, 0), pltpu.roll(rows(field, two, 0), 64, 1)
             )
             upper[field, pair // 2, to : to + 4, :] = jnp.where(
-                first_half, pltpu.roll(rows(pair, 1), 64, 1), rows(pair + 4, 1)
+                first_half, pltpu.roll(rows(field, one, 1), 64, 1), rows(field, two, 1)
             )
 
 
@@ -178,19 +212,19 @@
 
 
 def sweep_y(primitive):
-    left, right = [], []
-    for q in primitive:
-        ahead = shift_y(q, -1)
-        steps = [b - a for a, b in zip(q, ahead)]
-        behind = shift_y(steps, 1)
-        half = [0.5 * minmod(b, d) for b, d in zip(behind, steps)]
-        left.append([a + h for a, h in zip(q, half)])
-        right.append(shift_y([a - h for a, h in zip(q, half)], -1))
-    fluxes = [face_flux([l[i] for l in left], [r[i] for r in right], 1) for i in range(3)]
+    ahead = [shift_y(q, -1) for q in primitive]
+    steps = [[b - a for a, b in zip(q, after)] for q, after in zip(primitive, ahead)]
+    behind = [shift_y(d, 1) for d in steps]
+    half = [[0.5 * minmod(a, b) for a, b in zip(p, d)] for p, d in zip(behind, steps)]
+    beyond = [shift_y(h, -1) for h in half]
+    fluxes = []
+    for i in range(3):
+        left = [q[i] + h[i] for q, h in zip(primitive, half)]
+        right = [q[i] - h[i] for q, h in zip(ahead, beyond)]
+        fluxes.append(face_flux(left, right, 1))
     out = []
-    for field in range(FIELDS):
-        flux = [fluxes[i][field] for i in range(3)]
-        out.append([b - f for b, f in zip(shift_y(flux, 1), flux)])
+    for flux in zip(*fluxes):
+        out.append([b - f for b, f in zip(shift_y(list(flux), 1), flux)])
     return out
 
 
@@ -239,22 +273,28 @@
 EDGE = slice(2, 3)
 
 
-def inner_kernel(low, own, high, w0, change):
-    for base, piece in ((0, low), (QUARTER, own), (2 * QUARTER, high)):
-
-        def to_primitive(z, carry):
-            values = [piece[f, pl.ds(2 * z, 2)] for f in range(FIELDS)]
+def inner_kernel(first, own, second, w0, change):
+    for z in range(QUARTER):
+        index = (slice(None), slice(2 * z, 2 * z + 2))
+        below, above = below_above(first, second, index)
+        for base, piece in ((0, below), (QUARTER, own[index]), (2 * QUARTER, above)):
+            values = [piece[f] for f in range(FIELDS)]
             for f, value in enumerate(primitives(values)):
                 w0[f, base + z] = value
-            return carry
-
-        lax.fori_loop(0, QUARTER, to_primitive, 0)
     rate_x(change, w0, QUARTER + HALO, INNER)
     rate_z(change, w0, QUARTER + HALO, INNER)
 
 
+def first_step(layer, base, u1, w1, total):
+    values = [base[f] + TIME_STEP * total[f, layer, INNER] for f in range(FIELDS)]
+    for f, value in enumerate(values):
+        u1[f, layer] = value
+    for f, value in enumerate(primitives(values)):
+        w1[f, layer, INNER] = value
+
+
 def advance_kernel(
-    counts, low, own, high, w0, inner, from_above, from_below, message,
+    counts, first, own, second, w0, inner, from_above, from_below, message,
     uh, wh, changeh, total, u1, w1, change, done,
 ):
     wide = QUARTER + HALO
@@ -289,15 +329,15 @@
 
     lax.fori_loop(0, wide // Y_LAYERS, planes, 0)
 
-    for index, (piece, z) in enumerate(layers_of(low, own, high)):
-        values = [
-            piece[f, 2 * z : 2 * z + 2] + TIME_STEP * total[f, index, INNER]
-            for f in range(FIELDS)
-        ]
-        for f, value in enumerate(values):
-            u1[f, index] = value
-        for f, value in enumerate(primitives(values)):
-            w1[f, index, INNER] = value
+    for z in range(QUARTER):
+        index = (slice(None), slice(2 * z, 2 * z + 2))
+        if z >= 2:
+            layer, piece = z - 2, below_above(first, second, index)[0]
+            first_step(layer, piece, u1, w1, total)
+        else:
+            layer, piece = z + 2 + QUARTER, below_above(first, second, index)[1]
+            first_step(layer, piece, u1, w1, total)
+        first_step(z + 2, own[index], u1, w1, total)
     for z in range(QUARTER):
         values = [
             uh[f, z + 2] + TIME_STEP * (total[f, z + 2, EDGE] + changeh[f, z])
@@ -310,15 +350,15 @@
     rate_z(change, w1, QUARTER, INNER)
 
     def last_planes(step, carry):
-        z = step * Y_LAYERS
-        here, shifted = pl.ds(z, Y_LAYERS), pl.ds(z + 2, Y_LAYERS)
+        z = step * 4
+        here, shifted = pl.ds(z, 4), pl.ds(z + 2, 4)
         changes = sweep_y([[w1[f, shifted, i] for i in range(3)] for f in range(FIELDS)])
         for f in range(FIELDS):
             for i in range(2):
                 change[f, here, i] = change[f, here, i] + changes[f][i]
         return carry
 
-    lax.fori_loop(0, QUARTER // Y_LAYERS, last_planes, 0)
+    lax.fori_loop(0, 1, last_planes, 0)
 
     for z in range(QUARTER):
         for field in range(FIELDS):
@@ -335,20 +375,12 @@
     for device in range(GROUP):
         for slot in range(SLOTS):
             key = jnp.minimum(start + slot, KEYS - 1)
+            valid = slot < counts[device]
             for field in range(FIELDS):
-                message[device, field, pl.ds(slot, ROWS, stride=SLOTS), :] = done[key, field]
+                message[device, field, pl.ds(slot, ROWS, stride=SLOTS), :] = jnp.where(
+                    valid, done[key, field], 0.0
+                )
         start = start + counts[device]
-
-
-def join_kernel(count, received, state):
-    valid = lax.broadcasted_iota(jnp.int32, (SLOTS, LANES), 0) < count[0]
-    for field in range(FIELDS):
-        for part in range(GROUP):
-            for row in range(ROWS):
-                chunk = (part * ROWS + row) * LANES
-                state[field, :, chunk : chunk + LANES] = jnp.where(
-                    valid, received[part, field, 4 * row : 4 * row + 4, :], 0.0
-                )
 
 
 def body(state_old, counts_old, counts_new):
@@ -356,15 +388,13 @@
     places = lax.axis_size("blk")
     groups = places // GROUP
     slab = lax.axis_index("gz")
-    place = lax.axis_index("blk")
-    group = place // GROUP
+    group = lax.axis_index("blk") // GROUP
 
     def row_of(counts):
         return lax.dynamic_slice(counts, (slab, group, 0), (1, 1, GROUP)).reshape(GROUP)
 
     old_here = row_of(counts_old)
     new_here = row_of(counts_new)
-    count_here = lax.dynamic_slice(new_here, (place % GROUP,), (1,))
     members = [[g * GROUP + k for k in range(GROUP)] for g in range(groups)]
 
     def exchange(message):
@@ -374,29 +404,35 @@
         route = [(i, (i + by * GROUP) % places) for i in range(places)]
         return lax.ppermute(value, "blk", route)
 
-    def along_z(value, by):
+    def trade(value, offset):
+        def device_of(quarter):
+            g, k = divmod(quarter, GROUP)
+            return g, k if g % 2 == 0 else GROUP - 1 - k
+
         route = []
-        for g in range(slabs):
-            for i in range(places):
-                layer = (g * GROUP + i % GROUP + by) % (slabs * GROUP)
-                target = layer // GROUP * places + i // GROUP * GROUP + layer % GROUP
-                route.append((g * places + i, target))
+        for quarter in range(slabs * GROUP):
+            partner = (((quarter + offset) ^ 1) - offset) % (slabs * GROUP)
+            (g, j), (to_g, to_j) = device_of(quarter), device_of(partner)
+            for i in range(0, places, GROUP):
+                route.append((g * places + i + j, to_g * places + i + to_j))
         return lax.ppermute(value, ("gz", "blk"), route)
 
-    parts = f32(GROUP, FIELDS, ROWS * SLOTS, LANES)
-    cells = GROUP * ROWS * LANES
+    parts = f32(GROUP, FIELDS, LINES, LANES)
+    slots = f32(FIELDS, GROUP * LINES, LANES)
     wide = QUARTER + HALO
-    held = state_old.reshape(SLOTS, FIELDS, cells).transpose(1, 0, 2)
-    received = exchange(call(split_kernel, parts, [VMEM])(held))
+    held = state_old.reshape(SLOTS, FIELDS, GROUP * ROWS, LANES).transpose(1, 2, 0, 3)
+    held = held.reshape(slots.shape)
+    arrivals = [pltpu.SemaphoreType.DMA((GROUP,))]
+    received = exchange(call(split_kernel, parts, [HBM], arrivals)(held))
 
     own = call(gather_kernel, f32(FIELDS, 2 * QUARTER, ROWS, LANES), [SMEM, VMEM])(
         old_here, received
     )
-    low = along_z(own, 1)
-    high = along_z(own, -1)
+    first = trade(own, 0)
+    second = trade(own, 1)
 
     edge = f32(FIELDS, 2, ROWS, LANES)
-    lower, upper = call(edge_kernel, [edge, edge], [VMEM] * 3)(low, own, high)
+    lower, upper = call(edge_kernel, [edge, edge], [VMEM] * 3)(first, own, second)
     from_above = along_y(lower, -1)
     from_below = along_y(upper, 1)
     w0, inner = call(
@@ -404,7 +440,7 @@
         [f32(FIELDS, wide + HALO, 2, ROWS, LANES), f32(FIELDS, wide, 2, ROWS, LANES)],
         [VMEM] * 3,
         flops=1 << 24,
-    )(low, own, high)
+    )(first, own, second)
 
     def work(*shape):
         return pltpu.VMEM((FIELDS,) + shape + (ROWS, LANES), jnp.float32)
@@ -417,10 +453,11 @@
         + [work(wide, 2), work(wide, 3), work(QUARTER, 2)]
         + [pltpu.VMEM((KEYS, FIELDS, ROWS, LANES), jnp.float32)],
         flops=1 << 24,
-    )(new_here, low, own, high, w0, inner, from_above, from_below)
+    )(new_here, first, own, second, w0, inner, from_above, from_below)
     returned = exchange(finished)
-    state = call(join_kernel, f32(FIELDS, SLOTS, cells), [SMEM, VMEM])(count_here, returned)
-    return state.transpose(1, 0, 2)[None, None]
+    state = call(join_kernel, slots, [VMEM], arrivals, out=HBM)(returned)
+    state = state.reshape(FIELDS, GROUP * ROWS, SLOTS, LANES).transpose(2, 0, 1, 3)
+    return state.reshape(state_old.shape)
 
 
 def solution(mesh):

time: 69.1 us -> 64.3 us (0.931)
  the two profiles are of different devices: /device:TPU:2 before, /device:TPU:56 now
where the time goes in v4:
time: 64.3 us; the launch traced here: 63.7 us
  starting transfers between devices  29.5 us (46%)
  waiting for transfers between devices  14.7 us (23%)
  blocking collectives  10.1 us (16%)
  Pallas kernels  7.33 us (11%)
  local copies, waits for them, and re-layouts  2.04 us (3%)
    ppermute x2, starting transfers between devices, along_y(): return lax.ppermute(value, 'blk', route)  20.8 us
    all_to_all x1, blocking collectives, exchange(): return lax.all_to_all(message, 'blk', 0, 0, axis_index_groups=members)  10.1 us
    all_to_all x1, waiting for transfers between devices, exchange(): return lax.all_to_all(message, 'blk', 0, 0, axis_index_groups=members)  7.18 us
    ppermute x2, waiting for transfers between devices, trade(): return lax.ppermute(value, ('gz', 'blk'), route)  4.73 us
    ppermute x2, starting transfers between devices, trade(): return lax.ppermute(value, ('gz', 'blk'), route)  4.39 us
    all_to_all x1, starting transfers between devices, exchange(): return lax.all_to_all(message, 'blk', 0, 0, axis_index_groups=members)  4.3 us
    pallas_call x1, Pallas kernels, body(): call(advance_kernel, parts, [SMEM] + [VMEM] * 7, [work(wide, 1), work(wid...  3.49 us
    ppermute x2, waiting for transfers between devices, along_y(): return lax.ppermute(value, 'blk', route)  2.76 us
  transfers between devices with their start and end apart: 5, of which 4 were waited for; matrix products, arithmetic and copies ran while one was open for 2% of the time, Pallas kernels for 2%

profile of v4, /device:TPU:56, one launch (start us, length us, event | category | flops | bytes accessed | tf_op | source)
XLA Modules:
  0.0 63.7 jit_solution(5180310257172635648)
XLA Ops:
  0.0 0.0 copy-start
  0.0 0.0 copy-start.1
  0.0 1.0 %copy-done.1 = f32[1,1,4,5,4096]{4,2,3,1,0:T(4,128)S(1)} copy-done((f32[1,1,4,5,4096]{4,2,3,1,0:T(4,128)S(1)}, f32[1,1,4,5,4096]{4,2,3,1,0:T(4,128)}, u32[]{:S(2)}) %copy-start.1) | copy-done | bytes 327704
  1.0 0.8 %shard_map.37 = f32[4,5,32,128]{3,2,1,0:T(8,128)} custom-call(f32[5,128,128]{2,1,0:T(8,128)S(1)} %bitcast.10), custom_call_target="tpu_custom_call" | custom-call | bytes 1048576 | tf_op jit(solution)/shard_map/pallas_call | solution.py:426
  1.8 4.3 %all-to-all-start = ((f32[4,5,32,128]{3,2,1,0:T(8,128)}), f32[4,5,32,128]{3,2,1,0:T(8,128)S(1)}, u32[]{:S(2)}, u32[]{:S(2)}) async-start(f32[4,5,32,128]{3,2,1,0:T(8,128)} %shard_map.37), calls=%async_computation | async-start | bytes 655360 | tf_op jit(solution)/shard_map/all_to_all | solution.py:401
  6.1 0.0 copy-done
  6.1 0.2 dynamic-slice_reduce_fusion.counts
  6.3 7.2 %all-to-all-done.received = f32[4,5,32,128]{3,2,1,0:T(8,128)S(1)} async-done(((f32[4,5,32,128]{3,2,1,0:T(8,128)}), f32[4,5,32,128]{3,2,1,0:T(8,128)S(1)}, u32[]{:S(2)}, u32[]{:S(2)}) %all-to-all-start) | async-done | bytes 327712 | tf_op jit(solution)/shard_map/all_to_all | solution.py:401
  13.5 0.6 shard_map.38.own
  14.1 1.9 %collective-permute-start.1 = (f32[5,8,8,128]{3,2,1,0:T(8,128)S(1)}, f32[5,8,8,128]{3,2,1,0:T(8,128)S(1)}, u32[]{:S(2)}, u32[]{:S(2)}) collective-permute-start(f32[5,8,8,128]{3,2,1,0:T(8,128)S(1)} %shard_map.38.own), channel_id=1, source_target_pairs={{0,960},{4,964},{8,968},{12,972},{16,976},{20,980},{24,984},{28,98... | collective-permute-start | bytes 491528 | tf_op jit(solution)/shard_map/ppermute | solution.py:418
  16.1 2.5 %collective-permute-start = (f32[5,8,8,128]{3,2,1,0:T(8,128)S(1)}, f32[5,8,8,128]{3,2,1,0:T(8,128)S(1)}, u32[]{:S(2)}, u32[]{:S(2)}) collective-permute-start(f32[5,8,8,128]{3,2,1,0:T(8,128)S(1)} %shard_map.38.own), channel_id=1, source_target_pairs={{0,1},{4,5},{8,9},{12,13},{16,17},{20,21},{24,25},{28,29},{32,33},... | collective-permute-start | bytes 491528 | tf_op jit(solution)/shard_map/ppermute | solution.py:418
  18.5 2.2 %collective-permute-done.1.second = f32[5,8,8,128]{3,2,1,0:T(8,128)S(1)} collective-permute-done((f32[5,8,8,128]{3,2,1,0:T(8,128)S(1)}, f32[5,8,8,128]{3,2,1,0:T(8,128)S(1)}, u32[]{:S(2)}, u32[]{:S(2)}) %collective-permute-start.1) | collective-permute-done | bytes 163872 | tf_op jit(solution)/shard_map/ppermute | solution.py:418
  20.8 2.5 %collective-permute-done.first = f32[5,8,8,128]{3,2,1,0:T(8,128)S(1)} collective-permute-done((f32[5,8,8,128]{3,2,1,0:T(8,128)S(1)}, f32[5,8,8,128]{3,2,1,0:T(8,128)S(1)}, u32[]{:S(2)}, u32[]{:S(2)}) %collective-permute-start) | collective-permute-done | bytes 163872 | tf_op jit(solution)/shard_map/ppermute | solution.py:418
  23.3 0.1 shard_map.40
  23.4 18.9 %collective-permute-start.2 = (f32[5,2,8,128]{3,2,1,0:T(8,128)S(1)}, f32[5,2,8,128]{3,2,1,0:T(8,128)S(1)}, u32[]{:S(2)}, u32[]{:S(2)}) collective-permute-start(f32[5,2,8,128]{3,2,1,0:T(8,128)S(1)} %get-tuple-element.11), channel_id=1, source_target_pairs={{0,60},{1,61},{2,62},{3,63},{4,0},{5,1},{6,2},{7,3},{8,4},{9,5},{1... | collective-permute-start | bytes 122888 | tf_op jit(solution)/shard_map/ppermute | solution.py:405
  42.3 1.9 %collective-permute-start.3 = (f32[5,2,8,128]{3,2,1,0:T(8,128)S(1)}, f32[5,2,8,128]{3,2,1,0:T(8,128)S(1)}, u32[]{:S(2)}, u32[]{:S(2)}) collective-permute-start(f32[5,2,8,128]{3,2,1,0:T(8,128)S(1)} %get-tuple-element.12), channel_id=1, source_target_pairs={{0,4},{1,5},{2,6},{3,7},{4,8},{5,9},{6,10},{7,11},{8,12},{9,13},{1... | collective-permute-start | bytes 122888 | tf_op jit(solution)/shard_map/ppermute | solution.py:405
  44.2 0.9 %dynamic-slice_reduce_fusion.1.counts = s32[4]{0:T(128)S(1)} fusion(s32[16,16,4]{1,2,0:T(4,128)} %param.5, s32[]{:T(128)S(6)} %select_n.13, s32[]{:T(128)S(6)} %select_n.15), kind=kLoop, calls=%fused_computation.1 | loop fusion | bytes 40 | tf_op jit(solution)/shard_map/dynamic_slice | solution.py:394
  45.1 1.5 %shard_map.39 = (f32[5,12,2,8,128]{4,3,2,1,0:T(8,128)S(1)}, f32[5,8,2,8,128]{4,3,2,1,0:T(8,128)S(1)}) custom-call(f32[5,8,8,128]{3,2,1,0:T(8,128)S(1)} %collective-permute-done.first, f32[5,8,8,128]{3,2,1,0:T(8,128)S(1)} %shard_map.38.own, f32[5,8,8,128]{3,2,1,0:T(8,128)S(1)} %collective-permute-done.1.second), custom_call_target="tpu_custom_call" | custom-call | flops 16777216 | bytes 1048576 | tf_op jit(solution)/shard_map/pallas_call | solution.py:438
  46.6 0.0 collective-permute-done.2.from_above
  46.6 2.8 %collective-permute-done.3.from_below = f32[5,2,8,128]{3,2,1,0:T(8,128)S(1)} collective-permute-done((f32[5,2,8,128]{3,2,1,0:T(8,128)S(1)}, f32[5,2,8,128]{3,2,1,0:T(8,128)S(1)}, u32[]{:S(2)}, u32[]{:S(2)}) %collective-permute-start.3) | collective-permute-done | bytes 40992 | tf_op jit(solution)/shard_map/ppermute | solution.py:405
  49.4 3.5 %shard_map.41 = f32[4,5,32,128]{3,2,1,0:T(8,128)S(1)} custom-call(s32[4]{0:T(128)S(1)} %dynamic-slice_reduce_fusion.1.counts, f32[5,8,8,128]{3,2,1,0:T(8,128)S(1)} %collective-permute-done.first, f32[5,8,8,128]{3,2,1,0:T(8,128)S(1)} %shard_map.38.own, f32[5,8,8,128]{3,2,1,0:T(8,128)S(1)} %collective-permute-done.1.second, ...), custom_call_target="tpu_custom_call" | custom-call | flops 16777216 | bytes 1048576 | tf_op jit(solution)/shard_map/pallas_call | solution.py:448
  52.9 10.1 %all_to_all.10.received = f32[4,5,32,128]{3,2,1,0:T(8,128)S(1)} all-to-all(f32[4,5,32,128]{3,2,1,0:T(8,128)S(1)} %shard_map.41), channel_id=1, replica_groups={{0,1,2,3},{4,5,6,7},{8,9,10,11},{12,13,14,15},{16,17,18,19},{20,21,22,2..., dimensions={0} | all-to-all | bytes 655360 | tf_op jit(solution)/shard_map/all_to_all | solution.py:401
  62.9 0.8 %shard_map.42 = f32[5,128,128]{2,1,0:T(8,128)} custom-call(f32[4,5,32,128]{3,2,1,0:T(8,128)S(1)} %all_to_all.10.received), custom_call_target="tpu_custom_call" | custom-call | bytes 1048576 | tf_op jit(solution)/shard_map/pallas_call | solution.py:458
Async XLA Ops:
  0.0 6.1 %copy-start = (s32[16,16,4]{1,2,0:T(4,128)S(1)}, s32[16,16,4]{1,2,0:T(4,128)}, u32[]{:S(2)}) copy-start(s32[16,16,4]{1,2,0:T(4,128)} %param.4) | copy-start | bytes 12292
  0.0 1.0 %copy-start.1 = (f32[1,1,4,5,4096]{4,2,3,1,0:T(4,128)S(1)}, f32[1,1,4,5,4096]{4,2,3,1,0:T(4,128)}, u32[]{:S(2)}) copy-start(f32[1,1,4,5,4096]{4,2,3,1,0:T(4,128)} %param.3) | copy-start | bytes 983044
  1.8 11.7 %all-to-all-start = ((f32[4,5,32,128]{3,2,1,0:T(8,128)}), f32[4,5,32,128]{3,2,1,0:T(8,128)S(1)}, u32[]{:S(2)}, u32[]{:S(2)}) async-start(f32[4,5,32,128]{3,2,1,0:T(8,128)} %shard_map.37), calls=%async_computation | async-start | bytes 655360 | tf_op jit(solution)/shard_map/all_to_all | solution.py:401
  14.1 6.6 %collective-permute-start.1 = (f32[5,8,8,128]{3,2,1,0:T(8,128)S(1)}, f32[5,8,8,128]{3,2,1,0:T(8,128)S(1)}, u32[]{:S(2)}, u32[]{:S(2)}) collective-permute-start(f32[5,8,8,128]{3,2,1,0:T(8,128)S(1)} %shard_map.38.own), channel_id=1, source_target_pairs={{0,960},{4,964},{8,968},{12,972},{16,976},{20,980},{24,984},{28,98... | collective-permute-start | bytes 491528 | tf_op jit(solution)/shard_map/ppermute | solution.py:418
  16.1 7.2 %collective-permute-start = (f32[5,8,8,128]{3,2,1,0:T(8,128)S(1)}, f32[5,8,8,128]{3,2,1,0:T(8,128)S(1)}, u32[]{:S(2)}, u32[]{:S(2)}) collective-permute-start(f32[5,8,8,128]{3,2,1,0:T(8,128)S(1)} %shard_map.38.own), channel_id=1, source_target_pairs={{0,1},{4,5},{8,9},{12,13},{16,17},{20,21},{24,25},{28,29},{32,33},... | collective-permute-start | bytes 491528 | tf_op jit(solution)/shard_map/ppermute | solution.py:418
  23.4 23.2 %collective-permute-start.2 = (f32[5,2,8,128]{3,2,1,0:T(8,128)S(1)}, f32[5,2,8,128]{3,2,1,0:T(8,128)S(1)}, u32[]{:S(2)}, u32[]{:S(2)}) collective-permute-start(f32[5,2,8,128]{3,2,1,0:T(8,128)S(1)} %get-tuple-element.11), channel_id=1, source_target_pairs={{0,60},{1,61},{2,62},{3,63},{4,0},{5,1},{6,2},{7,3},{8,4},{9,5},{1... | collective-permute-start | bytes 122888 | tf_op jit(solution)/shard_map/ppermute | solution.py:405
  42.3 7.1 %collective-permute-start.3 = (f32[5,2,8,128]{3,2,1,0:T(8,128)S(1)}, f32[5,2,8,128]{3,2,1,0:T(8,128)S(1)}, u32[]{:S(2)}, u32[]{:S(2)}) collective-permute-start(f32[5,2,8,128]{3,2,1,0:T(8,128)S(1)} %get-tuple-element.12), channel_id=1, source_target_pairs={{0,4},{1,5},{2,6},{3,7},{4,8},{5,9},{6,10},{7,11},{8,12},{9,13},{1... | collective-permute-start | bytes 122888 | tf_op jit(solution)/shard_map/ppermute | solution.py:405

commit v5 on v4

--- a/solution.py
+++ b/solution.py
@@ -20,8 +20,7 @@
 GAMMA = 1.4
 
 VMEM = pl.BlockSpec(memory_space=pltpu.VMEM)
-SMEM = pl.BlockSpec(memory_space=pltpu.SMEM)
-HBM = pl.BlockSpec(memory_space=pltpu.HBM)
+HBM = pl.BlockSpec(memory_space=pl.ANY)
 
 
 def call(kernel, out_shapes, in_specs, scratch=(), flops=0, out=VMEM):
@@ -48,17 +47,10 @@
     return (lax.axis_index("blk") + lax.axis_index("gz")) % 2 == 0
 
 
-def split_kernel(state, message, arrived):
-    copies = []
+def split_kernel(state, message):
     for device in range(GROUP):
         rows = pl.ds(pl.multiple_of(quarter_of(device) * LINES, LINES), LINES)
-        copies.append(
-            pltpu.make_async_copy(state.at[:, rows], message.at[device], arrived.at[device])
-        )
-    for copy in copies:
-        copy.start()
-    for copy in copies:
-        copy.wait()
+        message[device] = state[:, rows]
 
 
 def join_kernel(received, state, arrived):
@@ -86,7 +78,9 @@
     return position, jnp.clip(key - first, 0, SLOTS - 1)
 
 
-def gather_kernel(counts, received, piece):
+def gather_kernel(held_counts, received, piece):
+    row = held_counts[...]
+    counts = [row[0, device] for device in range(GROUP)]
     for block_y in range(2):
         for xb in range(4):
             device, slot = place_of(counts, block_y * 4 + xb)
@@ -294,7 +288,7 @@
 
 
 def advance_kernel(
-    counts, first, own, second, w0, inner, from_above, from_below, message,
+    held_counts, first, own, second, w0, inner, from_below, from_above, message,
     uh, wh, changeh, total, u1, w1, change, done,
 ):
     wide = QUARTER + HALO
@@ -371,6 +365,8 @@
                         2 * xb : 2 * xb + 2, :
                     ]
 
+    row = held_counts[...]
+    counts = [row[0, GROUP + device] for device in range(GROUP)]
     start = jnp.int32(0)
     for device in range(GROUP):
         for slot in range(SLOTS):
@@ -393,8 +389,7 @@
     def row_of(counts):
         return lax.dynamic_slice(counts, (slab, group, 0), (1, 1, GROUP)).reshape(GROUP)
 
-    old_here = row_of(counts_old)
-    new_here = row_of(counts_new)
+    counts = jnp.concatenate([row_of(counts_old), row_of(counts_new)]).reshape(1, 2 * GROUP)
     members = [[g * GROUP + k for k in range(GROUP)] for g in range(groups)]
 
     def exchange(message):
@@ -423,18 +418,18 @@
     held = state_old.reshape(SLOTS, FIELDS, GROUP * ROWS, LANES).transpose(1, 2, 0, 3)
     held = held.reshape(slots.shape)
     arrivals = [pltpu.SemaphoreType.DMA((GROUP,))]
-    received = exchange(call(split_kernel, parts, [HBM], arrivals)(held))
-
-    own = call(gather_kernel, f32(FIELDS, 2 * QUARTER, ROWS, LANES), [SMEM, VMEM])(
-        old_here, received
+    received = exchange(call(split_kernel, parts, [VMEM])(held))
+
+    own = call(gather_kernel, f32(FIELDS, 2 * QUARTER, ROWS, LANES), [VMEM, VMEM])(
+        counts, received
     )
     first = trade(own, 0)
     second = trade(own, 1)
 
     edge = f32(FIELDS, 2, ROWS, LANES)
     lower, upper = call(edge_kernel, [edge, edge], [VMEM] * 3)(first, own, second)
+    from_below = along_y(upper, 1)
     from_above = along_y(lower, -1)
-    from_below = along_y(upper, 1)
     w0, inner = call(
         inner_kernel,
         [f32(FIELDS, wide + HALO, 2, ROWS, LANES), f32(FIELDS, wide, 2, ROWS, LANES)],
@@ -448,12 +443,12 @@
     finished = call(
         advance_kernel,
         parts,
-        [SMEM] + [VMEM] * 7,
+        [VMEM] * 8,
         [work(wide, 1), work(wide, 1), work(QUARTER, 1), work(wide, 3)]
         + [work(wide, 2), work(wide, 3), work(QUARTER, 2)]
         + [pltpu.VMEM((KEYS, FIELDS, ROWS, LANES), jnp.float32)],
         flops=1 << 24,
-    )(new_here, first, own, second, w0, inner, from_above, from_below)
+    )(counts, first, own, second, w0, inner, from_below, from_above)
     returned = exchange(finished)
     state = call(join_kernel, slots, [VMEM], arrivals, out=HBM)(returned)
     state = state.reshape(FIELDS, GROUP * ROWS, SLOTS, LANES).transpose(2, 0, 1, 3)

time: 64.3 us -> 60.3 us (0.938)
  the two profiles are of different devices: /device:TPU:56 before, /device:TPU:24 now
where the time goes in v5:
time: 60.3 us; the launch traced here: 59.9 us
  starting transfers between devices  28.8 us (48%)
  blocking collectives  11.6 us (19%)
  waiting for transfers between devices  11.2 us (19%)
  Pallas kernels  6.27 us (10%)
  local copies, waits for them, and re-layouts  1.88 us (3%)
    ppermute x2, starting transfers between devices, along_y(): return lax.ppermute(value, 'blk', route)  20.1 us
    all_to_all x1, blocking collectives, exchange(): return lax.all_to_all(message, 'blk', 0, 0, axis_index_groups=members)  11.6 us
    all_to_all x1, waiting for transfers between devices, exchange(): return lax.all_to_all(message, 'blk', 0, 0, axis_index_groups=members)  6.38 us
    ppermute x2, waiting for transfers between devices, trade(): return lax.ppermute(value, ('gz', 'blk'), route)  4.73 us
    ppermute x2, starting transfers between devices, trade(): return lax.ppermute(value, ('gz', 'blk'), route)  4.39 us
    all_to_all x1, starting transfers between devices, exchange(): return lax.all_to_all(message, 'blk', 0, 0, axis_index_groups=members)  4.29 us
    pallas_call x1, Pallas kernels, body(): call(advance_kernel, parts, [VMEM] * 8, [work(wide, 1), work(wide, 1), wo...  2.97 us
    pallas_call x1, Pallas kernels, body(): call(inner_kernel, [f32(FIELDS, wide + HALO, 2, ROWS, LANES), f32(FIELDS,...  1.53 us
  transfers between devices with their start and end apart: 5, of which 4 were waited for; matrix products, arithmetic and copies ran while one was open for 2% of the time, Pallas kernels for 3%

profile of v5, /device:TPU:24, one launch (start us, length us, event | category | flops | bytes accessed | tf_op | source)
XLA Modules:
  0.0 59.9 jit_solution(390432646798136743)
XLA Ops:
  0.0 0.0 copy-start
  0.0 1.0 %copy-done = f32[1,1,4,5,4096]{4,2,3,1,0:T(4,128)S(1)} copy-done((f32[1,1,4,5,4096]{4,2,3,1,0:T(4,128)S(1)}, f32[1,1,4,5,4096]{4,2,3,1,0:T(4,128)}, u32[]{:S(2)}) %copy-start) | copy-done | bytes 327704
  1.0 0.7 %shard_map.37 = f32[4,5,32,128]{3,2,1,0:T(8,128)} custom-call(f32[5,128,128]{2,1,0:T(8,128)S(1)} %bitcast.12), custom_call_target="tpu_custom_call" | custom-call | bytes 1048576 | tf_op jit(solution)/shard_map/pallas_call | solution.py:421
  1.7 4.3 %all-to-all-start = ((f32[4,5,32,128]{3,2,1,0:T(8,128)}), f32[4,5,32,128]{3,2,1,0:T(8,128)S(1)}, u32[]{:S(2)}, u32[]{:S(2)}) async-start(f32[4,5,32,128]{3,2,1,0:T(8,128)} %shard_map.37), calls=%async_computation | async-start | bytes 655360 | tf_op jit(solution)/shard_map/all_to_all | solution.py:396
  6.0 0.9 %dynamic-slice_reduce_fusion = (s32[4]{0:T(128)S(1)}, s32[4]{0:T(128)S(1)}) fusion(s32[16,16,4]{1,2,0:T(4,128)} %param.5, s32[]{:T(128)S(6)} %select_n.13, s32[]{:T(128)S(6)} %select_n.15, s32[16,16,4]{1,2,0:T(4,128)} %param.4), kind=kLoop, calls=%fused_computation | loop fusion | bytes 72 | tf_op jit(solution)/shard_map/dynamic_slice | solution.py:390
  6.9 0.1 add_bitcast_fusion.held_counts
  7.0 6.4 %all-to-all-done.received = f32[4,5,32,128]{3,2,1,0:T(8,128)S(1)} async-done(((f32[4,5,32,128]{3,2,1,0:T(8,128)}), f32[4,5,32,128]{3,2,1,0:T(8,128)S(1)}, u32[]{:S(2)}, u32[]{:S(2)}) %all-to-all-start) | async-done | bytes 327712 | tf_op jit(solution)/shard_map/all_to_all | solution.py:396
  13.4 0.2 shard_map.38.own
  13.6 1.9 %collective-permute-start.1 = (f32[5,8,8,128]{3,2,1,0:T(8,128)S(1)}, f32[5,8,8,128]{3,2,1,0:T(8,128)S(1)}, u32[]{:S(2)}, u32[]{:S(2)}) collective-permute-start(f32[5,8,8,128]{3,2,1,0:T(8,128)S(1)} %shard_map.38.own), channel_id=1, source_target_pairs={{0,960},{4,964},{8,968},{12,972},{16,976},{20,980},{24,984},{28,98... | collective-permute-start | bytes 491528 | tf_op jit(solution)/shard_map/ppermute | solution.py:413
  15.5 2.5 %collective-permute-start = (f32[5,8,8,128]{3,2,1,0:T(8,128)S(1)}, f32[5,8,8,128]{3,2,1,0:T(8,128)S(1)}, u32[]{:S(2)}, u32[]{:S(2)}) collective-permute-start(f32[5,8,8,128]{3,2,1,0:T(8,128)S(1)} %shard_map.38.own), channel_id=1, source_target_pairs={{0,1},{4,5},{8,9},{12,13},{16,17},{20,21},{24,25},{28,29},{32,33},... | collective-permute-start | bytes 491528 | tf_op jit(solution)/shard_map/ppermute | solution.py:413
  18.0 2.2 %collective-permute-done.1.second = f32[5,8,8,128]{3,2,1,0:T(8,128)S(1)} collective-permute-done((f32[5,8,8,128]{3,2,1,0:T(8,128)S(1)}, f32[5,8,8,128]{3,2,1,0:T(8,128)S(1)}, u32[]{:S(2)}, u32[]{:S(2)}) %collective-permute-start.1) | collective-permute-done | bytes 163872 | tf_op jit(solution)/shard_map/ppermute | solution.py:413
  20.2 2.5 %collective-permute-done.first = f32[5,8,8,128]{3,2,1,0:T(8,128)S(1)} collective-permute-done((f32[5,8,8,128]{3,2,1,0:T(8,128)S(1)}, f32[5,8,8,128]{3,2,1,0:T(8,128)S(1)}, u32[]{:S(2)}, u32[]{:S(2)}) %collective-permute-start) | collective-permute-done | bytes 163872 | tf_op jit(solution)/shard_map/ppermute | solution.py:413
  22.7 0.1 shard_map.40
  22.8 4.3 %collective-permute-start.2 = (f32[5,2,8,128]{3,2,1,0:T(8,128)S(1)}, f32[5,2,8,128]{3,2,1,0:T(8,128)S(1)}, u32[]{:S(2)}, u32[]{:S(2)}) collective-permute-start(f32[5,2,8,128]{3,2,1,0:T(8,128)S(1)} %get-tuple-element.11), channel_id=1, source_target_pairs={{0,4},{1,5},{2,6},{3,7},{4,8},{5,9},{6,10},{7,11},{8,12},{9,13},{1... | collective-permute-start | bytes 122888 | tf_op jit(solution)/shard_map/ppermute | solution.py:400
  27.1 15.9 %collective-permute-start.3 = (f32[5,2,8,128]{3,2,1,0:T(8,128)S(1)}, f32[5,2,8,128]{3,2,1,0:T(8,128)S(1)}, u32[]{:S(2)}, u32[]{:S(2)}) collective-permute-start(f32[5,2,8,128]{3,2,1,0:T(8,128)S(1)} %get-tuple-element.12), channel_id=1, source_target_pairs={{0,60},{1,61},{2,62},{3,63},{4,0},{5,1},{6,2},{7,3},{8,4},{9,5},{1... | collective-permute-start | bytes 122888 | tf_op jit(solution)/shard_map/ppermute | solution.py:400
  43.0 1.5 %shard_map.39 = (f32[5,12,2,8,128]{4,3,2,1,0:T(8,128)S(1)}, f32[5,8,2,8,128]{4,3,2,1,0:T(8,128)S(1)}) custom-call(f32[5,8,8,128]{3,2,1,0:T(8,128)S(1)} %collective-permute-done.first, f32[5,8,8,128]{3,2,1,0:T(8,128)S(1)} %shard_map.38.own, f32[5,8,8,128]{3,2,1,0:T(8,128)S(1)} %collective-permute-done.1.second), custom_call_target="tpu_custom_call" | custom-call | flops 16777216 | bytes 1048576 | tf_op jit(solution)/shard_map/pallas_call | solution.py:433
  44.5 0.0 collective-permute-done.2.from_below
  44.5 0.1 collective-permute-done.3.from_above
  44.6 3.0 %shard_map.41 = f32[4,5,32,128]{3,2,1,0:T(8,128)S(1)} custom-call(s32[1,8]{1,0:T(1,128)S(1)} %add_bitcast_fusion.held_counts, f32[5,8,8,128]{3,2,1,0:T(8,128)S(1)} %collective-permute-done.first, f32[5,8,8,128]{3,2,1,0:T(8,128)S(1)} %shard_map.38.own, f32[5,8,8,128]{3,2,1,0:T(8,128)S(1)} %collective-permute-done.1.second, ...), custom_call_target="tpu_custom_call" | custom-call | flops 16777216 | bytes 1048576 | tf_op jit(solution)/shard_map/pallas_call | solution.py:443
  47.6 11.6 %all_to_all.10.received = f32[4,5,32,128]{3,2,1,0:T(8,128)S(1)} all-to-all(f32[4,5,32,128]{3,2,1,0:T(8,128)S(1)} %shard_map.41), channel_id=1, replica_groups={{0,1,2,3},{4,5,6,7},{8,9,10,11},{12,13,14,15},{16,17,18,19},{20,21,22,2..., dimensions={0} | all-to-all | bytes 655360 | tf_op jit(solution)/shard_map/all_to_all | solution.py:396
  59.2 0.8 %shard_map.42 = f32[5,128,128]{2,1,0:T(8,128)} custom-call(f32[4,5,32,128]{3,2,1,0:T(8,128)S(1)} %all_to_all.10.received), custom_call_target="tpu_custom_call" | custom-call | bytes 1048576 | tf_op jit(solution)/shard_map/pallas_call | solution.py:453
Async XLA Ops:
  0.0 1.0 %copy-start = (f32[1,1,4,5,4096]{4,2,3,1,0:T(4,128)S(1)}, f32[1,1,4,5,4096]{4,2,3,1,0:T(4,128)}, u32[]{:S(2)}) copy-start(f32[1,1,4,5,4096]{4,2,3,1,0:T(4,128)} %param.3) | copy-start | bytes 983044
  1.7 11.7 %all-to-all-start = ((f32[4,5,32,128]{3,2,1,0:T(8,128)}), f32[4,5,32,128]{3,2,1,0:T(8,128)S(1)}, u32[]{:S(2)}, u32[]{:S(2)}) async-start(f32[4,5,32,128]{3,2,1,0:T(8,128)} %shard_map.37), calls=%async_computation | async-start | bytes 655360 | tf_op jit(solution)/shard_map/all_to_all | solution.py:396
  13.6 6.6 %collective-permute-start.1 = (f32[5,8,8,128]{3,2,1,0:T(8,128)S(1)}, f32[5,8,8,128]{3,2,1,0:T(8,128)S(1)}, u32[]{:S(2)}, u32[]{:S(2)}) collective-permute-start(f32[5,8,8,128]{3,2,1,0:T(8,128)S(1)} %shard_map.38.own), channel_id=1, source_target_pairs={{0,960},{4,964},{8,968},{12,972},{16,976},{20,980},{24,984},{28,98... | collective-permute-start | bytes 491528 | tf_op jit(solution)/shard_map/ppermute | solution.py:413
  15.5 7.2 %collective-permute-start = (f32[5,8,8,128]{3,2,1,0:T(8,128)S(1)}, f32[5,8,8,128]{3,2,1,0:T(8,128)S(1)}, u32[]{:S(2)}, u32[]{:S(2)}) collective-permute-start(f32[5,8,8,128]{3,2,1,0:T(8,128)S(1)} %shard_map.38.own), channel_id=1, source_target_pairs={{0,1},{4,5},{8,9},{12,13},{16,17},{20,21},{24,25},{28,29},{32,33},... | collective-permute-start | bytes 491528 | tf_op jit(solution)/shard_map/ppermute | solution.py:413
  22.8 21.7 %collective-permute-start.2 = (f32[5,2,8,128]{3,2,1,0:T(8,128)S(1)}, f32[5,2,8,128]{3,2,1,0:T(8,128)S(1)}, u32[]{:S(2)}, u32[]{:S(2)}) collective-permute-start(f32[5,2,8,128]{3,2,1,0:T(8,128)S(1)} %get-tuple-element.11), channel_id=1, source_target_pairs={{0,4},{1,5},{2,6},{3,7},{4,8},{5,9},{6,10},{7,11},{8,12},{9,13},{1... | collective-permute-start | bytes 122888 | tf_op jit(solution)/shard_map/ppermute | solution.py:400
  27.1 17.5 %collective-permute-start.3 = (f32[5,2,8,128]{3,2,1,0:T(8,128)S(1)}, f32[5,2,8,128]{3,2,1,0:T(8,128)S(1)}, u32[]{:S(2)}, u32[]{:S(2)}) collective-permute-start(f32[5,2,8,128]{3,2,1,0:T(8,128)S(1)} %get-tuple-element.12), channel_id=1, source_target_pairs={{0,60},{1,61},{2,62},{3,63},{4,0},{5,1},{6,2},{7,3},{8,4},{9,5},{1... | collective-permute-start | bytes 122888 | tf_op jit(solution)/shard_map/ppermute | solution.py:400

commit v6 on v5

--- a/solution.py
+++ b/solution.py
@@ -66,6 +66,14 @@
         copy.wait()
 
 
+def counts_here(held):
+    row = held[lax.axis_index("gz")]
+    device = lax.broadcasted_iota(jnp.int32, row.shape, 0)
+    group = lax.broadcasted_iota(jnp.int32, row.shape, 1)
+    here = jnp.where(group == lax.axis_index("blk") // GROUP, row, 0)
+    return [jnp.sum(jnp.where(device == k, here, 0)) for k in range(GROUP)]
+
+
 def place_of(counts, key):
     position = jnp.int32(0)
     first = jnp.int32(0)
@@ -79,8 +87,7 @@
 
 
 def gather_kernel(held_counts, received, piece):
-    row = held_counts[...]
-    counts = [row[0, device] for device in range(GROUP)]
+    counts = counts_here(held_counts)
     for block_y in range(2):
         for xb in range(4):
             device, slot = place_of(counts, block_y * 4 + xb)
@@ -100,7 +107,8 @@
     )
 
 
-def edge_kernel(first, own, second, lower, upper):
+def edge_kernel(first, own, second, x_change, lower, upper):
+    del x_change
     first_half = lax.broadcasted_iota(jnp.int32, (4, LANES), 1) < 64
 
     def rows(field, layer, block_y):
@@ -226,15 +234,15 @@
 Y_LAYERS = 4
 
 
-def rate_x(total, prim, count, blocks):
+def rate_x(total, prim, count, blocks, source=2, target=0, batch=X_LAYERS):
     def planes(step, carry):
-        z = step * X_LAYERS
-        values = [prim[f, pl.ds(z + 2, X_LAYERS), blocks] for f in range(FIELDS)]
+        z = step * batch
+        values = [prim[f, pl.ds(z + source, batch), blocks] for f in range(FIELDS)]
         for f, change in enumerate(sweep_x(values)):
-            total[f, pl.ds(z, X_LAYERS), blocks] = change
+            total[f, pl.ds(z + target, batch), blocks] = change
         return carry
 
-    lax.fori_loop(0, count // X_LAYERS, planes, 0)
+    lax.fori_loop(0, count // batch, planes, 0)
 
 
 def rate_z(total, prim, count, blocks):
@@ -267,15 +275,27 @@
 EDGE = slice(2, 3)
 
 
-def inner_kernel(first, own, second, w0, change):
+def own_kernel(own, prim, x_change):
     for z in range(QUARTER):
+        values = [own[f, 2 * z : 2 * z + 2] for f in range(FIELDS)]
+        for f, value in enumerate(primitives(values)):
+            prim[f, z] = value
+    rate_x(x_change, prim, QUARTER, INNER, 0, 0)
+
+
+def inner_kernel(first, prim, x_change, second, w0, change):
+    for z in range(HALO):
         index = (slice(None), slice(2 * z, 2 * z + 2))
         below, above = below_above(first, second, index)
-        for base, piece in ((0, below), (QUARTER, own[index]), (2 * QUARTER, above)):
+        for base, piece in ((0, below), (HALO + QUARTER, above)):
             values = [piece[f] for f in range(FIELDS)]
             for f, value in enumerate(primitives(values)):
                 w0[f, base + z] = value
-    rate_x(change, w0, QUARTER + HALO, INNER)
+    for f in range(FIELDS):
+        w0[f, HALO : HALO + QUARTER] = prim[f]
+        change[f, 2 : 2 + QUARTER] = x_change[f]
+    rate_x(change, w0, 2, INNER, 2, 0, 2)
+    rate_x(change, w0, 2, INNER, HALO + QUARTER, 2 + QUARTER, 2)
     rate_z(change, w0, QUARTER + HALO, INNER)
 
 
@@ -365,8 +385,7 @@
                         2 * xb : 2 * xb + 2, :
                     ]
 
-    row = held_counts[...]
-    counts = [row[0, GROUP + device] for device in range(GROUP)]
+    counts = counts_here(held_counts)
     start = jnp.int32(0)
     for device in range(GROUP):
         for slot in range(SLOTS):
@@ -383,13 +402,6 @@
     slabs = lax.axis_size("gz")
     places = lax.axis_size("blk")
     groups = places // GROUP
-    slab = lax.axis_index("gz")
-    group = lax.axis_index("blk") // GROUP
-
-    def row_of(counts):
-        return lax.dynamic_slice(counts, (slab, group, 0), (1, 1, GROUP)).reshape(GROUP)
-
-    counts = jnp.concatenate([row_of(counts_old), row_of(counts_new)]).reshape(1, 2 * GROUP)
     members = [[g * GROUP + k for k in range(GROUP)] for g in range(groups)]
 
     def exchange(message):
@@ -421,21 +433,25 @@
     received = exchange(call(split_kernel, parts, [VMEM])(held))
 
     own = call(gather_kernel, f32(FIELDS, 2 * QUARTER, ROWS, LANES), [VMEM, VMEM])(
-        counts, received
+        counts_old.transpose(0, 2, 1), received
     )
     first = trade(own, 0)
     second = trade(own, 1)
+    block = f32(FIELDS, QUARTER, 2, ROWS, LANES)
+    prim, x_change = call(own_kernel, [block, block], [VMEM], flops=1 << 24)(own)
 
     edge = f32(FIELDS, 2, ROWS, LANES)
-    lower, upper = call(edge_kernel, [edge, edge], [VMEM] * 3)(first, own, second)
+    lower, upper = call(edge_kernel, [edge, edge], [VMEM] * 4)(
+        first, own, second, x_change
+    )
     from_below = along_y(upper, 1)
     from_above = along_y(lower, -1)
     w0, inner = call(
         inner_kernel,
         [f32(FIELDS, wide + HALO, 2, ROWS, LANES), f32(FIELDS, wide, 2, ROWS, LANES)],
-        [VMEM] * 3,
+        [VMEM] * 4,
         flops=1 << 24,
-    )(first, own, second)
+    )(first, prim, x_change, second)
 
     def work(*shape):
         return pltpu.VMEM((FIELDS,) + shape + (ROWS, LANES), jnp.float32)
@@ -448,7 +464,7 @@
         + [work(wide, 2), work(wide, 3), work(QUARTER, 2)]
         + [pltpu.VMEM((KEYS, FIELDS, ROWS, LANES), jnp.float32)],
         flops=1 << 24,
-    )(counts, first, own, second, w0, inner, from_below, from_above)
+    )(counts_new.transpose(0, 2, 1), first, own, second, w0, inner, from_below, from_above)
     returned = exchange(finished)
     state = call(join_kernel, slots, [VMEM], arrivals, out=HBM)(returned)
     state = state.reshape(FIELDS, GROUP * ROWS, SLOTS, LANES).transpose(2, 0, 1, 3)

time: 60.3 us -> 58.5 us (0.970)
  the two profiles are of different devices: /device:TPU:24 before, /device:TPU:56 now
where the time goes in v6:
time: 58.5 us; the launch traced here: 58.2 us
  starting transfers between devices  24.5 us (42%)
  blocking collectives  22.2 us (38%)
  Pallas kernels  5.49 us (9%)
  waiting for transfers between devices  4.87 us (8%)
  local copies, waits for them, and re-layouts  0.98 us (2%)
    all_to_all x2, blocking collectives, exchange(): return lax.all_to_all(message, 'blk', 0, 0, axis_index_groups=members)  22.2 us
    ppermute x2, starting transfers between devices, along_y(): return lax.ppermute(value, 'blk', route)  20.1 us
    ppermute x2, starting transfers between devices, trade(): return lax.ppermute(value, ('gz', 'blk'), route)  4.39 us
    ppermute x2, waiting for transfers between devices, trade(): return lax.ppermute(value, ('gz', 'blk'), route)  4.19 us
    pallas_call x1, Pallas kernels, body(): call(advance_kernel, parts, [VMEM] * 8, [work(wide, 1), work(wide, 1), wo...  2.94 us
  transfers between devices with their start and end apart: 4, of which 3 were waited for; matrix products, arithmetic and copies ran while one was open for 0% of the time, Pallas kernels for 3%

profile of v6, /device:TPU:56, one launch (start us, length us, event | category | flops | bytes accessed | tf_op | source)
XLA Modules:
  0.0 58.2 jit_solution(12681945581106482057)
XLA Ops:
  0.0 0.0 copy-start
  0.0 1.0 %copy-done = f32[1,1,4,5,4096]{4,2,3,1,0:T(4,128)S(1)} copy-done((f32[1,1,4,5,4096]{4,2,3,1,0:T(4,128)S(1)}, f32[1,1,4,5,4096]{4,2,3,1,0:T(4,128)}, u32[]{:S(2)}) %copy-start) | copy-done | bytes 327704
  1.0 0.0 copy-start.1
  1.0 11.5 %all_to_all.10.received = f32[4,5,32,128]{3,2,1,0:T(8,128)S(1)} all-to-all(f32[4,5,32,128]{3,2,1,0:T(8,128)S(1)} %shard_map.37), channel_id=1, replica_groups={{0,1,2,3},{4,5,6,7},{8,9,10,11},{12,13,14,15},{16,17,18,19},{20,21,22,2..., dimensions={0} | all-to-all | bytes 655360 | tf_op jit(solution)/shard_map/all_to_all | solution.py:408
  12.5 0.0 copy-done.1
  12.5 0.2 shard_map.38.own
  12.7 2.5 %collective-permute-start = (f32[5,8,8,128]{3,2,1,0:T(8,128)S(1)}, f32[5,8,8,128]{3,2,1,0:T(8,128)S(1)}, u32[]{:S(2)}, u32[]{:S(2)}) collective-permute-start(f32[5,8,8,128]{3,2,1,0:T(8,128)S(1)} %shard_map.38.own), channel_id=1, source_target_pairs={{0,1},{4,5},{8,9},{12,13},{16,17},{20,21},{24,25},{28,29},{32,33},... | collective-permute-start | bytes 491528 | tf_op jit(solution)/shard_map/ppermute | solution.py:425
  15.2 1.9 %collective-permute-start.1 = (f32[5,8,8,128]{3,2,1,0:T(8,128)S(1)}, f32[5,8,8,128]{3,2,1,0:T(8,128)S(1)}, u32[]{:S(2)}, u32[]{:S(2)}) collective-permute-start(f32[5,8,8,128]{3,2,1,0:T(8,128)S(1)} %shard_map.38.own), channel_id=1, source_target_pairs={{0,960},{4,964},{8,968},{12,972},{16,976},{20,980},{24,984},{28,98... | collective-permute-start | bytes 491528 | tf_op jit(solution)/shard_map/ppermute | solution.py:425
  17.1 0.5 shard_map.39
  17.6 2.3 %collective-permute-done.first = f32[5,8,8,128]{3,2,1,0:T(8,128)S(1)} collective-permute-done((f32[5,8,8,128]{3,2,1,0:T(8,128)S(1)}, f32[5,8,8,128]{3,2,1,0:T(8,128)S(1)}, u32[]{:S(2)}, u32[]{:S(2)}) %collective-permute-start) | collective-permute-done | bytes 163872 | tf_op jit(solution)/shard_map/ppermute | solution.py:425
  19.9 1.9 %collective-permute-done.1.second = f32[5,8,8,128]{3,2,1,0:T(8,128)S(1)} collective-permute-done((f32[5,8,8,128]{3,2,1,0:T(8,128)S(1)}, f32[5,8,8,128]{3,2,1,0:T(8,128)S(1)}, u32[]{:S(2)}, u32[]{:S(2)}) %collective-permute-start.1) | collective-permute-done | bytes 163872 | tf_op jit(solution)/shard_map/ppermute | solution.py:425
  21.8 0.1 shard_map.41
  21.9 4.3 %collective-permute-start.2 = (f32[5,2,8,128]{3,2,1,0:T(8,128)S(1)}, f32[5,2,8,128]{3,2,1,0:T(8,128)S(1)}, u32[]{:S(2)}, u32[]{:S(2)}) collective-permute-start(f32[5,2,8,128]{3,2,1,0:T(8,128)S(1)} %get-tuple-element.15), channel_id=1, source_target_pairs={{0,4},{1,5},{2,6},{3,7},{4,8},{5,9},{6,10},{7,11},{8,12},{9,13},{1... | collective-permute-start | bytes 122888 | tf_op jit(solution)/shard_map/ppermute | solution.py:412
  26.2 15.9 %collective-permute-start.3 = (f32[5,2,8,128]{3,2,1,0:T(8,128)S(1)}, f32[5,2,8,128]{3,2,1,0:T(8,128)S(1)}, u32[]{:S(2)}, u32[]{:S(2)}) collective-permute-start(f32[5,2,8,128]{3,2,1,0:T(8,128)S(1)} %get-tuple-element.16), channel_id=1, source_target_pairs={{0,60},{1,61},{2,62},{3,63},{4,0},{5,1},{6,2},{7,3},{8,4},{9,5},{1... | collective-permute-start | bytes 122888 | tf_op jit(solution)/shard_map/ppermute | solution.py:412
  42.1 0.0 copy-start.2
  42.1 0.9 %shard_map.40 = (f32[5,12,2,8,128]{4,3,2,1,0:T(8,128)S(1)}, f32[5,8,2,8,128]{4,3,2,1,0:T(8,128)S(1)}) custom-call(f32[5,8,8,128]{3,2,1,0:T(8,128)S(1)} %collective-permute-done.first, f32[5,4,2,8,128]{4,3,2,1,0:T(8,128)S(1)} %get-tuple-element.11.prim, f32[5,4,2,8,128]{4,3,2,1,0:T(8,128)S(1)} %get-tuple-element.12.x_change, ...), custom_call_target="tpu_custom_call" | custom-call | flops 16777216 | bytes 1048576 | tf_op jit(solution)/shard_map/pallas_call | solution.py:449
  43.1 0.0 collective-permute-done.2.from_below
  43.1 0.7 %collective-permute-done.3.from_above = f32[5,2,8,128]{3,2,1,0:T(8,128)S(1)} collective-permute-done((f32[5,2,8,128]{3,2,1,0:T(8,128)S(1)}, f32[5,2,8,128]{3,2,1,0:T(8,128)S(1)}, u32[]{:S(2)}, u32[]{:S(2)}) %collective-permute-start.3) | collective-permute-done | bytes 40992 | tf_op jit(solution)/shard_map/ppermute | solution.py:412
  43.7 0.0 copy-done.2
  43.7 2.9 %shard_map.42 = f32[4,5,32,128]{3,2,1,0:T(8,128)S(1)} custom-call(s32[16,4,16]{2,1,0:T(4,128)S(1)} %bitcast.14, f32[5,8,8,128]{3,2,1,0:T(8,128)S(1)} %collective-permute-done.first, f32[5,8,8,128]{3,2,1,0:T(8,128)S(1)} %shard_map.38.own, f32[5,8,8,128]{3,2,1,0:T(8,128)S(1)} %collective-permute-done.1.second, f32[5,12,2,8,128]{4,3,2,1,0:T(8,128)S(1)} %get-tuple-element.13.w0, ...), custom_call_target="tpu_custom_call" | custom-call | flops 16777216 | bytes 1048576 | tf_op jit(solution)/shard_map/pallas_call | solution.py:459
  46.7 10.7 %all_to_all.11.received = f32[4,5,32,128]{3,2,1,0:T(8,128)S(1)} all-to-all(f32[4,5,32,128]{3,2,1,0:T(8,128)S(1)} %shard_map.42), channel_id=1, replica_groups={{0,1,2,3},{4,5,6,7},{8,9,10,11},{12,13,14,15},{16,17,18,19},{20,21,22,2..., dimensions={0} | all-to-all | bytes 655360 | tf_op jit(solution)/shard_map/all_to_all | solution.py:408
  57.4 0.8 %shard_map.43 = f32[5,128,128]{2,1,0:T(8,128)} custom-call(f32[4,5,32,128]{3,2,1,0:T(8,128)S(1)} %all_to_all.11.received), custom_call_target="tpu_custom_call" | custom-call | bytes 1048576 | tf_op jit(solution)/shard_map/pallas_call | solution.py:469
  (1 shorter events, 0.0 us)
Async XLA Ops:
  0.0 1.0 %copy-start = (f32[1,1,4,5,4096]{4,2,3,1,0:T(4,128)S(1)}, f32[1,1,4,5,4096]{4,2,3,1,0:T(4,128)}, u32[]{:S(2)}) copy-start(f32[1,1,4,5,4096]{4,2,3,1,0:T(4,128)} %param.3) | copy-start | bytes 983044
  1.0 11.5 %copy-start.1 = (s32[16,16,4]{1,2,0:T(4,128)S(1)}, s32[16,16,4]{1,2,0:T(4,128)}, u32[]{:S(2)}) copy-start(s32[16,16,4]{1,2,0:T(4,128)} %param.4) | copy-start | bytes 12292
  12.7 7.2 %collective-permute-start = (f32[5,8,8,128]{3,2,1,0:T(8,128)S(1)}, f32[5,8,8,128]{3,2,1,0:T(8,128)S(1)}, u32[]{:S(2)}, u32[]{:S(2)}) collective-permute-start(f32[5,8,8,128]{3,2,1,0:T(8,128)S(1)} %shard_map.38.own), channel_id=1, source_target_pairs={{0,1},{4,5},{8,9},{12,13},{16,17},{20,21},{24,25},{28,29},{32,33},... | collective-permute-start | bytes 491528 | tf_op jit(solution)/shard_map/ppermute | solution.py:425
  15.2 6.6 %collective-permute-start.1 = (f32[5,8,8,128]{3,2,1,0:T(8,128)S(1)}, f32[5,8,8,128]{3,2,1,0:T(8,128)S(1)}, u32[]{:S(2)}, u32[]{:S(2)}) collective-permute-start(f32[5,8,8,128]{3,2,1,0:T(8,128)S(1)} %shard_map.38.own), channel_id=1, source_target_pairs={{0,960},{4,964},{8,968},{12,972},{16,976},{20,980},{24,984},{28,98... | collective-permute-start | bytes 491528 | tf_op jit(solution)/shard_map/ppermute | solution.py:425
  21.9 21.1 %collective-permute-start.2 = (f32[5,2,8,128]{3,2,1,0:T(8,128)S(1)}, f32[5,2,8,128]{3,2,1,0:T(8,128)S(1)}, u32[]{:S(2)}, u32[]{:S(2)}) collective-permute-start(f32[5,2,8,128]{3,2,1,0:T(8,128)S(1)} %get-tuple-element.15), channel_id=1, source_target_pairs={{0,4},{1,5},{2,6},{3,7},{4,8},{5,9},{6,10},{7,11},{8,12},{9,13},{1... | collective-permute-start | bytes 122888 | tf_op jit(solution)/shard_map/ppermute | solution.py:412
  26.2 17.5 %collective-permute-start.3 = (f32[5,2,8,128]{3,2,1,0:T(8,128)S(1)}, f32[5,2,8,128]{3,2,1,0:T(8,128)S(1)}, u32[]{:S(2)}, u32[]{:S(2)}) collective-permute-start(f32[5,2,8,128]{3,2,1,0:T(8,128)S(1)} %get-tuple-element.16), channel_id=1, source_target_pairs={{0,60},{1,61},{2,62},{3,63},{4,0},{5,1},{6,2},{7,3},{8,4},{9,5},{1... | collective-permute-start | bytes 122888 | tf_op jit(solution)/shard_map/ppermute | solution.py:412
  42.1 1.7 %copy-start.2 = (s32[16,16,4]{1,2,0:T(4,128)S(1)}, s32[16,16,4]{1,2,0:T(4,128)}, u32[]{:S(2)}) copy-start(s32[16,16,4]{1,2,0:T(4,128)} %param.5) | copy-start | bytes 12292

commit v7 on v6

--- a/solution.py
+++ b/solution.py
@@ -190,11 +190,11 @@
     if amount > 0:
         moved = [pltpu.roll(v, 16, across) for v in value]
         upper = moved
-        lower = [moved[i - 1] for i in range(3)]
+        lower = moved[-1:] + moved[:-1]
         outer = lane < 16
     else:
         moved = [pltpu.roll(v, LANES - 16, across) for v in value]
-        upper = [moved[(i + 1) % 3] for i in range(3)]
+        upper = moved[1:] + moved[:1]
         lower = moved
         outer = lane >= LANES - 16
     edge = [
@@ -220,7 +220,7 @@
     half = [[0.5 * minmod(a, b) for a, b in zip(p, d)] for p, d in zip(behind, steps)]
     beyond = [shift_y(h, -1) for h in half]
     fluxes = []
-    for i in range(3):
+    for i in range(len(primitive[0])):
         left = [q[i] + h[i] for q, h in zip(primitive, half)]
         right = [q[i] - h[i] for q, h in zip(ahead, beyond)]
         fluxes.append(face_flux(left, right, 1))
@@ -230,6 +230,48 @@
     return out
 
 
+def sweep_strip(primitive):
+    def shift(value, amount):
+        return pltpu.roll(value, 16 if amount > 0 else LANES - 16, value.ndim - 1)
+
+    ahead = [shift(q, -1) for q in primitive]
+    steps = [b - q for q, b in zip(primitive, ahead)]
+    half = [0.5 * minmod(shift(d, 1), d) for d in steps]
+    left = [q + h for q, h in zip(primitive, half)]
+    right = [shift(q - h, -1) for q, h in zip(primitive, half)]
+    return [shift(f, 1) - f for f in face_flux(left, right, 1)]
+
+
+def lane_and_odd():
+    lane = lax.broadcasted_iota(jnp.int32, (ROWS, LANES), 1)
+    return lane, lax.broadcasted_iota(jnp.int32, (ROWS, LANES), 0) % 2 == 1
+
+
+def ends_of(low, high):
+    _, odd = lane_and_odd()
+    both = jnp.where(odd, high, low)
+    return pltpu.roll(both, LANES // 2, both.ndim - 1)
+
+
+def strip_halo():
+    lane, odd = lane_and_odd()
+    return odd == (lane >= LANES // 2)
+
+
+def put_ends(low, high, strip):
+    lane, odd = lane_and_odd()
+    ends = pltpu.roll(strip, LANES // 2, strip.ndim - 1)
+    low = jnp.where(jnp.logical_and(jnp.logical_not(odd), lane < 32), ends, low)
+    return low, jnp.where(jnp.logical_and(odd, lane >= LANES - 32), ends, high)
+
+
+def repeat(count, step):
+    if count == 1:
+        step(0, 0)
+    else:
+        lax.fori_loop(0, count, step, 0)
+
+
 X_LAYERS = 4
 Y_LAYERS = 4
 
@@ -242,7 +284,7 @@
             total[f, pl.ds(z + target, batch), blocks] = change
         return carry
 
-    lax.fori_loop(0, count // batch, planes, 0)
+    repeat(count // batch, planes)
 
 
 def rate_z(total, prim, count, blocks):
@@ -268,22 +310,36 @@
             total[f, z, blocks] = total[f, z, blocks] + (state[4][f] - after[4][f])
         return after
 
-    lax.fori_loop(0, count, layer, face(0, here, half, ahead, ahead_step))
+    lax.fori_loop(0, count, layer, face(0, here, half, ahead, ahead_step), unroll=True)
 
 
 INNER = slice(0, 2)
 EDGE = slice(2, 3)
 
 
-def own_kernel(own, prim, x_change):
+def rate_y(total, prim, count, source, target, batch):
+    def planes(step, carry):
+        here = pl.ds(step * batch + target, batch)
+        shifted = pl.ds(step * batch + source, batch)
+        changes = sweep_y([[prim[f, shifted, 0], prim[f, shifted, 1]] for f in range(FIELDS)])
+        for f in range(FIELDS):
+            for i in range(2):
+                total[f, here, i] = changes[f][i]
+        return carry
+
+    repeat(count // batch, planes)
+
+
+def own_kernel(own, prim, x_change, y_change):
     for z in range(QUARTER):
         values = [own[f, 2 * z : 2 * z + 2] for f in range(FIELDS)]
         for f, value in enumerate(primitives(values)):
             prim[f, z] = value
     rate_x(x_change, prim, QUARTER, INNER, 0, 0)
-
-
-def inner_kernel(first, prim, x_change, second, w0, change):
+    rate_y(y_change, prim, QUARTER, 0, 0, QUARTER)
+
+
+def inner_kernel(first, prim, x_change, y_change, second, change, along_y, w0):
     for z in range(HALO):
         index = (slice(None), slice(2 * z, 2 * z + 2))
         below, above = below_above(first, second, index)
@@ -294,22 +350,17 @@
     for f in range(FIELDS):
         w0[f, HALO : HALO + QUARTER] = prim[f]
         change[f, 2 : 2 + QUARTER] = x_change[f]
+        along_y[f, 2 : 2 + QUARTER] = y_change[f]
     rate_x(change, w0, 2, INNER, 2, 0, 2)
     rate_x(change, w0, 2, INNER, HALO + QUARTER, 2 + QUARTER, 2)
+    rate_y(along_y, w0, 2, 2, 0, 2)
+    rate_y(along_y, w0, 2, HALO + QUARTER, 2 + QUARTER, 2)
     rate_z(change, w0, QUARTER + HALO, INNER)
 
 
-def first_step(layer, base, u1, w1, total):
-    values = [base[f] + TIME_STEP * total[f, layer, INNER] for f in range(FIELDS)]
-    for f, value in enumerate(values):
-        u1[f, layer] = value
-    for f, value in enumerate(primitives(values)):
-        w1[f, layer, INNER] = value
-
-
 def advance_kernel(
-    held_counts, first, own, second, w0, inner, from_below, from_above, message,
-    uh, wh, changeh, total, u1, w1, change, done,
+    held_counts, first, own, second, inner, along_y, from_below, from_above, message,
+    us, ws, changes_h, u1s, u1, w1, w1s, change, done,
 ):
     wide = QUARTER + HALO
     first_half = lax.broadcasted_iota(jnp.int32, (4, LANES), 1) < 64
@@ -319,66 +370,76 @@
             above = from_above[field, pair // 2, rows, :]
             below = from_below[field, pair // 2, rows, :]
             for z, halo in (
-                (pair, jnp.where(first_half, above, pltpu.roll(below, 64, 1))),
-                (pair + 4, jnp.where(first_half, pltpu.roll(above, 64, 1), below)),
+                (pair, jnp.where(first_half, below, pltpu.roll(above, 64, 1))),
+                (pair + 4, jnp.where(first_half, pltpu.roll(below, 64, 1), above)),
             ):
-                uh[field, z, 0, pl.ds(0, 4, stride=2), :] = halo
-                uh[field, z, 0, pl.ds(1, 4, stride=2), :] = halo
-    for f, value in enumerate(primitives([uh[f] for f in range(FIELDS)])):
-        wh[f] = value
-
-    rate_x(changeh, wh, QUARTER, slice(0, 1))
-    rate_z(changeh, wh, QUARTER, slice(0, 1))
-
-    def planes(step, carry):
-        z = step * Y_LAYERS
-        here, shifted = pl.ds(z, Y_LAYERS), pl.ds(z + 2, Y_LAYERS)
-        prims = [[w0[f, shifted, 0], w0[f, shifted, 1], wh[f, here, 0]] for f in range(FIELDS)]
-        changes = sweep_y(prims)
-        for f in range(FIELDS):
-            for i in range(2):
-                total[f, here, i] = inner[f, here, i] + changes[f][i]
-            total[f, here, 2] = changes[f][2]
-        return carry
-
-    lax.fori_loop(0, wide // Y_LAYERS, planes, 0)
-
-    for z in range(QUARTER):
-        index = (slice(None), slice(2 * z, 2 * z + 2))
-        if z >= 2:
-            layer, piece = z - 2, below_above(first, second, index)[0]
-            first_step(layer, piece, u1, w1, total)
-        else:
-            layer, piece = z + 2 + QUARTER, below_above(first, second, index)[1]
-            first_step(layer, piece, u1, w1, total)
-        first_step(z + 2, own[index], u1, w1, total)
-    for z in range(QUARTER):
+                us[field, z, 0, pl.ds(0, 4, stride=2), :] = halo
+                us[field, z, 0, pl.ds(1, 4, stride=2), :] = halo
+
+    def u0_of(layer):
+        if 2 <= layer < 2 + QUARTER:
+            return own[:, 2 * (layer - 2) : 2 * (layer - 2) + 2]
+        if layer < 2:
+            return below_above(first, second, (slice(None), slice(2 * layer + 4, 2 * layer + 6)))[0]
+        at = 2 * (layer - 2 - QUARTER)
+        return below_above(first, second, (slice(None), slice(at, at + 2)))[1]
+
+    halo = strip_halo()
+    for layer in range(wide):
+        base = u0_of(layer)
         values = [
-            uh[f, z + 2] + TIME_STEP * (total[f, z + 2, EDGE] + changeh[f, z])
+            jnp.where(halo, us[f, layer, 0], ends_of(base[f, 0], base[f, 1]))
             for f in range(FIELDS)
         ]
+        for f, value in enumerate(values):
+            us[f, layer, 0] = value
         for f, value in enumerate(primitives(values)):
-            w1[f, z + 2, EDGE] = value
+            ws[f, layer, 0] = value
+
+    rate_x(changes_h, ws, QUARTER, slice(0, 1))
+    rate_z(changes_h, ws, QUARTER, slice(0, 1))
+
+    sweeps = sweep_strip([ws[f, :, 0] for f in range(FIELDS)])
+    for f in range(FIELDS):
+        u1s[f, :, 0] = sweeps[f]
+
+    for layer in range(wide):
+        base = u0_of(layer)
+        low, high, strip = [], [], []
+        for f in range(FIELDS):
+            rest = ends_of(inner[f, layer, 0], inner[f, layer, 1])
+            if 2 <= layer < 2 + QUARTER:
+                rest = jnp.where(halo, changes_h[f, layer - 2, 0], rest)
+            strip.append(us[f, layer, 0] + TIME_STEP * (rest + u1s[f, layer, 0]))
+            ends = [
+                base[f, i] + TIME_STEP * (inner[f, layer, i] + along_y[f, layer, i])
+                for i in range(2)
+            ]
+            ends = put_ends(ends[0], ends[1], strip[f])
+            low.append(ends[0])
+            high.append(ends[1])
+            u1[f, layer, 0], u1[f, layer, 1] = ends
+        for f, value in enumerate(primitives(low)):
+            w1[f, layer, 0] = value
+        for f, value in enumerate(primitives(high)):
+            w1[f, layer, 1] = value
+        if 2 <= layer < 2 + QUARTER:
+            strip = [jnp.where(halo, s, ends_of(l, h)) for s, l, h in zip(strip, low, high)]
+            for f, value in enumerate(primitives(strip)):
+                w1s[f, layer - 2] = value
 
     rate_x(change, w1, QUARTER, INNER)
     rate_z(change, w1, QUARTER, INNER)
-
-    def last_planes(step, carry):
-        z = step * 4
-        here, shifted = pl.ds(z, 4), pl.ds(z + 2, 4)
-        changes = sweep_y([[w1[f, shifted, i] for i in range(3)] for f in range(FIELDS)])
-        for f in range(FIELDS):
-            for i in range(2):
-                change[f, here, i] = change[f, here, i] + changes[f][i]
-        return carry
-
-    lax.fori_loop(0, 1, last_planes, 0)
-
-    for z in range(QUARTER):
-        for field in range(FIELDS):
-            for block_y in range(2):
+    shifted = slice(2, 2 + QUARTER)
+    sweeps = sweep_y([[w1[f, shifted, 0], w1[f, shifted, 1]] for f in range(FIELDS)])
+    strips_y = sweep_strip([w1s[f] for f in range(FIELDS)])
+    for field in range(FIELDS):
+        sweeps_y = put_ends(sweeps[field][0], sweeps[field][1], strips_y[field])
+        for block_y in range(2):
+            for z in range(QUARTER):
+                rate = change[field, z, block_y] + sweeps_y[block_y][z]
                 value = 0.5 * own[field, 2 * z + block_y] + 0.5 * (
-                    u1[field, z + 2, block_y] + TIME_STEP * change[field, z, block_y]
+                    u1[field, z + 2, block_y] + TIME_STEP * rate
                 )
                 for xb in range(4):
                     done[block_y * 4 + xb, field, 2 * z : 2 * z + 2, :] = value[
@@ -438,7 +499,7 @@
     first = trade(own, 0)
     second = trade(own, 1)
     block = f32(FIELDS, QUARTER, 2, ROWS, LANES)
-    prim, x_change = call(own_kernel, [block, block], [VMEM], flops=1 << 24)(own)
+    prim, x_change, y_change = call(own_kernel, [block] * 3, [VMEM], flops=1 << 24)(own)
 
     edge = f32(FIELDS, 2, ROWS, LANES)
     lower, upper = call(edge_kernel, [edge, edge], [VMEM] * 4)(
@@ -446,25 +507,23 @@
     )
     from_below = along_y(upper, 1)
     from_above = along_y(lower, -1)
-    w0, inner = call(
-        inner_kernel,
-        [f32(FIELDS, wide + HALO, 2, ROWS, LANES), f32(FIELDS, wide, 2, ROWS, LANES)],
-        [VMEM] * 4,
-        flops=1 << 24,
-    )(first, prim, x_change, second)
 
     def work(*shape):
         return pltpu.VMEM((FIELDS,) + shape + (ROWS, LANES), jnp.float32)
 
+    change = f32(FIELDS, wide, 2, ROWS, LANES)
+    inner, inner_y = call(
+        inner_kernel, [change, change], [VMEM] * 5, [work(wide + HALO, 2)], flops=1 << 24
+    )(first, prim, x_change, y_change, second)
     finished = call(
         advance_kernel,
         parts,
         [VMEM] * 8,
-        [work(wide, 1), work(wide, 1), work(QUARTER, 1), work(wide, 3)]
-        + [work(wide, 2), work(wide, 3), work(QUARTER, 2)]
+        [work(wide, 1), work(wide, 1), work(QUARTER, 1), work(wide, 1)]
+        + [work(wide, 2), work(wide, 2), work(QUARTER), work(QUARTER, 2)]
         + [pltpu.VMEM((KEYS, FIELDS, ROWS, LANES), jnp.float32)],
         flops=1 << 24,
-    )(counts_new.transpose(0, 2, 1), first, own, second, w0, inner, from_below, from_above)
+    )(counts_new.transpose(0, 2, 1), first, own, second, inner, inner_y, from_below, from_above)
     returned = exchange(finished)
     state = call(join_kernel, slots, [VMEM], arrivals, out=HBM)(returned)
     state = state.reshape(FIELDS, GROUP * ROWS, SLOTS, LANES).transpose(2, 0, 1, 3)

time: 58.5 us -> 58.1 us (level)
  no operation moved by 1% of the time
where the time goes in v7:
time: 58.1 us; the launch traced here: 57.7 us
  starting transfers between devices  24.5 us (42%)
  blocking collectives  22.2 us (38%)
  Pallas kernels  5.48 us (9%)
  waiting for transfers between devices  4.39 us (8%)
  local copies, waits for them, and re-layouts  0.98 us (2%)
    all_to_all x2, blocking collectives, exchange(): return lax.all_to_all(message, 'blk', 0, 0, axis_index_groups=members)  22.2 us
    ppermute x2, starting transfers between devices, along_y(): return lax.ppermute(value, 'blk', route)  20.1 us
    ppermute x2, starting transfers between devices, trade(): return lax.ppermute(value, ('gz', 'blk'), route)  4.39 us
    ppermute x2, waiting for transfers between devices, trade(): return lax.ppermute(value, ('gz', 'blk'), route)  3.86 us
    pallas_call x1, Pallas kernels, body(): call(advance_kernel, parts, [VMEM] * 8, [work(wide, 1), work(wide, 1), wo...  2.46 us
  transfers between devices with their start and end apart: 4, of which 3 were waited for; matrix products, arithmetic and copies ran while one was open for 0% of the time, Pallas kernels for 3%

profile of v7, /device:TPU:56, one launch (start us, length us, event | category | flops | bytes accessed | tf_op | source)
XLA Modules:
  0.0 57.7 jit_solution(10778007033963397804)
XLA Ops:
  0.0 0.0 copy-start
  0.0 1.0 %copy-done = f32[1,1,4,5,4096]{4,2,3,1,0:T(4,128)S(1)} copy-done((f32[1,1,4,5,4096]{4,2,3,1,0:T(4,128)S(1)}, f32[1,1,4,5,4096]{4,2,3,1,0:T(4,128)}, u32[]{:S(2)}) %copy-start) | copy-done | bytes 327704
  1.0 0.0 copy-start.1
  1.0 11.5 %all_to_all.10.received = f32[4,5,32,128]{3,2,1,0:T(8,128)S(1)} all-to-all(f32[4,5,32,128]{3,2,1,0:T(8,128)S(1)} %shard_map.37), channel_id=1, replica_groups={{0,1,2,3},{4,5,6,7},{8,9,10,11},{12,13,14,15},{16,17,18,19},{20,21,22,2..., dimensions={0} | all-to-all | bytes 655360 | tf_op jit(solution)/shard_map/all_to_all | solution.py:469
  12.5 0.0 copy-done.1
  12.5 0.2 shard_map.38.own
  12.7 2.5 %collective-permute-start = (f32[5,8,8,128]{3,2,1,0:T(8,128)S(1)}, f32[5,8,8,128]{3,2,1,0:T(8,128)S(1)}, u32[]{:S(2)}, u32[]{:S(2)}) collective-permute-start(f32[5,8,8,128]{3,2,1,0:T(8,128)S(1)} %shard_map.38.own), channel_id=1, source_target_pairs={{0,1},{4,5},{8,9},{12,13},{16,17},{20,21},{24,25},{28,29},{32,33},... | collective-permute-start | bytes 491528 | tf_op jit(solution)/shard_map/ppermute | solution.py:486
  15.2 1.9 %collective-permute-start.1 = (f32[5,8,8,128]{3,2,1,0:T(8,128)S(1)}, f32[5,8,8,128]{3,2,1,0:T(8,128)S(1)}, u32[]{:S(2)}, u32[]{:S(2)}) collective-permute-start(f32[5,8,8,128]{3,2,1,0:T(8,128)S(1)} %shard_map.38.own), channel_id=1, source_target_pairs={{0,960},{4,964},{8,968},{12,972},{16,976},{20,980},{24,984},{28,98... | collective-permute-start | bytes 491528 | tf_op jit(solution)/shard_map/ppermute | solution.py:486
  17.1 0.8 %shard_map.39 = (f32[5,4,2,8,128]{4,3,2,1,0:T(8,128)S(1)}, f32[5,4,2,8,128]{4,3,2,1,0:T(8,128)S(1)}, f32[5,4,2,8,128]{4,3,2,1,0:T(8,128)S(1)}) custom-call(f32[5,8,8,128]{3,2,1,0:T(8,128)S(1)} %shard_map.38.own), custom_call_target="tpu_custom_call" | custom-call | flops 16777216 | bytes 1048576 | tf_op jit(solution)/shard_map/pallas_call | solution.py:502
  17.9 2.0 %collective-permute-done.first = f32[5,8,8,128]{3,2,1,0:T(8,128)S(1)} collective-permute-done((f32[5,8,8,128]{3,2,1,0:T(8,128)S(1)}, f32[5,8,8,128]{3,2,1,0:T(8,128)S(1)}, u32[]{:S(2)}, u32[]{:S(2)}) %collective-permute-start) | collective-permute-done | bytes 163872 | tf_op jit(solution)/shard_map/ppermute | solution.py:486
  19.9 1.9 %collective-permute-done.1.second = f32[5,8,8,128]{3,2,1,0:T(8,128)S(1)} collective-permute-done((f32[5,8,8,128]{3,2,1,0:T(8,128)S(1)}, f32[5,8,8,128]{3,2,1,0:T(8,128)S(1)}, u32[]{:S(2)}, u32[]{:S(2)}) %collective-permute-start.1) | collective-permute-done | bytes 163872 | tf_op jit(solution)/shard_map/ppermute | solution.py:486
  21.8 0.1 shard_map.41
  21.9 4.3 %collective-permute-start.2 = (f32[5,2,8,128]{3,2,1,0:T(8,128)S(1)}, f32[5,2,8,128]{3,2,1,0:T(8,128)S(1)}, u32[]{:S(2)}, u32[]{:S(2)}) collective-permute-start(f32[5,2,8,128]{3,2,1,0:T(8,128)S(1)} %get-tuple-element.17), channel_id=1, source_target_pairs={{0,4},{1,5},{2,6},{3,7},{4,8},{5,9},{6,10},{7,11},{8,12},{9,13},{1... | collective-permute-start | bytes 122888 | tf_op jit(solution)/shard_map/ppermute | solution.py:473
  26.2 15.9 %collective-permute-start.3 = (f32[5,2,8,128]{3,2,1,0:T(8,128)S(1)}, f32[5,2,8,128]{3,2,1,0:T(8,128)S(1)}, u32[]{:S(2)}, u32[]{:S(2)}) collective-permute-start(f32[5,2,8,128]{3,2,1,0:T(8,128)S(1)} %get-tuple-element.18), channel_id=1, source_target_pairs={{0,60},{1,61},{2,62},{3,63},{4,0},{5,1},{6,2},{7,3},{8,4},{9,5},{1... | collective-permute-start | bytes 122888 | tf_op jit(solution)/shard_map/ppermute | solution.py:473
  42.1 0.0 copy-start.2
  42.1 1.1 %shard_map.40 = (f32[5,8,2,8,128]{4,3,2,1,0:T(8,128)S(1)}, f32[5,8,2,8,128]{4,3,2,1,0:T(8,128)S(1)}) custom-call(f32[5,8,8,128]{3,2,1,0:T(8,128)S(1)} %collective-permute-done.first, f32[5,4,2,8,128]{4,3,2,1,0:T(8,128)S(1)} %get-tuple-element.12.prim, f32[5,4,2,8,128]{4,3,2,1,0:T(8,128)S(1)} %get-tuple-element.13.x_change, ...), custom_call_target="tpu_custom_call" | custom-call | flops 16777216 | bytes 1048576 | tf_op jit(solution)/shard_map/pallas_call | solution.py:515
  43.2 0.0 collective-permute-done.2.from_below
  43.2 0.5 collective-permute-done.3.from_above
  43.7 0.0 copy-done.2
  43.7 2.5 %shard_map.42 = f32[4,5,32,128]{3,2,1,0:T(8,128)S(1)} custom-call(s32[16,4,16]{2,1,0:T(4,128)S(1)} %bitcast.14, f32[5,8,8,128]{3,2,1,0:T(8,128)S(1)} %collective-permute-done.first, f32[5,8,8,128]{3,2,1,0:T(8,128)S(1)} %shard_map.38.own, f32[5,8,8,128]{3,2,1,0:T(8,128)S(1)} %collective-permute-done.1.second, ...), custom_call_target="tpu_custom_call" | custom-call | flops 16777216 | bytes 1048576 | tf_op jit(solution)/shard_map/pallas_call | solution.py:518
  46.2 10.7 %all_to_all.11.received = f32[4,5,32,128]{3,2,1,0:T(8,128)S(1)} all-to-all(f32[4,5,32,128]{3,2,1,0:T(8,128)S(1)} %shard_map.42), channel_id=1, replica_groups={{0,1,2,3},{4,5,6,7},{8,9,10,11},{12,13,14,15},{16,17,18,19},{20,21,22,2..., dimensions={0} | all-to-all | bytes 655360 | tf_op jit(solution)/shard_map/all_to_all | solution.py:469
  56.9 0.8 %shard_map.43 = f32[5,128,128]{2,1,0:T(8,128)} custom-call(f32[4,5,32,128]{3,2,1,0:T(8,128)S(1)} %all_to_all.11.received), custom_call_target="tpu_custom_call" | custom-call | bytes 1048576 | tf_op jit(solution)/shard_map/pallas_call | solution.py:528
  (1 shorter events, 0.0 us)
Async XLA Ops:
  0.0 1.0 %copy-start = (f32[1,1,4,5,4096]{4,2,3,1,0:T(4,128)S(1)}, f32[1,1,4,5,4096]{4,2,3,1,0:T(4,128)}, u32[]{:S(2)}) copy-start(f32[1,1,4,5,4096]{4,2,3,1,0:T(4,128)} %param.3) | copy-start | bytes 983044
  1.0 11.5 %copy-start.1 = (s32[16,16,4]{1,2,0:T(4,128)S(1)}, s32[16,16,4]{1,2,0:T(4,128)}, u32[]{:S(2)}) copy-start(s32[16,16,4]{1,2,0:T(4,128)} %param.4) | copy-start | bytes 12292
  12.7 7.2 %collective-permute-start = (f32[5,8,8,128]{3,2,1,0:T(8,128)S(1)}, f32[5,8,8,128]{3,2,1,0:T(8,128)S(1)}, u32[]{:S(2)}, u32[]{:S(2)}) collective-permute-start(f32[5,8,8,128]{3,2,1,0:T(8,128)S(1)} %shard_map.38.own), channel_id=1, source_target_pairs={{0,1},{4,5},{8,9},{12,13},{16,17},{20,21},{24,25},{28,29},{32,33},... | collective-permute-start | bytes 491528 | tf_op jit(solution)/shard_map/ppermute | solution.py:486
  15.2 6.6 %collective-permute-start.1 = (f32[5,8,8,128]{3,2,1,0:T(8,128)S(1)}, f32[5,8,8,128]{3,2,1,0:T(8,128)S(1)}, u32[]{:S(2)}, u32[]{:S(2)}) collective-permute-start(f32[5,8,8,128]{3,2,1,0:T(8,128)S(1)} %shard_map.38.own), channel_id=1, source_target_pairs={{0,960},{4,964},{8,968},{12,972},{16,976},{20,980},{24,984},{28,98... | collective-permute-start | bytes 491528 | tf_op jit(solution)/shard_map/ppermute | solution.py:486
  21.9 21.3 %collective-permute-start.2 = (f32[5,2,8,128]{3,2,1,0:T(8,128)S(1)}, f32[5,2,8,128]{3,2,1,0:T(8,128)S(1)}, u32[]{:S(2)}, u32[]{:S(2)}) collective-permute-start(f32[5,2,8,128]{3,2,1,0:T(8,128)S(1)} %get-tuple-element.17), channel_id=1, source_target_pairs={{0,4},{1,5},{2,6},{3,7},{4,8},{5,9},{6,10},{7,11},{8,12},{9,13},{1... | collective-permute-start | bytes 122888 | tf_op jit(solution)/shard_map/ppermute | solution.py:473
  26.2 17.5 %collective-permute-start.3 = (f32[5,2,8,128]{3,2,1,0:T(8,128)S(1)}, f32[5,2,8,128]{3,2,1,0:T(8,128)S(1)}, u32[]{:S(2)}, u32[]{:S(2)}) collective-permute-start(f32[5,2,8,128]{3,2,1,0:T(8,128)S(1)} %get-tuple-element.18), channel_id=1, source_target_pairs={{0,60},{1,61},{2,62},{3,63},{4,0},{5,1},{6,2},{7,3},{8,4},{9,5},{1... | collective-permute-start | bytes 122888 | tf_op jit(solution)/shard_map/ppermute | solution.py:473
  42.1 1.7 %copy-start.2 = (s32[16,16,4]{1,2,0:T(4,128)S(1)}, s32[16,16,4]{1,2,0:T(4,128)}, u32[]{:S(2)}) copy-start(s32[16,16,4]{1,2,0:T(4,128)} %param.5) | copy-start | bytes 12292

commit v8 on v7

--- a/solution.py
+++ b/solution.py
@@ -339,7 +339,17 @@
     rate_y(y_change, prim, QUARTER, 0, 0, QUARTER)
 
 
-def inner_kernel(first, prim, x_change, y_change, second, change, along_y, w0):
+def inner_kernel(
+    first, own, prim, x_change, y_change, second, middle, strips, rests, change, along_y, w0
+):
+    def u0_of(layer):
+        if 2 <= layer < 2 + QUARTER:
+            return own[:, 2 * (layer - 2) : 2 * (layer - 2) + 2]
+        if layer < 2:
+            return below_above(first, second, (slice(None), slice(2 * layer + 4, 2 * layer + 6)))[0]
+        at = 2 * (layer - 2 - QUARTER)
+        return below_above(first, second, (slice(None), slice(at, at + 2)))[1]
+
     for z in range(HALO):
         index = (slice(None), slice(2 * z, 2 * z + 2))
         below, above = below_above(first, second, index)
@@ -357,9 +367,16 @@
     rate_y(along_y, w0, 2, HALO + QUARTER, 2 + QUARTER, 2)
     rate_z(change, w0, QUARTER + HALO, INNER)
 
+    for layer in range(QUARTER + HALO):
+        base = u0_of(layer)
+        for f in range(FIELDS):
+            middle[f, layer] = base[f] + TIME_STEP * (change[f, layer] + along_y[f, layer])
+            strips[f, layer] = ends_of(base[f, 0], base[f, 1])
+            rests[f, layer] = ends_of(change[f, layer, 0], change[f, layer, 1])
+
 
 def advance_kernel(
-    held_counts, first, own, second, inner, along_y, from_below, from_above, message,
+    held_counts, own, middle, strips, rests, from_below, from_above, message,
     us, ws, changes_h, u1s, u1, w1, w1s, change, done,
 ):
     wide = QUARTER + HALO
@@ -376,21 +393,9 @@
                 us[field, z, 0, pl.ds(0, 4, stride=2), :] = halo
                 us[field, z, 0, pl.ds(1, 4, stride=2), :] = halo
 
-    def u0_of(layer):
-        if 2 <= layer < 2 + QUARTER:
-            return own[:, 2 * (layer - 2) : 2 * (layer - 2) + 2]
-        if layer < 2:
-            return below_above(first, second, (slice(None), slice(2 * layer + 4, 2 * layer + 6)))[0]
-        at = 2 * (layer - 2 - QUARTER)
-        return below_above(first, second, (slice(None), slice(at, at + 2)))[1]
-
     halo = strip_halo()
     for layer in range(wide):
-        base = u0_of(layer)
-        values = [
-            jnp.where(halo, us[f, layer, 0], ends_of(base[f, 0], base[f, 1]))
-            for f in range(FIELDS)
-        ]
+        values = [jnp.where(halo, us[f, layer, 0], strips[f, layer]) for f in range(FIELDS)]
         for f, value in enumerate(values):
             us[f, layer, 0] = value
         for f, value in enumerate(primitives(values)):
@@ -404,18 +409,13 @@
         u1s[f, :, 0] = sweeps[f]
 
     for layer in range(wide):
-        base = u0_of(layer)
         low, high, strip = [], [], []
         for f in range(FIELDS):
-            rest = ends_of(inner[f, layer, 0], inner[f, layer, 1])
+            rest = rests[f, layer]
             if 2 <= layer < 2 + QUARTER:
                 rest = jnp.where(halo, changes_h[f, layer - 2, 0], rest)
             strip.append(us[f, layer, 0] + TIME_STEP * (rest + u1s[f, layer, 0]))
-            ends = [
-                base[f, i] + TIME_STEP * (inner[f, layer, i] + along_y[f, layer, i])
-                for i in range(2)
-            ]
-            ends = put_ends(ends[0], ends[1], strip[f])
+            ends = put_ends(middle[f, layer, 0], middle[f, layer, 1], strip[f])
             low.append(ends[0])
             high.append(ends[1])
             u1[f, layer, 0], u1[f, layer, 1] = ends
@@ -512,18 +512,23 @@
         return pltpu.VMEM((FIELDS,) + shape + (ROWS, LANES), jnp.float32)
 
     change = f32(FIELDS, wide, 2, ROWS, LANES)
-    inner, inner_y = call(
-        inner_kernel, [change, change], [VMEM] * 5, [work(wide + HALO, 2)], flops=1 << 24
-    )(first, prim, x_change, y_change, second)
+    strip = f32(FIELDS, wide, ROWS, LANES)
+    middle, strips, rests = call(
+        inner_kernel,
+        [change, strip, strip],
+        [VMEM] * 6,
+        [work(wide, 2), work(wide, 2), work(wide + HALO, 2)],
+        flops=1 << 24,
+    )(first, own, prim, x_change, y_change, second)
     finished = call(
         advance_kernel,
         parts,
-        [VMEM] * 8,
+        [VMEM] * 7,
         [work(wide, 1), work(wide, 1), work(QUARTER, 1), work(wide, 1)]
         + [work(wide, 2), work(wide, 2), work(QUARTER), work(QUARTER, 2)]
         + [pltpu.VMEM((KEYS, FIELDS, ROWS, LANES), jnp.float32)],
         flops=1 << 24,
-    )(counts_new.transpose(0, 2, 1), first, own, second, inner, inner_y, from_below, from_above)
+    )(counts_new.transpose(0, 2, 1), own, middle, strips, rests, from_below, from_above)
     returned = exchange(finished)
     state = call(join_kernel, slots, [VMEM], arrivals, out=HBM)(returned)
     state = state.reshape(FIELDS, GROUP * ROWS, SLOTS, LANES).transpose(2, 0, 1, 3)

time: 58.1 us -> 57.6 us (level)
  transfers between devices with their start and end apart: 4 -> 4, of which waited for: 3 -> 3; matrix products, arithmetic and copies ran while one was open for 0% -> 0% of each run, Pallas kernels for 3% -> 4%
where the time goes in v8:
time: 57.6 us; the launch traced here: 57.2 us
  starting transfers between devices  24.5 us (43%)
  blocking collectives  22.2 us (39%)
  Pallas kernels  5.18 us (9%)
  waiting for transfers between devices  4.15 us (7%)
  local copies, waits for them, and re-layouts  0.98 us (2%)
    all_to_all x2, blocking collectives, exchange(): return lax.all_to_all(message, 'blk', 0, 0, axis_index_groups=members)  22.2 us
    ppermute x2, starting transfers between devices, along_y(): return lax.ppermute(value, 'blk', route)  20.1 us
    ppermute x2, starting transfers between devices, trade(): return lax.ppermute(value, ('gz', 'blk'), route)  4.39 us
    ppermute x2, waiting for transfers between devices, trade(): return lax.ppermute(value, ('gz', 'blk'), route)  3.86 us
    pallas_call x1, Pallas kernels, body(): call(advance_kernel, parts, [VMEM] * 7, [work(wide, 1), work(wide, 1), wo...  1.92 us
    pallas_call x1, Pallas kernels, body(): call(inner_kernel, [change, strip, strip], [VMEM] * 6, [work(wide, 2), wo...  1.34 us
  transfers between devices with their start and end apart: 4, of which 3 were waited for; matrix products, arithmetic and copies ran while one was open for 0% of the time, Pallas kernels for 4%

profile of v8, /device:TPU:56, one launch (start us, length us, event | category | flops | bytes accessed | tf_op | source)
XLA Modules:
  0.0 57.2 jit_solution(5967010042558432955)
XLA Ops:
  0.0 0.0 copy-start
  0.0 1.0 %copy-done = f32[1,1,4,5,4096]{4,2,3,1,0:T(4,128)S(1)} copy-done((f32[1,1,4,5,4096]{4,2,3,1,0:T(4,128)S(1)}, f32[1,1,4,5,4096]{4,2,3,1,0:T(4,128)}, u32[]{:S(2)}) %copy-start) | copy-done | bytes 327704
  1.0 0.0 copy-start.1
  1.0 11.5 %all_to_all.10.received = f32[4,5,32,128]{3,2,1,0:T(8,128)S(1)} all-to-all(f32[4,5,32,128]{3,2,1,0:T(8,128)S(1)} %shard_map.37), channel_id=1, replica_groups={{0,1,2,3},{4,5,6,7},{8,9,10,11},{12,13,14,15},{16,17,18,19},{20,21,22,2..., dimensions={0} | all-to-all | bytes 655360 | tf_op jit(solution)/shard_map/all_to_all | solution.py:469
  12.5 0.0 copy-done.1
  12.5 0.2 shard_map.38.own
  12.7 2.5 %collective-permute-start = (f32[5,8,8,128]{3,2,1,0:T(8,128)S(1)}, f32[5,8,8,128]{3,2,1,0:T(8,128)S(1)}, u32[]{:S(2)}, u32[]{:S(2)}) collective-permute-start(f32[5,8,8,128]{3,2,1,0:T(8,128)S(1)} %shard_map.38.own), channel_id=1, source_target_pairs={{0,1},{4,5},{8,9},{12,13},{16,17},{20,21},{24,25},{28,29},{32,33},... | collective-permute-start | bytes 491528 | tf_op jit(solution)/shard_map/ppermute | solution.py:486
  15.2 1.9 %collective-permute-start.1 = (f32[5,8,8,128]{3,2,1,0:T(8,128)S(1)}, f32[5,8,8,128]{3,2,1,0:T(8,128)S(1)}, u32[]{:S(2)}, u32[]{:S(2)}) collective-permute-start(f32[5,8,8,128]{3,2,1,0:T(8,128)S(1)} %shard_map.38.own), channel_id=1, source_target_pairs={{0,960},{4,964},{8,968},{12,972},{16,976},{20,980},{24,984},{28,98... | collective-permute-start | bytes 491528 | tf_op jit(solution)/shard_map/ppermute | solution.py:486
  17.1 0.8 %shard_map.39 = (f32[5,4,2,8,128]{4,3,2,1,0:T(8,128)S(1)}, f32[5,4,2,8,128]{4,3,2,1,0:T(8,128)S(1)}, f32[5,4,2,8,128]{4,3,2,1,0:T(8,128)S(1)}) custom-call(f32[5,8,8,128]{3,2,1,0:T(8,128)S(1)} %shard_map.38.own), custom_call_target="tpu_custom_call" | custom-call | flops 16777216 | bytes 1048576 | tf_op jit(solution)/shard_map/pallas_call | solution.py:502
  17.9 2.0 %collective-permute-done.first = f32[5,8,8,128]{3,2,1,0:T(8,128)S(1)} collective-permute-done((f32[5,8,8,128]{3,2,1,0:T(8,128)S(1)}, f32[5,8,8,128]{3,2,1,0:T(8,128)S(1)}, u32[]{:S(2)}, u32[]{:S(2)}) %collective-permute-start) | collective-permute-done | bytes 163872 | tf_op jit(solution)/shard_map/ppermute | solution.py:486
  19.9 1.9 %collective-permute-done.1.second = f32[5,8,8,128]{3,2,1,0:T(8,128)S(1)} collective-permute-done((f32[5,8,8,128]{3,2,1,0:T(8,128)S(1)}, f32[5,8,8,128]{3,2,1,0:T(8,128)S(1)}, u32[]{:S(2)}, u32[]{:S(2)}) %collective-permute-start.1) | collective-permute-done | bytes 163872 | tf_op jit(solution)/shard_map/ppermute | solution.py:486
  21.8 0.1 shard_map.41
  21.9 4.3 %collective-permute-start.2 = (f32[5,2,8,128]{3,2,1,0:T(8,128)S(1)}, f32[5,2,8,128]{3,2,1,0:T(8,128)S(1)}, u32[]{:S(2)}, u32[]{:S(2)}) collective-permute-start(f32[5,2,8,128]{3,2,1,0:T(8,128)S(1)} %get-tuple-element.19), channel_id=1, source_target_pairs={{0,4},{1,5},{2,6},{3,7},{4,8},{5,9},{6,10},{7,11},{8,12},{9,13},{1... | collective-permute-start | bytes 122888 | tf_op jit(solution)/shard_map/ppermute | solution.py:473
  26.2 15.9 %collective-permute-start.3 = (f32[5,2,8,128]{3,2,1,0:T(8,128)S(1)}, f32[5,2,8,128]{3,2,1,0:T(8,128)S(1)}, u32[]{:S(2)}, u32[]{:S(2)}) collective-permute-start(f32[5,2,8,128]{3,2,1,0:T(8,128)S(1)} %get-tuple-element.20), channel_id=1, source_target_pairs={{0,60},{1,61},{2,62},{3,63},{4,0},{5,1},{6,2},{7,3},{8,4},{9,5},{1... | collective-permute-start | bytes 122888 | tf_op jit(solution)/shard_map/ppermute | solution.py:473
  42.1 0.0 copy-start.2
  42.1 1.3 %shard_map.40 = (f32[5,8,2,8,128]{4,3,2,1,0:T(8,128)S(1)}, f32[5,8,8,128]{3,2,1,0:T(8,128)S(1)}, f32[5,8,8,128]{3,2,1,0:T(8,128)S(1)}) custom-call(f32[5,8,8,128]{3,2,1,0:T(8,128)S(1)} %collective-permute-done.first, f32[5,8,8,128]{3,2,1,0:T(8,128)S(1)} %shard_map.38.own, f32[5,4,2,8,128]{4,3,2,1,0:T(8,128)S(1)} %get-tuple-element.13.prim, ...), custom_call_target="tpu_custom_call" | custom-call | flops 16777216 | bytes 1048576 | tf_op jit(solution)/shard_map/pallas_call | solution.py:516
  43.4 0.0 collective-permute-done.2.from_below
  43.4 0.3 collective-permute-done.3.from_above
  43.7 0.0 copy-done.2
  43.7 1.9 %shard_map.42 = f32[4,5,32,128]{3,2,1,0:T(8,128)S(1)} custom-call(s32[16,4,16]{2,1,0:T(4,128)S(1)} %bitcast.14, f32[5,8,8,128]{3,2,1,0:T(8,128)S(1)} %shard_map.38.own, f32[5,8,2,8,128]{4,3,2,1,0:T(8,128)S(1)} %get-tuple-element.16.middle, f32[5,8,8,128]{3,2,1,0:T(8,128)S(1)} %get-tuple-element.17.strips, f32[5,8,8,128]{3,2,1,0:T(8,128)S(1)} %get-tuple-element.18.rests, ...), custom_call_target="tpu_custom_call" | custom-call | flops 16777216 | bytes 1048576 | tf_op jit(solution)/shard_map/pallas_call | solution.py:523
  45.7 10.7 %all_to_all.11.received = f32[4,5,32,128]{3,2,1,0:T(8,128)S(1)} all-to-all(f32[4,5,32,128]{3,2,1,0:T(8,128)S(1)} %shard_map.42), channel_id=1, replica_groups={{0,1,2,3},{4,5,6,7},{8,9,10,11},{12,13,14,15},{16,17,18,19},{20,21,22,2..., dimensions={0} | all-to-all | bytes 655360 | tf_op jit(solution)/shard_map/all_to_all | solution.py:469
  56.4 0.8 %shard_map.43 = f32[5,128,128]{2,1,0:T(8,128)} custom-call(f32[4,5,32,128]{3,2,1,0:T(8,128)S(1)} %all_to_all.11.received), custom_call_target="tpu_custom_call" | custom-call | bytes 1048576 | tf_op jit(solution)/shard_map/pallas_call | solution.py:533
  (1 shorter events, 0.0 us)
Async XLA Ops:
  0.0 1.0 %copy-start = (f32[1,1,4,5,4096]{4,2,3,1,0:T(4,128)S(1)}, f32[1,1,4,5,4096]{4,2,3,1,0:T(4,128)}, u32[]{:S(2)}) copy-start(f32[1,1,4,5,4096]{4,2,3,1,0:T(4,128)} %param.3) | copy-start | bytes 983044
  1.0 11.5 %copy-start.1 = (s32[16,16,4]{1,2,0:T(4,128)S(1)}, s32[16,16,4]{1,2,0:T(4,128)}, u32[]{:S(2)}) copy-start(s32[16,16,4]{1,2,0:T(4,128)} %param.4) | copy-start | bytes 12292
  12.7 7.2 %collective-permute-start = (f32[5,8,8,128]{3,2,1,0:T(8,128)S(1)}, f32[5,8,8,128]{3,2,1,0:T(8,128)S(1)}, u32[]{:S(2)}, u32[]{:S(2)}) collective-permute-start(f32[5,8,8,128]{3,2,1,0:T(8,128)S(1)} %shard_map.38.own), channel_id=1, source_target_pairs={{0,1},{4,5},{8,9},{12,13},{16,17},{20,21},{24,25},{28,29},{32,33},... | collective-permute-start | bytes 491528 | tf_op jit(solution)/shard_map/ppermute | solution.py:486
  15.2 6.6 %collective-permute-start.1 = (f32[5,8,8,128]{3,2,1,0:T(8,128)S(1)}, f32[5,8,8,128]{3,2,1,0:T(8,128)S(1)}, u32[]{:S(2)}, u32[]{:S(2)}) collective-permute-start(f32[5,8,8,128]{3,2,1,0:T(8,128)S(1)} %shard_map.38.own), channel_id=1, source_target_pairs={{0,960},{4,964},{8,968},{12,972},{16,976},{20,980},{24,984},{28,98... | collective-permute-start | bytes 491528 | tf_op jit(solution)/shard_map/ppermute | solution.py:486
  21.9 21.5 %collective-permute-start.2 = (f32[5,2,8,128]{3,2,1,0:T(8,128)S(1)}, f32[5,2,8,128]{3,2,1,0:T(8,128)S(1)}, u32[]{:S(2)}, u32[]{:S(2)}) collective-permute-start(f32[5,2,8,128]{3,2,1,0:T(8,128)S(1)} %get-tuple-element.19), channel_id=1, source_target_pairs={{0,4},{1,5},{2,6},{3,7},{4,8},{5,9},{6,10},{7,11},{8,12},{9,13},{1... | collective-permute-start | bytes 122888 | tf_op jit(solution)/shard_map/ppermute | solution.py:473
  26.2 17.5 %collective-permute-start.3 = (f32[5,2,8,128]{3,2,1,0:T(8,128)S(1)}, f32[5,2,8,128]{3,2,1,0:T(8,128)S(1)}, u32[]{:S(2)}, u32[]{:S(2)}) collective-permute-start(f32[5,2,8,128]{3,2,1,0:T(8,128)S(1)} %get-tuple-element.20), channel_id=1, source_target_pairs={{0,60},{1,61},{2,62},{3,63},{4,0},{5,1},{6,2},{7,3},{8,4},{9,5},{1... | collective-permute-start | bytes 122888 | tf_op jit(solution)/shard_map/ppermute | solution.py:473
  42.1 1.7 %copy-start.2 = (s32[16,16,4]{1,2,0:T(4,128)S(1)}, s32[16,16,4]{1,2,0:T(4,128)}, u32[]{:S(2)}) copy-start(s32[16,16,4]{1,2,0:T(4,128)} %param.5) | copy-start | bytes 12292
